TPU v7x, 32 devices: a whole 2x2x4 slice. The times are simulated.
32 devices in a mesh: row: 2 (over x), col: 16 (over z, y, core), smp: 1.
Axes of the slice: x: 2, y: 2, z: 4, core: 2. Of those that a mesh axis runs over, the one named last changes fastest.
Arguments:
- pair_repr: bfloat16 [256, 256, 128], P('row', 'col'), may hold values from -6 to 6
- tri_weight: bfloat16 [128, 512], replicated, may hold values from -0.75 to 0.75
- tri_bias_weight: bfloat16 [128, 4], replicated, may hold values from -40 to 40
- tri_output_weight: bfloat16 [128, 128], replicated, may hold values from -0.5 to 0.5
- samples: bfloat16 [4, 256, 768], P('smp'), may hold values from -6 to 6
- levels: int32 [4], P('smp'), may hold values from 0 to 199
- single_cond: bfloat16 [256, 384], replicated, may hold values from -6 to 6
- noise_weight: bfloat16 [256, 384], replicated, may hold values from -0.375 to 0.375
- modulation_weight: bfloat16 [384, 1536], replicated, may hold values from -0.3125 to 0.3125
- attention_weight: bfloat16 [768, 3072], replicated, may hold values from -0.5 to 0.5
- pair_bias_weight: bfloat16 [128, 16], replicated, may hold values from -40 to 40
- output_weight: bfloat16 [768, 768], replicated, may hold values from -0.21875 to 0.21875
- output_gate_weight: bfloat16 [384, 768], replicated, may hold values from -0.3125 to 0.3125
Outputs:
- new_pair: bfloat16 [256, 256, 128], P('row', 'col')
- attn_update: bfloat16 [4, 256, 768], P('smp', ('row', 'col'))
All inputs are finite; a program needn't handle non-finite values.
Results may differ from a plain program's by a relative error of at most 0.02.
The roundings to bfloat16 on the way count: a program that leaves them out, or rounds other values in their place, can miss the bound.
Values may be sent and summed in bfloat16 or wider, within the bound.
No kernel may reach another device: no remote copies, remote signals or barrier semaphores. Data moves between devices by JAX's collectives and lax.ppermute only.
A program may use at most 128 MiB of HBM per device.

v0:
```python
import math

import jax
import jax.numpy as jnp
from jax import lax
from jax.sharding import PartitionSpec as P

HT = 4
DT = 32
CA = 768
HD = 16
DH = 48
NE = 256
LEVELS = 200


NORM_EPSILON = 1e-05
SIGMA_DATA = 16.0
SIGMA_MAX = 160.0
SIGMA_MIN = 0.0004


def normalize(values):
    values = values.astype(jnp.float32)
    average = jnp.mean(values, axis=-1, keepdims=True)
    centred = values - average
    variance = jnp.mean(centred * centred, axis=-1, keepdims=True)
    return centred * lax.rsqrt(variance + NORM_EPSILON)


def noise_features(levels):
    fraction = levels.astype(jnp.float32) / (LEVELS - 1)
    upper_root = SIGMA_MAX ** (1.0 / 7.0)
    lower_root = SIGMA_MIN ** (1.0 / 7.0)
    noise_sigma = SIGMA_DATA * (upper_root + fraction * (lower_root - upper_root)) ** 7
    scaled = 0.25 * jnp.log(noise_sigma / SIGMA_DATA)
    frequency = (
        2.0
        * math.pi
        * jnp.exp(jnp.arange(NE // 2, dtype=jnp.float32) * (math.log(100.0) / (NE // 2)))
    )
    angles = scaled[:, None] * frequency[None, :]
    return jnp.concatenate([jnp.cos(angles), jnp.sin(angles)], axis=-1)


def attend_columns(pair_cols, bias_full, tri_weight, tri_output_weight):
    row_count, col_count, channels = pair_cols.shape
    normed = normalize(pair_cols).astype(jnp.bfloat16)
    projected = jnp.dot(
        normed.reshape(row_count * col_count, channels),
        tri_weight,
        preferred_element_type=jnp.float32,
    )
    projected = projected.reshape(row_count, col_count, 4, HT * DT)
    query_part = (projected[:, :, 0] * DT ** (-0.5)).astype(jnp.bfloat16)
    key_part = projected[:, :, 1].astype(jnp.bfloat16)
    value_part = projected[:, :, 2].astype(jnp.bfloat16)
    gate_part = projected[:, :, 3]

    def one_column(column):
        query_col = lax.dynamic_index_in_dim(query_part, column, 1, keepdims=False).reshape(
            row_count, HT, DT
        )
        key_col = lax.dynamic_index_in_dim(key_part, column, 1, keepdims=False).reshape(
            row_count, HT, DT
        )
        value_col = lax.dynamic_index_in_dim(value_part, column, 1, keepdims=False).reshape(
            row_count, HT, DT
        )
        gate_col = lax.dynamic_index_in_dim(gate_part, column, 1, keepdims=False)
        scores = jnp.einsum("ihd,khd->hik", query_col, key_col, preferred_element_type=jnp.float32)
        scores = scores + bias_full
        row_peak = jnp.max(scores, axis=-1, keepdims=True)
        exponent = jnp.exp(scores - row_peak)
        row_total = jnp.sum(exponent, axis=-1)
        attended = jnp.einsum(
            "hik,khd->ihd",
            exponent.astype(jnp.bfloat16),
            value_col,
            preferred_element_type=jnp.float32,
        )
        attended = attended / jnp.transpose(row_total)[:, :, None]
        return (jax.nn.sigmoid(gate_col) * attended.reshape(row_count, HT * DT)).astype(
            jnp.bfloat16
        )

    gated = lax.map(one_column, jnp.arange(col_count, dtype=jnp.int32))
    update = jnp.einsum("jic,cz->ijz", gated, tri_output_weight, preferred_element_type=jnp.float32)
    return (pair_cols.astype(jnp.float32) + update).astype(jnp.bfloat16)


def local(
    pair_repr,
    tri_weight,
    tri_bias_weight,
    tri_output_weight,
    samples,
    levels,
    single_cond,
    noise_weight,
    modulation_weight,
    attention_weight,
    pair_bias_weight,
    output_weight,
    output_gate_weight,
):
    rows_here, cols_here, channels = pair_repr.shape
    col_count = lax.axis_size("col")
    row_index = lax.axis_index("row")
    col_index = lax.axis_index("col")
    normed_tile = normalize(pair_repr).astype(jnp.bfloat16)
    local_bias = jnp.einsum(
        "kiz,zh->hik", normed_tile, tri_bias_weight, preferred_element_type=jnp.float32
    )
    partial_bias = lax.all_gather(local_bias, "row", axis=2, tiled=True)
    bias_full = lax.all_gather(partial_bias, "col", axis=1, tiled=True)
    columns = lax.all_to_all(pair_repr, "row", split_axis=1, concat_axis=0, tiled=True)
    updated = attend_columns(columns, bias_full, tri_weight, tri_output_weight)
    new_tile = lax.all_to_all(updated, "row", split_axis=0, concat_axis=1, tiled=True)
    sample_count = samples.shape[0]
    token_total = samples.shape[1]
    own_count = rows_here // col_count
    own_start = col_index * own_count
    query_start = row_index * rows_here
    features = noise_features(levels).astype(jnp.bfloat16)
    noise_terms = jnp.dot(features, noise_weight, preferred_element_type=jnp.float32)
    pair_renormed = normalize(new_tile).astype(jnp.bfloat16)
    pair_bias = jnp.einsum(
        "ikz,zh->hik", pair_renormed, pair_bias_weight, preferred_element_type=jnp.float32
    )
    trunk = single_cond.astype(jnp.float32)
    conditioned = normalize(trunk[None, :, :] + noise_terms[:, None, :]).astype(jnp.bfloat16)
    modulation = jnp.einsum(
        "stc,cd->std", conditioned, modulation_weight, preferred_element_type=jnp.float32
    )
    adapted = (
        jax.nn.sigmoid(modulation[..., :CA]) * normalize(samples) + modulation[..., CA:]
    ).astype(jnp.bfloat16)
    own_global = query_start + own_start
    cond_own = lax.dynamic_slice_in_dim(conditioned, own_global, own_count, 1)
    adapted_own = lax.dynamic_slice_in_dim(adapted, own_global, own_count, 1)
    query_part = jnp.einsum(
        "stc,cd->std", adapted_own, attention_weight[:, :CA], preferred_element_type=jnp.float32
    )
    query_part = (
        (query_part * DH ** (-0.5)).astype(jnp.bfloat16).reshape(sample_count, own_count, HD, DH)
    )
    key_value = jnp.einsum(
        "stc,cd->std", adapted, attention_weight[:, CA : 3 * CA], preferred_element_type=jnp.float32
    )
    key_part = key_value[..., :CA].astype(jnp.bfloat16).reshape(sample_count, token_total, HD, DH)
    value_part = key_value[..., CA:].astype(jnp.bfloat16).reshape(sample_count, token_total, HD, DH)
    own_pair_bias = lax.all_to_all(pair_bias, "col", split_axis=1, concat_axis=2, tiled=True)
    scores = (
        jnp.einsum("sihd,skhd->shik", query_part, key_part, preferred_element_type=jnp.float32)
        + own_pair_bias[None]
    )
    row_peak = jnp.max(scores, axis=-1)
    exponent = jnp.exp(scores - row_peak[..., None])
    row_total = jnp.sum(exponent, axis=-1)
    summed = jnp.einsum(
        "shik,skhd->sihd",
        exponent.astype(jnp.bfloat16),
        value_part,
        preferred_element_type=jnp.float32,
    )
    summed = summed.reshape(sample_count, own_count, CA)
    attended = (
        summed.reshape(sample_count, own_count, HD, DH)
        / jnp.transpose(row_total, (0, 2, 1))[..., None]
    )
    attended = attended.reshape(sample_count, own_count, CA)
    gate_part = jnp.einsum(
        "stc,cd->std",
        adapted_own,
        attention_weight[:, 3 * CA :],
        preferred_element_type=jnp.float32,
    )
    gated = (jax.nn.sigmoid(gate_part) * attended).astype(jnp.bfloat16)
    projected_out = jnp.einsum(
        "stc,cd->std", gated, output_weight, preferred_element_type=jnp.float32
    )
    out_gate = jax.nn.sigmoid(
        jnp.einsum("stc,cd->std", cond_own, output_gate_weight, preferred_element_type=jnp.float32)
    )
    attn_update = (out_gate * projected_out).astype(jnp.bfloat16)
    return (new_tile, attn_update)


def solution(mesh):
    return jax.shard_map(
        local,
        mesh=mesh,
        in_specs=(
            P("row", "col", None),
            P(),
            P(),
            P(),
            P("smp", None, None),
            P("smp"),
            P(),
            P(),
            P(),
            P(),
            P(),
            P(),
            P(),
        ),
        out_specs=(P("row", "col", None), P("smp", ("row", "col"), None)),
        check_vma=False,
    )
```

profile of v0, /device:TPU:0, one launch (start us, length us, event | category | flops | bytes accessed | tf_op | source)
XLA Modules:
  0.0 174.5 jit_solution(15134570914302706417)
XLA Ops:
  7.2 2.1 %copy.95 = bf16[128,16,128]{2,0,1:T(8,128)(2,1)} copy(bf16[128,16,128]{2,1,0:T(8,128)(2,1)} %param.15) | data formatting | bytes 1048576 | tf_op args[0]
  9.3 4.2 %all-to-all-start = ((bf16[128,16,128]{2,0,1:T(8,128)(2,1)}), bf16[128,16,128]{2,0,1:T(8,128)(2,1)S(1)}, u32[]{:S(2)}, u32[]{:S(2)}) async-start(bf16[128,16,128]{2,0,1:T(8,128)(2,1)} %copy.95), calls=%async_computation | async-start | bytes 1048576 | tf_op jit(solution)/shard_map/all_to_all | solution.py:117
  14.5 1.4 convolution_bitcast_fusion.4
  16.7 6.2 %all_gather.6 = f32[4,16,256]{2,1,0:T(8,128)S(1)} all-gather(f32[4,16,128]{2,1,0:T(8,128)} %copy.98), channel_id=1, replica_groups=mesh['row'=2,'col'=16,'smp'=1] {'row'}, dimensions={2}, use_global_device_ids=true | all-gather | bytes 98304 | tf_op jit(solution)/shard_map/all_gather | solution.py:115
  23.7 1.0 convert_element_type.128
  24.7 1.1 fusion.100
  27.5 1.9 %fusion.31 = f32[4,256,1536]{2,1,0:T(8,128)S(1)} fusion(bf16[384,1536]{1,0:T(8,128)(2,1)S(1)} %copy-done, f32[4,256]{1,0:T(4,128)S(1)} %add_rsqrt_fusion.3, f32[4,256]{1,0:T(4,128)S(1)} %broadcast_multiply_fusion.3, f32[4,384]{1,0:T(4,128)S(1)} %fusion.100, f32[256,384]{1,0:T(8,128)S(1)} %convert_element_type.128), kind=kOutput, calls=%fused_computation.52 | convolution fusion | flops 1209532416 | bytes 7878656 | tf_op jit(solution)/shard_map/stc,cd->std/dot_general | solution.py:133
  29.3 1.2 fusion.11
  30.5 1.1 copy-done.5
  31.6 4.1 %convolution_convert_fusion = bf16[4,256,1536]{2,1,0:T(8,128)(2,1)} fusion(bf16[4,256,768]{2,1,0:T(8,128)(2,1)S(1)} %fusion.11, bf16[768,3072]{1,0:T(8,128)(2,1)S(1)} %bitcast.183), kind=kOutput, calls=%fused_computation.16 | convolution fusion | flops 2417491968 | bytes 7077888 | tf_op jit(solution)/shard_map/stc,cd->std/dot_general | solution.py:148
  35.8 1.1 copy.96
  39.5 1.2 slice_bitcast_fusion.1
  40.6 1.3 fusion.77
  42.0 20.8 %all-gather.2.cloned.1.call-done = f32[4,256,256]{2,0,1:T(4,128)} async-done(((f32[4,16,256]{2,0,1:T(4,128)}), f32[4,256,256]{2,0,1:T(4,128)}) %all-gather.2.cloned.1.call-update) | async-done | bytes 1048592 | tf_op jit(solution)/shard_map/all_gather | solution.py:116
  62.8 1.6 copy.104
  64.4 58.5 %while.10 = (s32[]{:T(128)}, bf16[8,256,128]{1,2,0:T(8,128)(2,1)}, s32[8]{0:T(128)S(1)}, f32[256,8,128]{2,0,1:T(8,128)}, bf16[256,8,128]{2,0,1:T(8,128)(2,1)}, /...) while((s32[]{:T(128)}, bf16[8,256,128]{1,2,0:T(8,128)(2,1)}, ...), condition=%wide.region_7.8_spmd, body=%wide.region_4.7_spmd.sunk | while | flops 35321860 | bytes 6181543 | solution.py:87
  122.9 1.7 fusion.22
  124.6 1.1 copy.106
  125.8 3.7 %all-to-all-start.1 = ((bf16[256,8,128]{2,1,0:T(8,128)(2,1)}), bf16[256,8,128]{2,1,0:T(8,128)(2,1)S(1)}, u32[]{:S(2)}, u32[]{:S(2)}) async-start(bf16[256,8,128]{2,1,0:T(8,128)(2,1)} %copy.106), calls=%async_computation.1 | async-start | bytes 1048576 | tf_op jit(solution)/shard_map/all_to_all | solution.py:119
  129.4 3.7 %fusion.117 = (bf16[4,256,768]{2,1,0:T(8,128)(2,1)}, bf16[4,256,768]{2,1,0:T(8,128)(2,1)}) fusion(bf16[4,256,1536]{2,1,0:T(8,128)(2,1)} %convolution_convert_fusion), kind=kLoop, calls=%fused_computation.140 | loop fusion | bytes 6291456 | tf_op jit(solution)/shard_map/slice | solution.py:151
  133.2 2.3 %fusion.63 = bf16[4,8,768]{2,1,0:T(8,128)(2,1)} fusion(bf16[768,3072]{1,0:T(8,128)(2,1)} %param.24, bf16[4,256,768]{2,1,0:T(8,128)(2,1)} %copy-done.5, s32[]{:T(128)S(6)} %select_n.12), kind=kOutput, calls=%fused_computation.71 | convolution fusion | flops 37797888 | bytes 1277956 | tf_op jit(solution)/shard_map/stc,cd->std/dot_general | solution.py:142
  135.4 2.5 %all-to-all-done.1 = bf16[256,8,128]{2,1,0:T(8,128)(2,1)S(1)} async-done(((bf16[256,8,128]{2,1,0:T(8,128)(2,1)}), bf16[256,8,128]{2,1,0:T(8,128)(2,1)S(1)}, u32[]{:S(2)}, u32[]{:S(2)}) %all-to-all-start.1) | async-done | bytes 524320 | tf_op jit(solution)/shard_map/all_to_all | solution.py:119
  141.0 1.0 reshape.232
  142.1 4.2 %all-to-all-start.2 = ((f32[16,1,2048]{2,1,0:T(1,128)}), f32[16,1,2048]{2,1,0:T(1,128)}, u32[]{:S(2)}, u32[]{:S(2)}) async-start(f32[16,1,2048]{2,1,0:T(1,128)} %reshape.232), calls=%async_computation.2 | async-start | bytes 262144 | tf_op jit(solution)/shard_map/all_to_all | solution.py:153
  147.4 1.7 copy.110
  149.1 2.6 %copy.109 = bf16[4,256,768]{1,2,0:T(8,128)(2,1)} copy(bf16[4,256,768]{2,1,0:T(8,128)(2,1)} %get-tuple-element.108) | data formatting | bytes 3145728 | tf_op jit(solution)/shard_map/slice | solution.py:152
  151.7 1.9 %fusion.59 = f32[4,8,768]{2,1,0:T(8,128)} fusion(bf16[384,768]{1,0:T(8,128)(2,1)} %param.27, bf16[4,256,384]{2,1,0:T(8,128)(2,1)S(1)} %fusion.20, s32[]{:T(128)S(6)} %select_n.12), kind=kOutput, calls=%fused_computation.69 | convolution fusion | flops 18948096 | bytes 712708 | tf_op jit(solution)/shard_map/stc,cd->std/dot_general | solution.py:184
  154.7 1.9 %reduce.4 = f32[16,2048]{1,0:T(8,128)S(1)} reduce(f32[16,1,2048]{2,1,0:T(1,128)} %all-to-all-done.2, f32[]{:T(128)} %broadcast.231), dimensions={1}, to_apply=%all_to_all.36.reduce_sub_computation | reduce | bytes 262148 | tf_op jit(solution)/shard_map/all_to_all | solution.py:153
  156.5 1.3 reshape.233
  157.9 3.0 %copy.118 = f32[16,8,16,16]{3,2,1,0:T(8,128)} copy(f32[16,8,16,16]{0,3,1,2:T(8,128)} %bitcast.175) | data formatting | bytes 262144 | tf_op jit(solution)/shard_map/all_to_all | solution.py:153
  160.9 1.6 add.135
  165.2 2.5 %fusion.60 = bf16[4,8,768]{2,1,0:T(8,128)(2,1)} fusion(f32[4,8,768]{2,1,0:T(8,128)S(1)} %copy-done.11, bf16[768,768]{1,0:T(8,128)(2,1)S(1)} %copy-done.7, f32[4,8,768]{2,1,0:T(8,128)S(1)} %reshape.217, bf16[768,3072]{1,0:T(8,128)(2,1)} %param.24, bf16[4,256,768]{2,1,0:T(8,128)(2,1)} %copy-done.5, s32[]{:T(128)S(6)} %select_n.12), kind=kOutput, calls=%fused_computation.70 | convolution fusion | flops 75669504 | bytes 2654212 | tf_op jit(solution)/shard_map/stc,cd->std/dot_general | solution.py:180
  (182 shorter events, 56.2 us)
Async XLA Ops:
  7.2 20.3 %copy-start = (bf16[384,1536]{1,0:T(8,128)(2,1)S(1)}, bf16[384,1536]{1,0:T(8,128)(2,1)}, u32[]{:S(2)}) copy-start(bf16[384,1536]{1,0:T(8,128)(2,1)} %param.23) | copy-start | bytes 3538948
  7.2 6.3 %copy-start.4 = (bf16[128,16,128]{2,1,0:T(8,128)(2,1)S(1)}, bf16[128,16,128]{2,1,0:T(8,128)(2,1)}, u32[]{:S(2)}) copy-start(bf16[128,16,128]{2,1,0:T(8,128)(2,1)} %param.15) | copy-start | bytes 1572868
  7.2 7.4 %copy-start.15 = (bf16[128,4]{0,1:T(4,128)(2,1)S(1)}, bf16[128,4]{0,1:T(4,128)(2,1)}, u32[]{:S(2)}) copy-start(bf16[128,4]{0,1:T(4,128)(2,1)} %param.17) | copy-start | bytes 3076
  9.3 26.5 %all-to-all-start = ((bf16[128,16,128]{2,0,1:T(8,128)(2,1)}), bf16[128,16,128]{2,0,1:T(8,128)(2,1)S(1)}, u32[]{:S(2)}, u32[]{:S(2)}) async-start(bf16[128,16,128]{2,0,1:T(8,128)(2,1)} %copy.95), calls=%async_computation | async-start | bytes 1048576 | tf_op jit(solution)/shard_map/all_to_all | solution.py:117
  13.5 49.3 %all-gather.2.cloned.1.call-start = ((), (), s32[]{:S(2)}) async-start(), calls=%async_computation.3 | async-start | bytes 1114112 | tf_op jit(solution)/shard_map/all_gather | solution.py:116
  13.9 9.8 %copy-start.16 = (s32[4]{0:T(128)S(1)}, s32[4]{0:T(128)}, u32[]{:S(2)}) copy-start(s32[4]{0:T(128)} %param.20) | copy-start | bytes 52
  15.9 10.6 %copy-start.1 = (bf16[4,256,768]{2,1,0:T(8,128)(2,1)S(1)}, bf16[4,256,768]{2,1,0:T(8,128)(2,1)}, u32[]{:S(2)}) copy-start(bf16[4,256,768]{2,1,0:T(8,128)(2,1)} %param.19) | copy-start | bytes 4718596
  24.6 2.8 %copy-start.2 = (f32[256,384]{1,0:T(8,128)}, f32[256,384]{1,0:T(8,128)S(1)}, u32[]{:S(2)}) copy-start(f32[256,384]{1,0:T(8,128)S(1)} %convert_element_type.128) | copy-start | bytes 1179652
  27.4 4.2 %slice-start = ((s8[4718592]{0:T(1024)(128)(4,1)}), s8[4194304]{0:T(1024)(128)(4,1)S(1)}, s32[]{:S(2)}) async-start(s8[4718592]{0:T(1024)(128)(4,1)} %bitcast.182), calls=%async_computation.4 | async-start | bytes 8388608
  29.3 2.3 %slice-start.1 = ((s8[4718592]{0:T(1024)(128)(4,1)}), s8[524288]{0:T(1024)(128)(4,1)S(1)}, s32[]{:S(2)}) async-start(s8[4718592]{0:T(1024)(128)(4,1)} %bitcast.182), calls=%async_computation.5 | async-start | bytes 1048576
  30.5 1.1 copy-start.5
  31.6 4.1 %copy-start.10 = (bf16[128,512]{1,0:T(8,128)(2,1)S(1)}, bf16[128,512]{1,0:T(8,128)(2,1)}, u32[]{:S(2)}) copy-start(bf16[128,512]{1,0:T(8,128)(2,1)} %param.16) | copy-start | bytes 393220
  64.3 58.6 %copy-start.13 = (bf16[128,128]{1,0:T(8,128)(2,1)S(1)}, bf16[128,128]{1,0:T(8,128)(2,1)}, u32[]{:S(2)}) copy-start(bf16[128,128]{1,0:T(8,128)(2,1)} %param.18) | copy-start | bytes 98308
  125.8 12.2 %all-to-all-start.1 = ((bf16[256,8,128]{2,1,0:T(8,128)(2,1)}), bf16[256,8,128]{2,1,0:T(8,128)(2,1)S(1)}, u32[]{:S(2)}, u32[]{:S(2)}) async-start(bf16[256,8,128]{2,1,0:T(8,128)(2,1)} %copy.106), calls=%async_computation.1 | async-start | bytes 1048576 | tf_op jit(solution)/shard_map/all_to_all | solution.py:119
  133.2 6.9 %copy-start.14 = (bf16[128,16]{0,1:T(8,128)(2,1)S(1)}, bf16[128,16]{0,1:T(8,128)(2,1)}, u32[]{:S(2)}) copy-start(bf16[128,16]{0,1:T(8,128)(2,1)} %param.25) | copy-start | bytes 12292
  139.3 0.8 copy-start.9
  140.1 6.1 %copy-start.3 = (f32[256,384]{1,0:T(8,128)S(1)}, f32[256,384]{1,0:T(8,128)}, u32[]{:S(2)}) copy-start(f32[256,384]{1,0:T(8,128)} %copy-done.2) | copy-start | bytes 1179652
  141.0 5.6 %copy-start.12 = (bf16[4,8,768]{2,1,0:T(8,128)(2,1)S(1)}, bf16[4,8,768]{2,1,0:T(8,128)(2,1)}, u32[]{:S(2)}) copy-start(bf16[4,8,768]{2,1,0:T(8,128)(2,1)} %fusion.63) | copy-start | bytes 147460
  142.1 12.1 %all-to-all-start.2 = ((f32[16,1,2048]{2,1,0:T(1,128)}), f32[16,1,2048]{2,1,0:T(1,128)}, u32[]{:S(2)}, u32[]{:S(2)}) async-start(f32[16,1,2048]{2,1,0:T(1,128)} %reshape.232), calls=%async_computation.2 | async-start | bytes 262144 | tf_op jit(solution)/shard_map/all_to_all | solution.py:153
  157.9 4.6 %copy-start.8 = (bf16[4,8,16,48]{3,2,1,0:T(8,128)(2,1)S(1)}, bf16[4,8,16,48]{3,2,1,0:T(8,128)(2,1)}, u32[]{:S(2)}) copy-start(bf16[4,8,16,48]{3,2,1,0:T(8,128)(2,1)} %reshape.215) | copy-start | bytes 147460
  162.5 1.4 copy-start.6
  163.9 1.3 copy-start.7
  163.9 1.3 copy-start.11
Sparse Core Ops, SparseCore 0:
  23.7 38.9 all-gather.1
where the time goes:
time: 176 us; the launch traced here: 175 us
  local copies, waits for them, and re-layouts  58.6 us (33%)
  matrix products  24.5 us (14%)
  waiting for transfers between devices  23.8 us (14%)
  other arithmetic  18 us (10%)
  loops' own time  17 us (10%)
  between operations  14.4 us (8%)
  starting transfers between devices  12 us (7%)
  blocking collectives  6.24 us (4%)
    all_gather x1, waiting for transfers between devices, local(): bias_full = lax.all_gather(partial_bias, 'col', axis=1, tiled=True)  20.8 us
    another operation x1, loops' own time, attend_columns(): gated = lax.map(one_column, jnp.arange(col_count, dtype=jnp.int32))  17 us
    dynamic_slice x16, local copies, waits for them, and re-layouts, one_column(): gate_col = lax.dynamic_index_in_dim(gate_part, column, 1, keepdims=False)  8.11 us
    dynamic_slice x16, local copies, waits for them, and re-layouts, one_column(): lax.dynamic_index_in_dim(key_part, column, 1, keepdims=False)  7.95 us
    dynamic_slice x16, local copies, waits for them, and re-layouts, one_column(): lax.dynamic_index_in_dim(value_part, column, 1, keepdims=False)  7.66 us
    unnamed x41, local copies, waits for them, and re-layouts  7.66 us
    all_gather x1, blocking collectives, local(): partial_bias = lax.all_gather(local_bias, 'row', axis=2, tiled=True)  6.24 us
    slice x2, local copies, waits for them, and re-layouts, local(): key_value[..., :CA].astype(jnp.bfloat16)  5.44 us
  transfers between devices with their start and end apart: 4, of which 3 were waited for; matrix products, arithmetic and copies ran while one was open for 20% of the time, Pallas kernels for 0%

commit v1 on v0

v1 whole, which is shorter than its diff:
```python
import functools
import math

import jax
import jax.numpy as jnp
from jax import lax
from jax.experimental import pallas as pl
from jax.experimental.pallas import tpu as pltpu
from jax.sharding import PartitionSpec as P

HT = 4
DT = 32
CA = 768
HD = 16
DH = 48
NE = 256
LEVELS = 200

NORM_EPSILON = 1e-05
SIGMA_DATA = 16.0
SIGMA_MAX = 160.0
SIGMA_MIN = 0.0004

VMEM_LIMIT = 60 << 20

F32 = jnp.float32
BF16 = jnp.bfloat16
NT = (((1,), (1,)), ((), ()))


def normalize(values):
    values = values.astype(F32)
    average = jnp.mean(values, axis=-1, keepdims=True)
    centred = values - average
    variance = jnp.mean(centred * centred, axis=-1, keepdims=True)
    return centred * lax.rsqrt(variance + NORM_EPSILON)


def noise_features(levels):
    fraction = levels.astype(F32) / (LEVELS - 1)
    upper_root = SIGMA_MAX ** (1.0 / 7.0)
    lower_root = SIGMA_MIN ** (1.0 / 7.0)
    noise_sigma = SIGMA_DATA * (upper_root + fraction * (lower_root - upper_root)) ** 7
    scaled = 0.25 * jnp.log(noise_sigma / SIGMA_DATA)
    frequency = (
        2.0 * math.pi * jnp.exp(jnp.arange(NE // 2, dtype=F32) * (math.log(100.0) / (NE // 2)))
    )
    angles = scaled[:, None] * frequency[None, :]
    return jnp.concatenate([jnp.cos(angles), jnp.sin(angles)], axis=-1)


def nbytes(*shapes):
    return sum(math.prod(s.shape) * jnp.dtype(s.dtype).itemsize for s in shapes)


def held(operand):
    return pltpu.VMEM(operand.shape, operand.dtype)


def call(kernel, out_shape, operands, scratch=(), copies=0, after=(), flops=0, exps=0):
    in_specs = [pl.BlockSpec(memory_space=pltpu.HBM)] * len(operands)
    in_specs += [pl.BlockSpec(memory_space=pl.ANY)] * len(after)
    moved = nbytes(*operands, *out_shape)
    count = len(operands)

    def body(*refs):
        kernel(*refs[:count], *refs[count + len(after) :])

    return pl.pallas_call(
        body,
        out_shape=out_shape,
        in_specs=in_specs,
        out_specs=tuple(pl.BlockSpec(memory_space=pltpu.HBM) for _ in out_shape),
        scratch_shapes=[*scratch, pltpu.SemaphoreType.DMA((copies,))],
        compiler_params=pltpu.CompilerParams(vmem_limit_bytes=VMEM_LIMIT),
        cost_estimate=pl.CostEstimate(flops=flops, bytes_accessed=moved, transcendentals=exps),
    )(*operands, *after)


def start(pairs, sems, first=0):
    copies = [
        pltpu.make_async_copy(source, target, sems.at[first + at])
        for at, (source, target) in enumerate(pairs)
    ]
    for copy in copies:
        copy.start()
    return copies


def places(high, ranks, lo):
    span = high // ranks
    rest = [(h + lo % ranks * span) % high for h in range(high)]
    if lo % ranks == 0:
        rest = [h // span * span + span - 1 - h % span for h in rest]
    return rest


def turns(high, low):
    slow = sorted(range(high), key=lambda h: (h < high // 2, abs(2 * h - high)))
    return [h * low + lo for h in slow for lo in range(low)]


def hold(value, after):
    return pl.pallas_call(
        lambda *refs: None,
        out_shape=jax.ShapeDtypeStruct(value.shape, value.dtype),
        in_specs=[
            pl.BlockSpec(memory_space=pltpu.HBM),
            pl.BlockSpec(memory_space=pl.ANY),
        ],
        out_specs=pl.BlockSpec(memory_space=pltpu.HBM),
        input_output_aliases={0: 0},
        compiler_params=pltpu.CompilerParams(vmem_limit_bytes=VMEM_LIMIT),
    )(value, after)


def own_place():
    low = lax.axis_size("lo")
    return lax.axis_index("hi") * low + lax.axis_index("lo"), lax.axis_size("hi") * low


def norm_kernel(pair_hbm, weight_hbm, bias_hbm, normed_hbm, pair, weight, wide, bias, normed, sems):
    rows, cols, channels = pair.shape
    pieces = 4
    some = rows // pieces
    slices = [pl.ds(at * some, some) for at in range(pieces)]
    loads = start([(weight_hbm, weight)] + [(pair_hbm.at[h], pair.at[h]) for h in slices], sems)
    for at, load in enumerate(loads[1:]):
        load.wait()
        tile = pair[at * some : (at + 1) * some].astype(F32).reshape(some * cols, channels)
        wide[at * some * cols : (at + 1) * some * cols, :] = normalize(tile)
    loads[0].wait()
    for col in range(cols):
        one = wide[pl.ds(col, rows, stride=cols), :].astype(BF16)
        normed[col] = one
        bias[:, col, :] = lax.dot_general(weight[...], one, NT, preferred_element_type=F32)
    copies = bias_hbm.shape[0]
    pairs = [(bias, bias_hbm.at[at]) for at in range(copies)] + [(normed, normed_hbm)]
    for copy in start(pairs, sems, 1 + pieces):
        copy.wait()


def first_sample(share, each, flip=0):
    return (lax.rem(lax.axis_index("lo"), share) ^ flip) * each


def condition_kernel(share, *refs):
    levels_hbm, cond_hbm, noise_hbm, modulation_hbm, samples_hbm, attention_hbm = refs[:6]
    key_hbm, value_hbm, rows_hbm, cond_rows_hbm = refs[6:10]
    levels, cond, noise, modulation, samples, attention, key, value = refs[10:18]
    adapted, conditions, sems = refs[18:]
    count, tokens, width = samples.shape
    extra = rows_hbm.shape[1]
    first = first_sample(share, count)
    loads = start(
        [
            (levels_hbm, levels),
            (noise_hbm, noise),
            (cond_hbm, cond),
            (modulation_hbm, modulation),
            (samples_hbm.at[pl.ds(first, count)], samples),
            (attention_hbm.at[:, pl.ds(width, width)], attention.at[0]),
            (attention_hbm.at[:, pl.ds(2 * width, width)], attention.at[1]),
        ],
        sems,
    )
    loads[0].wait()
    row = lax.broadcasted_iota(jnp.int32, (8, NE // 2), 0)
    level = jnp.zeros((8, NE // 2), F32)
    for sample in range(count):
        level = jnp.where(row == sample, levels[first + sample].astype(F32), level)
    fraction = level / (LEVELS - 1)
    upper_root = SIGMA_MAX ** (1.0 / 7.0)
    lower_root = SIGMA_MIN ** (1.0 / 7.0)
    root = upper_root + fraction * (lower_root - upper_root)
    square = root * root
    sigma = SIGMA_DATA * (square * square * square * root)
    scaled = 0.25 * jnp.log(sigma / SIGMA_DATA)
    step = lax.broadcasted_iota(jnp.int32, scaled.shape, 1).astype(F32)
    angles = scaled * (2.0 * math.pi * jnp.exp(step * (math.log(100.0) / (NE // 2))))
    features = jnp.concatenate([jnp.cos(angles), jnp.sin(angles)], axis=-1).astype(BF16)
    loads[1].wait()
    terms = jnp.dot(features, noise[...], preferred_element_type=F32)
    for load in loads[2:4]:
        load.wait()

    loads[4].wait()
    for sample in range(count):
        trunk = cond[...].astype(F32) + terms[sample : sample + 1]
        conditioned = normalize(trunk).astype(BF16)
        conditions[sample] = conditioned
        modulated = jnp.dot(conditioned, modulation[...], preferred_element_type=F32)
        gain = jax.nn.sigmoid(modulated[:, :width])
        one = gain * normalize(samples[sample]) + modulated[:, width:]
        adapted[sample] = one.astype(BF16)
    place, places = own_place()
    chip = lax.div(lax.axis_index("row") * places + place, share) * extra
    here = pl.ds(pl.multiple_of(chip, extra), extra)
    stores = start(
        [(adapted.at[:, here], rows_hbm), (conditions.at[:, here], cond_rows_hbm)], sems, 7
    )
    for at, (part, target) in enumerate(((key, key_hbm), (value, value_hbm))):
        loads[5 + at].wait()
        for sample in range(count):
            part[sample] = jnp.dot(
                adapted[sample], attention[at], preferred_element_type=F32
            ).astype(BF16)
        stores += start([(part, target)], sems, 9 + at)
    for store in stores:
        store.wait()


def token_kernel(share, *refs):
    attention_hbm, gate_hbm, rows_hbm, cond_hbm, key_hbm = refs[:5]
    targets, refs = refs[5 : 5 + share], refs[5 + share :]
    attention, gate_weight, rows, cond, key, found, wide, sems = refs
    count, tokens, width = key.shape
    extra = rows.shape[1]
    own = extra // share
    loads = start(
        [
            (rows_hbm, rows),
            (attention_hbm.at[:, pl.ds(0, width)], attention.at[0]),
            (key_hbm, key),
            (attention_hbm.at[:, pl.ds(3 * width, width)], attention.at[1]),
            (cond_hbm, cond),
            (gate_hbm, gate_weight),
        ],
        sems,
    )
    for load in loads[:2]:
        load.wait()
    flat = rows[...].reshape(count * extra, width)
    raw = jnp.dot(flat, attention[0], preferred_element_type=F32)
    query = (raw * DH ** (-0.5)).astype(BF16).astype(F32)
    masks = head_masks(width)
    loads[2].wait()
    for sample in range(count):
        stacked = []
        for core in range(share):
            at = sample * extra + core * own
            one = query[at : at + own]
            stacked += [jnp.where(m, one, 0.0) for m in masks]
        stacked = jnp.concatenate(stacked, axis=0).astype(BF16)
        raw = lax.dot_general(key[sample], stacked, NT, preferred_element_type=F32)
        for core in range(share):
            found[core, sample, :tokens, :] = raw[:, core * HD * own : (core + 1) * HD * own]
    loads[3].wait()
    wide[0] = jax.nn.sigmoid(jnp.dot(flat, attention[1], preferred_element_type=F32))
    for load in loads[4:]:
        load.wait()
    flat = cond[...].reshape(count * extra, cond.shape[2])
    wide[1] = jax.nn.sigmoid(jnp.dot(flat, gate_weight[...], preferred_element_type=F32))
    lanes = found.shape[3]
    for core in range(share):
        for sample in range(count):
            at = sample * extra + core * own
            to = tokens
            for kind in range(2):
                for lane in range(0, width, lanes):
                    found[core, sample, to : to + own, :] = wide[
                        kind, at : at + own, lane : lane + lanes
                    ]
                    to += own
    mine = lax.rem(lax.axis_index("lo"), share)
    stores = start(
        [(found.at[mine ^ flip], targets[flip]) for flip in range(share)], sems, len(loads)
    )
    for store in stores:
        store.wait()


def triangle_kernel(ranks, low, *refs):
    pair_hbm, weight_hbm, out_weight_hbm, bias_weight_hbm = refs[:4]
    gathered_hbm, refs = refs[4 : 4 + low], refs[4 + low :]
    normed_hbm, refs = refs[:ranks], refs[ranks:]
    new_hbm, pair_bias_hbm, refs = refs[0], refs[1], refs[2:]
    pair, weight, out_weight, bias_weight = refs[:4]
    gathered, normed, new, pair_bias, refs = refs[4], refs[5], refs[6], refs[7], refs[8:]
    bias_rows, bias, query, key, value, gate, wide = refs[:7]
    slots, sems = (refs[7:10], refs[10:13]), refs[13]
    rows, cols, channels = pair.shape
    width = HT * DT
    span = gathered.shape[2]
    loads = start(
        [
            (weight_hbm, weight),
            *[(normed_hbm[at], normed.at[at]) for at in range(ranks)],
            *[(gathered_hbm[at], gathered.at[at]) for at in range(low)],
            (pair_hbm, pair),
            (out_weight_hbm, out_weight),
            (bias_weight_hbm, bias_weight),
        ],
        sems,
    )
    for load in loads[: 1 + ranks + low]:
        load.wait()
    row, fast = lax.axis_index("row"), lax.axis_index("lo")
    for flip in range(low):
        for slow in range(span):
            sender = fast ^ flip
            block = jnp.where(lax.rem(sender, ranks) == 0, span - 1 - slow, slow)
            first = pl.multiple_of((block * low + sender) * cols, cols)
            for source in range(ranks):
                step = lax.rem(source + ranks - row, ranks)
                bias_rows[step, :, pl.ds(first, cols), :] = gathered[flip, source, slow]
    turned = jnp.transpose(weight[...].astype(F32)).astype(BF16)
    own_lines = jnp.concatenate([turned[:width], turned[2 * width :]], axis=0)
    peer_lines = turned[2 * width : 3 * width]
    batch = 4
    tiles = [(step, head) for step in range(ranks) for head in range(HT)]
    groups = cols // batch
    for group in range(groups):
        at = group * batch
        for step in range(ranks):
            some = normed[step, at : at + batch].reshape(batch * rows, channels)
            here = slice(step * rows, (step + 1) * rows)
            raw = jnp.dot(some, weight[:, width : 2 * width], preferred_element_type=F32)
            key[at : at + batch, here, :] = raw.astype(BF16).reshape(batch, rows, width)
            lines = own_lines if step == 0 else peer_lines
            raw = lax.dot_general(lines, some, NT, preferred_element_type=F32)
            for side in range(batch):
                part = raw[:, side * rows : (side + 1) * rows]
                if step == 0:
                    query[at + side] = (part[:width] * DT ** (-0.5)).astype(BF16)
                    gate[at + side] = jax.nn.sigmoid(part[2 * width :])
                    part = part[width : 2 * width]
                value[at + side, :, here] = part.astype(BF16)
        for step, head in tiles[group::groups]:
            bias[step * rows : (step + 1) * rows, head * rows : (head + 1) * rows] = jnp.transpose(
                bias_rows[step, head]
            )
    for load in loads[1 + ranks + low :]:
        load.wait()

    def score(col, slot):
        scores, peak, _ = slots[slot]
        own = query[col]
        blocks = []
        for head in range(HT):
            zeros = [jnp.zeros((size, rows), BF16) for size in (head * DT, width - (head + 1) * DT)]
            block = [zeros[0], own[head * DT : (head + 1) * DT], zeros[1]]
            blocks.append(jnp.concatenate([b for b in block if b.shape[0]], axis=0))
        stacked = jnp.concatenate(blocks, axis=1)
        raw = jnp.dot(key[col], stacked, preferred_element_type=F32) + bias[...]
        scores[...] = raw
        peak[...] = jnp.max(raw, axis=0, keepdims=True)

    def attend(col, slot):
        scores, peak, weights = slots[slot]
        exponent = jnp.exp(scores[...] - peak[...])
        scale = 1.0 / jnp.sum(exponent, axis=0, keepdims=True)
        weights[...] = exponent.astype(BF16)
        parts = []
        for head in range(0, HT, 2):
            here = slice(head * rows, (head + 2) * rows)
            summed = jnp.dot(
                value[col, head * DT : (head + 2) * DT, :],
                weights[:, here],
                preferred_element_type=F32,
            )
            summed = summed * scale[:, here]
            parts += [summed[:DT, :rows], summed[DT:, rows:]]
        gated = (gate[col] * jnp.concatenate(parts, axis=0)).astype(BF16)
        wide[pl.ds(col, rows, stride=cols), :] = lax.dot_general(
            gated, out_weight[...], (((0,), (0,)), ((), ())), preferred_element_type=F32
        )

    score(0, 0)

    @pl.loop(0, cols // batch)
    def _(group):
        for side in range(batch):
            col = group * batch + side
            score(jnp.minimum(col + 1, cols - 1), (side + 1) % 2)
            attend(col, side % 2)

    updated = (pair[...].astype(F32).reshape(rows * cols, channels) + wide[...]).astype(BF16)
    new[...] = updated.reshape(rows, cols, channels)
    stores = start([(new, new_hbm)], sems, len(loads))
    owners, _, lanes = pair_bias.shape
    own = rows // owners
    lane = lax.broadcasted_iota(jnp.int32, (lanes, HD), 0)
    pick = (lane // own == lax.broadcasted_iota(jnp.int32, (lanes, HD), 1)).astype(BF16)
    spread = jnp.dot(pick, bias_weight[...], preferred_element_type=F32)
    token_of = lax.rem(lax.broadcasted_iota(jnp.int32, (lanes, channels), 0), own)
    renormed = normalize(updated).astype(BF16).reshape(owners, own, cols, channels)
    total = jnp.zeros((owners * cols, lanes), F32)
    for token in range(own):
        total += lax.dot_general(
            renormed[:, token].reshape(owners * cols, channels),
            jnp.where(token_of == token, spread, 0.0).astype(BF16),
            NT,
            preferred_element_type=F32,
        )
    total = total.reshape(owners, cols, lanes)
    for place, owner in enumerate(turns(owners // low, low)):
        pair_bias[place] = total[owner]
    stores += start([(pair_bias, pair_bias_hbm)], sems, len(loads) + 1)
    for store in stores:
        store.wait()


def head_masks(width):
    lane = lax.broadcasted_iota(jnp.int32, (1, width), 1)
    return [(lane >= head * DH) & (lane < (head + 1) * DH) for head in range(HD)]


def attend_kernel(share, *refs):
    bias_hbm, weight_hbm = refs[:2]
    found_hbm, value_hbm, refs = refs[2 : 2 + share], refs[2 + share : 2 + 2 * share], refs[2 + 2 * share :]
    out_hbm, bias, weight, found, value, out, sems = refs
    count, tokens, wider = value.shape
    width = weight.shape[0]
    each = count // share
    own = out.shape[0] // count
    value[:, :, width:] = jnp.ones((count, tokens, wider - width), BF16)
    firsts = [first_sample(share, each, flip) for flip in range(share)]
    loads = start(
        [
            (bias_hbm, bias),
            *[(found_hbm[flip], found.at[pl.ds(firsts[flip], each)]) for flip in range(share)],
            *[
                (value_hbm[flip].at[at], value.at[firsts[flip] + at, :, pl.ds(0, width)])
                for flip in range(share)
                for at in range(each)
            ],
            (weight_hbm, weight),
        ],
        sems,
    )
    for load in loads[: 1 + share]:
        load.wait()
    low = lax.axis_size("lo")
    order = turns(bias.shape[0] // low, low)
    turned = jnp.concatenate([bias[order.index(c)] for c in range(len(order))], axis=0)
    masks = head_masks(width)
    weights = []
    for sample in range(count):
        total_scores = found[sample, :tokens] + turned
        peak = jnp.max(total_scores, axis=0, keepdims=True)
        weights.append(jnp.exp(total_scores - peak).astype(BF16))
    rows = []
    for sample in range(count):
        if sample == 0:
            for load in loads[1 + share : 1 + share + count]:
                load.wait()
        summed = lax.dot_general(
            weights[sample], value[sample], (((0,), (0,)), ((), ())), preferred_element_type=F32
        )
        scale = 1.0 / summed[:, width : width + 1]
        summed = summed[:, :width] * scale
        attended = jnp.where(masks[0], summed[:own], 0.0)
        for head in range(1, HD):
            attended = jnp.where(masks[head], summed[head * own : (head + 1) * own], attended)
        rows.append(attended)

    def gates(kind):
        parts = []
        lanes = found.shape[2]
        for sample in range(count):
            first = tokens + kind * own * (width // lanes)
            blocks = [
                found[sample, first + at * own : first + (at + 1) * own]
                for at in range(width // lanes)
            ]
            parts.append(jnp.concatenate(blocks, axis=1))
        return jnp.concatenate(parts, axis=0)

    loads[-1].wait()
    gated = (gates(0) * jnp.concatenate(rows, axis=0)).astype(BF16)
    projected = jnp.dot(gated, weight[...], preferred_element_type=F32)
    out[...] = (gates(1) * projected).astype(BF16)
    for store in start([(out, out_hbm)], sems, len(loads)):
        store.wait()


def local(
    pair_repr,
    tri_weight,
    tri_bias_weight,
    tri_output_weight,
    samples,
    levels,
    single_cond,
    noise_weight,
    modulation_weight,
    attention_weight,
    pair_bias_weight,
    output_weight,
    output_gate_weight,
):
    rows, cols, channels = pair_repr.shape
    ranks, high, low = (lax.axis_size(name) for name in ("row", "hi", "lo"))
    col_count = high * low
    sample_count, tokens, width = samples.shape
    own = rows // col_count
    span = high // ranks
    keys = ranks * rows
    shape = jax.ShapeDtypeStruct

    turned = jnp.transpose(tri_bias_weight)
    normed_shape = shape((cols, rows, channels), BF16)
    bias_shape = shape((HT, cols, rows), F32)
    wide = pltpu.VMEM((rows * cols, channels), F32)
    copies_shape = shape((ranks * high, *bias_shape.shape), F32)
    bias, normed = call(
        norm_kernel,
        (copies_shape, normed_shape),
        (pair_repr, turned),
        scratch=(held(pair_repr), held(turned), wide, held(bias_shape), held(normed_shape)),
        copies=6 + ranks * high,
        flops=2 * rows * cols * channels * HT,
    )
    groups = [
        [
            (r * high + h) * low + lo
            for r in range(ranks)
            for h in places(high, ranks, lo)
        ]
        for lo in range(low)
    ]
    placed = lax.all_to_all(
        bias, ("row", "hi", "lo"), split_axis=0, concat_axis=0, axis_index_groups=groups
    )
    peers = [
        lax.ppermute(normed, "row", [((r + step) % ranks, r) for r in range(ranks)])
        for step in range(1, ranks)
    ]

    share = 2 if low % 2 == 0 and sample_count % 2 == 0 else 1
    each = sample_count // share
    part = (each, tokens, width)
    extra = share * own
    conditions = single_cond.shape[1]
    key, value, own_rows, cond_rows = call(
        functools.partial(condition_kernel, share),
        (
            shape(part, BF16),
            shape(part, BF16),
            shape((each, extra, width), BF16),
            shape((each, extra, conditions), BF16),
        ),
        (
            levels,
            single_cond,
            noise_weight,
            modulation_weight,
            samples,
            attention_weight,
        ),
        scratch=(
            pltpu.SMEM(levels.shape, levels.dtype),
            held(single_cond),
            held(noise_weight),
            held(modulation_weight),
            pltpu.VMEM(part, BF16),
            pltpu.VMEM((2, width, width), BF16),
            pltpu.VMEM(part, BF16),
            pltpu.VMEM(part, BF16),
            pltpu.VMEM(part, BF16),
            pltpu.VMEM((each, *single_cond.shape), BF16),
        ),
        copies=11,
        after=(bias,),
        flops=4 * each * tokens * width * 2 * width,
        exps=each * tokens * width,
    )
    placed = placed.reshape(ranks, high, *bias_shape.shape)
    place = lax.axis_index("row") + ranks - lax.rem(lax.axis_index("lo"), ranks)
    gathered = [lax.dynamic_slice_in_dim(placed, lax.rem(place, ranks) * span, span, 1)]
    found_shape = shape((each, tokens + 2 * width // HD, HD * own), F32)
    found = list(
        call(
            functools.partial(token_kernel, share),
            (found_shape,) * share,
            (attention_weight, output_gate_weight, own_rows, cond_rows, key),
            scratch=(
                pltpu.VMEM((2, width, width), BF16),
                held(output_gate_weight),
                held(own_rows),
                held(cond_rows),
                held(key),
                pltpu.VMEM((share, *found_shape.shape), F32),
                pltpu.VMEM((2, each * extra, width), F32),
            ),
            copies=6 + share,
            after=(gathered[0],),
            flops=64 * rows * cols * channels * HT * DT,
        )
    )
    bit = low // 2
    while bit:
        flip = [(c ^ bit, c) for c in range(low)]
        ready = [gathered[0], *(hold(part, found[0]) for part in gathered[1:])]
        more = [lax.ppermute(part, "lo", flip) for part in ready]
        gathered = [part for both in zip(ready, more) for part in both]
        bit //= 2
    values = [value]
    if share == 2:
        other = [(c ^ 1, c) for c in range(low)]
        values.append(lax.ppermute(value, "lo", other))
        found[1] = lax.ppermute(found[1], "lo", other)

    pair_weight = jnp.transpose(pair_bias_weight)
    outs = (shape((rows, cols, channels), BF16), shape((col_count, cols, HD * own), F32))
    new_pair, pair_bias = call(
        functools.partial(triangle_kernel, ranks, low),
        outs,
        (
            pair_repr,
            tri_weight,
            tri_output_weight,
            pair_weight,
            *gathered,
            normed,
            *peers,
        ),
        scratch=(
            held(pair_repr),
            held(tri_weight),
            held(tri_output_weight),
            held(pair_weight),
            pltpu.VMEM((low, ranks, span, HT, cols, rows), F32),
            pltpu.VMEM((ranks, cols, rows, channels), BF16),
            held(outs[0]),
            held(outs[1]),
            pltpu.VMEM((ranks, HT, rows, rows), F32),
            pltpu.VMEM((keys, HT * rows), F32),
            pltpu.VMEM((cols, HT * DT, rows), BF16),
            pltpu.VMEM((cols, keys, HT * DT), BF16),
            pltpu.VMEM((cols, HT * DT, keys), BF16),
            pltpu.VMEM((cols, HT * DT, rows), F32),
            wide,
            *[
                pltpu.VMEM(*slot)
                for slot in (
                    ((keys, HT * rows), F32),
                    ((1, HT * rows), F32),
                    ((keys, HT * rows), BF16),
                )
                * 2
            ],
        ),
        copies=6 + ranks + low,
        after=(found[0],),
        flops=4 * HT * rows * cols * keys * HT * DT,
        exps=HT * rows * cols * keys,
    )
    own_bias = lax.all_to_all(
        pair_bias, ("hi", "lo"), split_axis=0, concat_axis=0, axis_index_groups=[turns(high, low)]
    )

    outs = (shape((sample_count * own, width), BF16),)
    (attn_update,) = call(
        functools.partial(attend_kernel, share),
        outs,
        (own_bias, output_weight, *found, *values),
        scratch=(
            held(own_bias),
            held(output_weight),
            pltpu.VMEM((sample_count, *found_shape.shape[1:]), F32),
            pltpu.VMEM((sample_count, tokens, width + 128), BF16),
            held(outs[0]),
        ),
        copies=3 + share + sample_count,
        flops=2 * sample_count * HD * own * tokens * width,
        exps=sample_count * HD * own * tokens,
    )
    return (new_pair, attn_update.reshape(sample_count, own, width))


def solution(mesh):
    ranks, col_count, groups = (mesh.shape[name] for name in ("row", "col", "smp"))
    low = math.gcd(col_count // ranks, 4)
    finer = jax.sharding.Mesh(
        mesh.devices.reshape(ranks, col_count // low, low, groups), ("row", "hi", "lo", "smp")
    )
    tile = P("row", ("hi", "lo"), None)
    return jax.shard_map(
        local,
        mesh=finer,
        in_specs=(tile, P(), P(), P(), P("smp", None, None), P("smp"), *[P()] * 7),
        out_specs=(tile, P("smp", ("row", "hi", "lo"), None)),
        check_vma=False,
    )
```

time: 176 us -> 52.4 us (0.30)
  local copies, waits for them, and re-layouts: 58.6 us -> 2.24 us
  Pallas kernels: 0 us -> 25.3 us
  matrix products: 24.5 us -> 0 us
  other arithmetic: 18 us -> 0 us
  waiting for transfers between devices: 23.8 us -> 6.65 us
  loops' own time: 17 us -> 0 us
  between operations: 14.4 us -> 0.76 us
  blocking collectives: 6.24 us -> 0 us
  starting transfers between devices: 12 us -> 16.8 us
    dynamic_slice x64 -> x1, local copies, waits for them, and re-layouts: 29.9 us -> 0.02 us  [local(): lax.dynamic_slice_in_dim(placed, lax.rem(place, ranks) * span, span, 1)]
    pallas_call x0 -> x6, Pallas kernels: none -> 25.3 us  [the longest x5 25.3 us: call(): pl.pallas_call(body, out_shape=out_shape, in_specs=in_specs, out_specs=tu...]
    dot_general x28 -> x0, matrix products: 24.5 us -> none  [the longest x1 4.06 us: local(): jnp.einsum('stc,cd->std', adapted, attention_weight[:, CA:3 * CA], prefer...]
    all_gather x1 -> x0, waiting for transfers between devices: 20.8 us -> none  [local(): bias_full = lax.all_gather(partial_bias, 'col', axis=1, tiled=True)]
    another operation x1 -> x0, loops' own time: 17 us -> none  [attend_columns(): gated = lax.map(one_column, jnp.arange(col_count, dtype=jnp.int32))]
    slice x3 -> x0, local copies, waits for them, and re-layouts: 8.04 us -> none  [the longest x2 5.44 us: local(): key_value[..., :CA].astype(jnp.bfloat16)]
    all_gather x1 -> x0, blocking collectives: 6.24 us -> none  [local(): partial_bias = lax.all_gather(local_bias, 'row', axis=2, tiled=True)]
    reduce_sum x19 -> x0, other arithmetic: 6.09 us -> none  [the longest x5 2.97 us: normalize(): variance = jnp.mean(centred * centred, axis=-1, keepdims=True)]
  transfers between devices with their start and end apart: 4 -> 8, of which waited for: 3 -> 3; matrix products, arithmetic and copies ran while one was open for 20% -> 0% of each run, Pallas kernels for 0% -> 36%
where the time goes in v1:
time: 52.4 us; the launch traced here: 51.8 us
  Pallas kernels  25.3 us (48%)
  starting transfers between devices  16.8 us (32%)
  waiting for transfers between devices  6.65 us (13%)
  local copies, waits for them, and re-layouts  2.24 us (4%)
  between operations  0.76 us (1%)
    pallas_call x5, Pallas kernels, call(): pl.pallas_call(body, out_shape=out_shape, in_specs=in_specs, out_specs=tu...  25.3 us
    all_to_all x1, starting transfers between devices, local(): lax.all_to_all(bias, ('row', 'hi', 'lo'), split_axis=0, concat_axis=0, ax...  7.82 us
    all_to_all x1, starting transfers between devices, local(): lax.all_to_all(pair_bias, ('hi', 'lo'), split_axis=0, concat_axis=0, axis...  5.19 us
    all_to_all x1, waiting for transfers between devices, local(): lax.all_to_all(pair_bias, ('hi', 'lo'), split_axis=0, concat_axis=0, axis...  4.45 us
    unnamed x16, local copies, waits for them, and re-layouts  2.22 us
    ppermute x3, starting transfers between devices, local(): more = [lax.ppermute(part, 'lo', flip) for part in ready]  1.78 us
    ppermute x1, waiting for transfers between devices, local(): lax.ppermute(normed, 'row', [((r + step) % ranks, r) for r in range(ranks)])  1.57 us
    ppermute x1, starting transfers between devices, local(): lax.ppermute(normed, 'row', [((r + step) % ranks, r) for r in range(ranks)])  1.46 us
  transfers between devices with their start and end apart: 8, of which 3 were waited for; matrix products, arithmetic and copies ran while one was open for 0% of the time, Pallas kernels for 36%

profile of v1, /device:TPU:0, one launch (start us, length us, event | category | flops | bytes accessed | tf_op | source)
XLA Modules:
  0.0 51.8 jit_solution(9917897756429333523)
XLA Ops:
  0.6 3.3 %shard_map.140 = (f32[8,4,16,128]{3,2,1,0:T(8,128)}, bf16[16,128,128]{2,1,0:T(8,128)(2,1)}) custom-call(bf16[128,16,128]{2,1,0:T(8,128)(2,1)} %refs_0_.7, bf16[4,128]{1,0:T(4,128)(2,1)} %bitcast.6), custom_call_target="tpu_custom_call" | custom-call | flops 2097152 | bytes 1311744 | tf_op jit(solution)/shard_map/pallas_call | solution.py:69
  4.0 7.8 %all-to-all-start = ((f32[8,4,16,128]{3,2,1,0:T(8,128)}), f32[8,4,16,128]{3,2,1,0:T(8,128)S(1)}, u32[]{:S(2)}, u32[]{:S(2)}) async-start(f32[8,4,16,128]{3,2,1,0:T(8,128)} %get-tuple-element.12.refs_6_), calls=%async_computation | async-start | bytes 524288 | tf_op jit(solution)/shard_map/all_to_all | solution.py:523
  11.8 1.5 %collective-permute-start.3 = (bf16[16,128,128]{2,1,0:T(8,128)(2,1)}, bf16[16,128,128]{2,1,0:T(8,128)(2,1)S(1)}, u32[]{:S(2)}, u32[]{:S(2)}) collective-permute-start(bf16[16,128,128]{2,1,0:T(8,128)(2,1)} %get-tuple-element.17.refs_8_), channel_id=1, source_target_pairs={{16,0},{0,16},{17,1},{1,17},{18,2},{2,18},{19,3},{3,19},{20,4},{4,... | collective-permute-start | bytes 1572872 | tf_op jit(solution)/shard_map/ppermute | solution.py:527
  13.2 5.6 %shard_map.141 = (bf16[2,256,768]{2,1,0:T(8,128)(2,1)}, bf16[2,256,768]{2,1,0:T(8,128)(2,1)}, bf16[2,16,768]{2,1,0:T(8,128)(2,1)}, bf16[2,16,384]{2,1,0:T(8,128)(2,1)}) custom-call(s32[4]{0:T(128)} %refs_0_.5, bf16[256,384]{1,0:T(8,128)(2,1)} %refs_1_.4, bf16[256,384]{1,0:T(8,128)(2,1)} %refs_2_.2, bf16[384,1536]{1,0:T(8,128)(2,1)} %refs_3_.1, ...), custom_call_target="tpu_custom_call" | custom-call | flops 2415919104 | bytes 9510928 | tf_op jit(solution)/shard_map/pallas_call | solution.py:69
  18.8 0.1 collective-permute-start.5
  18.9 0.0 all-to-all-done
  18.9 0.0 copy-start.4
  18.9 1.6 %collective-permute-start.1 = (f32[2,2,4,16,128]{4,3,2,1,0:T(8,128)S(1)}, f32[2,2,4,16,128]{4,3,2,1,0:T(8,128)S(1)}, u32[]{:S(2)}, u32[]{:S(2)}) collective-permute-start(f32[2,2,4,16,128]{4,3,2,1,0:T(8,128)S(1)} %constant_dynamic-slice_fusion.refs_5_.refs_4_), channel_id=1, source_target_pairs={{2,0},{3,1},{0,2},{1,3},{6,4},{7,5},{4,6},{5,7},{10,8},{11,9},{8,1... | collective-permute-start | bytes 393224 | tf_op jit(solution)/shard_map/ppermute | solution.py:596
  20.5 0.2 collective-permute-start
  20.7 0.0 copy-done.4
  20.7 3.5 %shard_map.142 = (f32[2,352,128]{2,1,0:T(8,128)}, f32[2,352,128]{2,1,0:T(8,128)}) custom-call(bf16[768,3072]{1,0:T(8,128)(2,1)} %refs_0_.6, bf16[384,768]{1,0:T(8,128)(2,1)} %refs_1_.5, bf16[2,16,768]{2,1,0:T(8,128)(2,1)} %get-tuple-element.13.refs_2_, bf16[2,16,384]{2,1,0:T(8,128)(2,1)} %get-tuple-element.14.refs_3_, ...), custom_call_target="tpu_custom_call" | custom-call | flops 2147483648 | bytes 6889472 | tf_op jit(solution)/shard_map/pallas_call | solution.py:69
  24.3 0.6 %collective-permute-done.1.refs_0_ = f32[2,2,4,16,128]{4,3,2,1,0:T(8,128)S(1)} collective-permute-done((f32[2,2,4,16,128]{4,3,2,1,0:T(8,128)S(1)}, f32[2,2,4,16,128]{4,3,2,1,0:T(8,128)S(1)}, u32[]{:S(2)}, u32[]{:S(2)}) %collective-permute-start.1) | collective-permute-done | bytes 131104 | tf_op jit(solution)/shard_map/ppermute | solution.py:596
  24.9 0.7 %copy-done.3 = f32[2,2,4,16,128]{4,3,2,1,0:T(8,128)} copy-done((f32[2,2,4,16,128]{4,3,2,1,0:T(8,128)}, f32[2,2,4,16,128]{4,3,2,1,0:T(8,128)S(1)}, u32[]{:S(2)}) %copy-start.3) | copy-done | bytes 131096
  25.5 0.0 collective-permute-start.2
  25.5 0.5 collective-permute-start.4
  26.0 1.6 %collective-permute-done.3.refs_9_ = bf16[16,128,128]{2,1,0:T(8,128)(2,1)S(1)} collective-permute-done((bf16[16,128,128]{2,1,0:T(8,128)(2,1)}, bf16[16,128,128]{2,1,0:T(8,128)(2,1)S(1)}, u32[]{:S(2)}, u32[]{:S(2)}) %collective-permute-start.3) | collective-permute-done | bytes 524320 | tf_op jit(solution)/shard_map/ppermute | solution.py:527
  27.6 0.0 collective-permute-done.refs_5_
  27.6 0.0 collective-permute-done.2.refs_7_
  27.6 0.0 copy-start.7
  27.6 0.8 %copy-done.5 = bf16[16,128,128]{2,1,0:T(8,128)(2,1)} copy-done((bf16[16,128,128]{2,1,0:T(8,128)(2,1)}, bf16[16,128,128]{2,1,0:T(8,128)(2,1)S(1)}, u32[]{:S(2)}) %copy-start.5) | copy-done | bytes 524312
  28.4 0.1 copy-done.6
  28.5 0.0 copy-done.7
  28.5 9.7 %shard_map.144 = (bf16[128,16,128]{2,1,0:T(8,128)(2,1)}, f32[16,16,128]{2,1,0:T(8,128)}) custom-call(bf16[128,16,128]{2,1,0:T(8,128)(2,1)} %refs_0_.7, bf16[128,512]{1,0:T(8,128)(2,1)} %refs_1_.6, bf16[128,128]{1,0:T(8,128)(2,1)} %refs_2_.3, bf16[16,128]{1,0:T(8,128)(2,1)} %bitcast.7, f32[2,2,4,16,128]{4,3,2,1,0:T(8,128)} %copy-done.4, ...), custom_call_target="tpu_custom_call" | custom-call | flops 1073741824 | bytes 2920448 | tf_op jit(solution)/shard_map/pallas_call | solution.py:69
  38.2 5.2 %all-to-all-start.1 = ((f32[16,16,128]{2,1,0:T(8,128)}), f32[16,16,128]{2,1,0:T(8,128)S(1)}, u32[]{:S(2)}, u32[]{:S(2)}) async-start(f32[16,16,128]{2,1,0:T(8,128)} %get-tuple-element.19), calls=%async_computation.1 | async-start | bytes 262144 | tf_op jit(solution)/shard_map/all_to_all | solution.py:650
  43.4 0.0 collective-permute-done.5.refs_5_
  43.4 0.0 copy-start
  43.4 0.0 collective-permute-done.4.refs_3_
  43.4 0.0 copy-start.2
  43.4 4.5 %all-to-all-done.1.refs_0_ = f32[16,16,128]{2,1,0:T(8,128)S(1)} async-done(((f32[16,16,128]{2,1,0:T(8,128)}), f32[16,16,128]{2,1,0:T(8,128)S(1)}, u32[]{:S(2)}, u32[]{:S(2)}) %all-to-all-start.1) | async-done | bytes 131104 | tf_op jit(solution)/shard_map/all_to_all | solution.py:650
  47.9 0.0 copy-done
  47.9 0.7 %copy-done.1 = f32[16,16,128]{2,1,0:T(8,128)} copy-done((f32[16,16,128]{2,1,0:T(8,128)}, f32[16,16,128]{2,1,0:T(8,128)S(1)}, u32[]{:S(2)}) %copy-start.1) | copy-done | bytes 131096
  48.5 3.3 %shard_map.145 = bf16[32,768]{1,0:T(8,128)(2,1)} custom-call(f32[16,16,128]{2,1,0:T(8,128)} %copy-done.1, bf16[768,768]{1,0:T(8,128)(2,1)} %refs_1_.7, f32[2,352,128]{2,1,0:T(8,128)} %get-tuple-element.16.refs_1_.refs_10_.refs_2_, f32[2,352,128]{2,1,0:T(8,128)} %copy-done.2, bf16[2,256,768]{2,1,0:T(8,128)(2,1)} %get-tuple-element.21.refs_4_, ...), custom_call_target="tpu_custom_call" | custom-call | flops 201326592 | bytes 3653632 | tf_op jit(solution)/shard_map/pallas_call | solution.py:69
  (7 shorter events, 0.0 us)
Async XLA Ops:
  4.0 14.9 %all-to-all-start = ((f32[8,4,16,128]{3,2,1,0:T(8,128)}), f32[8,4,16,128]{3,2,1,0:T(8,128)S(1)}, u32[]{:S(2)}, u32[]{:S(2)}) async-start(f32[8,4,16,128]{3,2,1,0:T(8,128)} %get-tuple-element.12.refs_6_), calls=%async_computation | async-start | bytes 524288 | tf_op jit(solution)/shard_map/all_to_all | solution.py:523
  11.8 15.8 %collective-permute-start.3 = (bf16[16,128,128]{2,1,0:T(8,128)(2,1)}, bf16[16,128,128]{2,1,0:T(8,128)(2,1)S(1)}, u32[]{:S(2)}, u32[]{:S(2)}) collective-permute-start(bf16[16,128,128]{2,1,0:T(8,128)(2,1)} %get-tuple-element.17.refs_8_), channel_id=1, source_target_pairs={{16,0},{0,16},{17,1},{1,17},{18,2},{2,18},{19,3},{3,19},{20,4},{4,... | collective-permute-start | bytes 1572872 | tf_op jit(solution)/shard_map/ppermute | solution.py:527
  18.8 24.6 %collective-permute-start.5 = (bf16[2,256,768]{2,1,0:T(8,128)(2,1)}, bf16[2,256,768]{2,1,0:T(8,128)(2,1)S(1)}, u32[]{:S(2)}, u32[]{:S(2)}) collective-permute-start(bf16[2,256,768]{2,1,0:T(8,128)(2,1)} %get-tuple-element.21.refs_4_), channel_id=1, source_target_pairs={{1,0},{0,1},{3,2},{2,3},{5,4},{4,5},{7,6},{6,7},{9,8},{8,9},{11,10... | collective-permute-start | bytes 2359304 | tf_op jit(solution)/shard_map/ppermute | solution.py:602
  18.9 1.8 %copy-start.4 = (f32[2,2,4,16,128]{4,3,2,1,0:T(8,128)}, f32[2,2,4,16,128]{4,3,2,1,0:T(8,128)S(1)}, u32[]{:S(2)}) copy-start(f32[2,2,4,16,128]{4,3,2,1,0:T(8,128)S(1)} %constant_dynamic-slice_fusion.refs_5_.refs_4_) | copy-start | bytes 393220
  18.9 5.9 %collective-permute-start.1 = (f32[2,2,4,16,128]{4,3,2,1,0:T(8,128)S(1)}, f32[2,2,4,16,128]{4,3,2,1,0:T(8,128)S(1)}, u32[]{:S(2)}, u32[]{:S(2)}) collective-permute-start(f32[2,2,4,16,128]{4,3,2,1,0:T(8,128)S(1)} %constant_dynamic-slice_fusion.refs_5_.refs_4_), channel_id=1, source_target_pairs={{2,0},{3,1},{0,2},{1,3},{6,4},{7,5},{4,6},{5,7},{10,8},{11,9},{8,1... | collective-permute-start | bytes 393224 | tf_op jit(solution)/shard_map/ppermute | solution.py:596
  20.5 7.1 %collective-permute-start = (f32[2,2,4,16,128]{4,3,2,1,0:T(8,128)S(1)}, f32[2,2,4,16,128]{4,3,2,1,0:T(8,128)S(1)}, u32[]{:S(2)}, u32[]{:S(2)}) collective-permute-start(f32[2,2,4,16,128]{4,3,2,1,0:T(8,128)S(1)} %constant_dynamic-slice_fusion.refs_5_.refs_4_), channel_id=1, source_target_pairs={{1,0},{0,1},{3,2},{2,3},{5,4},{4,5},{7,6},{6,7},{9,8},{8,9},{11,10... | collective-permute-start | bytes 393224 | tf_op jit(solution)/shard_map/ppermute | solution.py:596
  24.9 0.7 %copy-start.3 = (f32[2,2,4,16,128]{4,3,2,1,0:T(8,128)}, f32[2,2,4,16,128]{4,3,2,1,0:T(8,128)S(1)}, u32[]{:S(2)}) copy-start(f32[2,2,4,16,128]{4,3,2,1,0:T(8,128)S(1)} %collective-permute-done.1.refs_0_) | copy-start | bytes 393220
  25.5 2.1 %collective-permute-start.2 = (f32[2,2,4,16,128]{4,3,2,1,0:T(8,128)}, f32[2,2,4,16,128]{4,3,2,1,0:T(8,128)S(1)}, u32[]{:S(2)}, u32[]{:S(2)}) collective-permute-start(f32[2,2,4,16,128]{4,3,2,1,0:T(8,128)} %shard_map.143.refs_6_), channel_id=1, source_target_pairs={{1,0},{0,1},{3,2},{2,3},{5,4},{4,5},{7,6},{6,7},{9,8},{8,9},{11,10... | collective-permute-start | bytes 393224 | tf_op jit(solution)/shard_map/ppermute | solution.py:596
  25.5 17.9 %collective-permute-start.4 = (f32[2,352,128]{2,1,0:T(8,128)}, f32[2,352,128]{2,1,0:T(8,128)S(1)}, u32[]{:S(2)}, u32[]{:S(2)}) collective-permute-start(f32[2,352,128]{2,1,0:T(8,128)} %get-tuple-element.20), channel_id=1, source_target_pairs={{1,0},{0,1},{3,2},{2,3},{5,4},{4,5},{7,6},{6,7},{9,8},{8,9},{11,10... | collective-permute-start | bytes 1081352 | tf_op jit(solution)/shard_map/ppermute | solution.py:603
  27.6 0.8 %copy-start.5 = (bf16[16,128,128]{2,1,0:T(8,128)(2,1)}, bf16[16,128,128]{2,1,0:T(8,128)(2,1)S(1)}, u32[]{:S(2)}) copy-start(bf16[16,128,128]{2,1,0:T(8,128)(2,1)S(1)} %collective-permute-done.3.refs_9_) | copy-start | bytes 1572868
  27.6 0.9 %copy-start.6 = (f32[2,2,4,16,128]{4,3,2,1,0:T(8,128)}, f32[2,2,4,16,128]{4,3,2,1,0:T(8,128)S(1)}, u32[]{:S(2)}) copy-start(f32[2,2,4,16,128]{4,3,2,1,0:T(8,128)S(1)} %collective-permute-done.refs_5_) | copy-start | bytes 393220
  27.6 0.9 %copy-start.7 = (f32[2,2,4,16,128]{4,3,2,1,0:T(8,128)}, f32[2,2,4,16,128]{4,3,2,1,0:T(8,128)S(1)}, u32[]{:S(2)}) copy-start(f32[2,2,4,16,128]{4,3,2,1,0:T(8,128)S(1)} %collective-permute-done.2.refs_7_) | copy-start | bytes 393220
  38.2 9.7 %all-to-all-start.1 = ((f32[16,16,128]{2,1,0:T(8,128)}), f32[16,16,128]{2,1,0:T(8,128)S(1)}, u32[]{:S(2)}, u32[]{:S(2)}) async-start(f32[16,16,128]{2,1,0:T(8,128)} %get-tuple-element.19), calls=%async_computation.1 | async-start | bytes 262144 | tf_op jit(solution)/shard_map/all_to_all | solution.py:650
  43.4 4.5 %copy-start = (bf16[2,256,768]{2,1,0:T(8,128)(2,1)}, bf16[2,256,768]{2,1,0:T(8,128)(2,1)S(1)}, u32[]{:S(2)}) copy-start(bf16[2,256,768]{2,1,0:T(8,128)(2,1)S(1)} %collective-permute-done.5.refs_5_) | copy-start | bytes 2359300
  43.4 4.5 %copy-start.2 = (f32[2,352,128]{2,1,0:T(8,128)}, f32[2,352,128]{2,1,0:T(8,128)S(1)}, u32[]{:S(2)}) copy-start(f32[2,352,128]{2,1,0:T(8,128)S(1)} %collective-permute-done.4.refs_3_) | copy-start | bytes 1081348
  47.9 0.7 %copy-start.1 = (f32[16,16,128]{2,1,0:T(8,128)}, f32[16,16,128]{2,1,0:T(8,128)S(1)}, u32[]{:S(2)}) copy-start(f32[16,16,128]{2,1,0:T(8,128)S(1)} %all-to-all-done.1.refs_0_) | copy-start | bytes 393220

commit v2 on v1

--- a/solution.py
+++ b/solution.py
@@ -22,6 +22,7 @@
 SIGMA_MIN = 0.0004
 
 VMEM_LIMIT = 60 << 20
+NEAR_LIMIT = 48 << 20
 
 F32 = jnp.float32
 BF16 = jnp.bfloat16
@@ -57,8 +58,8 @@
     return pltpu.VMEM(operand.shape, operand.dtype)
 
 
-def call(kernel, out_shape, operands, scratch=(), copies=0, after=(), flops=0, exps=0):
-    in_specs = [pl.BlockSpec(memory_space=pltpu.HBM)] * len(operands)
+def call(kernel, out_shape, operands, scratch=(), copies=0, after=(), near=False, flops=0, exps=0):
+    in_specs = [pl.BlockSpec(memory_space=pltpu.VMEM if near else pltpu.HBM)] * len(operands)
     in_specs += [pl.BlockSpec(memory_space=pl.ANY)] * len(after)
     moved = nbytes(*operands, *out_shape)
     count = len(operands)
@@ -72,7 +73,7 @@
         in_specs=in_specs,
         out_specs=tuple(pl.BlockSpec(memory_space=pltpu.HBM) for _ in out_shape),
         scratch_shapes=[*scratch, pltpu.SemaphoreType.DMA((copies,))],
-        compiler_params=pltpu.CompilerParams(vmem_limit_bytes=VMEM_LIMIT),
+        compiler_params=pltpu.CompilerParams(vmem_limit_bytes=NEAR_LIMIT if near else VMEM_LIMIT),
         cost_estimate=pl.CostEstimate(flops=flops, bytes_accessed=moved, transcendentals=exps),
     )(*operands, *after)
 
@@ -407,71 +408,49 @@
 
 
 def attend_kernel(share, *refs):
-    bias_hbm, weight_hbm = refs[:2]
-    found_hbm, value_hbm, refs = refs[2 : 2 + share], refs[2 + share : 2 + 2 * share], refs[2 + 2 * share :]
-    out_hbm, bias, weight, found, value, out, sems = refs
-    count, tokens, wider = value.shape
-    width = weight.shape[0]
-    each = count // share
-    own = out.shape[0] // count
-    value[:, :, width:] = jnp.ones((count, tokens, wider - width), BF16)
-    firsts = [first_sample(share, each, flip) for flip in range(share)]
-    loads = start(
-        [
-            (bias_hbm, bias),
-            *[(found_hbm[flip], found.at[pl.ds(firsts[flip], each)]) for flip in range(share)],
-            *[
-                (value_hbm[flip].at[at], value.at[firsts[flip] + at, :, pl.ds(0, width)])
-                for flip in range(share)
-                for at in range(each)
-            ],
-            (weight_hbm, weight),
-        ],
-        sems,
-    )
-    for load in loads[: 1 + share]:
-        load.wait()
+    bias, weight, refs = refs[0], refs[1], refs[2:]
+    found, value, refs = refs[:share], refs[share : 2 * share], refs[2 * share :]
+    out_hbm, wide, out, sems = refs
+    count, own, width = wide.shape
+    each, tokens, _ = value[0].shape
     low = lax.axis_size("lo")
     order = turns(bias.shape[0] // low, low)
     turned = jnp.concatenate([bias[order.index(c)] for c in range(len(order))], axis=0)
     masks = head_masks(width)
-    weights = []
-    for sample in range(count):
-        total_scores = found[sample, :tokens] + turned
-        peak = jnp.max(total_scores, axis=0, keepdims=True)
-        weights.append(jnp.exp(total_scores - peak).astype(BF16))
+    ones = jnp.ones((tokens, turned.shape[1]), BF16)
+    turn = (((0,), (0,)), ((), ()))
+    slots = [(flip, at) for flip in range(share) for at in range(each)]
     rows = []
-    for sample in range(count):
-        if sample == 0:
-            for load in loads[1 + share : 1 + share + count]:
-                load.wait()
-        summed = lax.dot_general(
-            weights[sample], value[sample], (((0,), (0,)), ((), ())), preferred_element_type=F32
-        )
-        scale = 1.0 / summed[:, width : width + 1]
-        summed = summed[:, :width] * scale
+    for flip, at in slots:
+        scores = found[flip][at, :tokens] + turned
+        peak = jnp.max(scores, axis=0, keepdims=True)
+        weights = jnp.exp(scores - peak).astype(BF16)
+        summed = lax.dot_general(weights, value[flip][at], turn, preferred_element_type=F32)
+        total = lax.dot_general(weights, ones, turn, preferred_element_type=F32)
+        summed = summed * (1.0 / total[:, :1])
         attended = jnp.where(masks[0], summed[:own], 0.0)
         for head in range(1, HD):
             attended = jnp.where(masks[head], summed[head * own : (head + 1) * own], attended)
         rows.append(attended)
 
     def gates(kind):
-        parts = []
-        lanes = found.shape[2]
-        for sample in range(count):
-            first = tokens + kind * own * (width // lanes)
-            blocks = [
-                found[sample, first + at * own : first + (at + 1) * own]
-                for at in range(width // lanes)
-            ]
-            parts.append(jnp.concatenate(blocks, axis=1))
-        return jnp.concatenate(parts, axis=0)
-
-    loads[-1].wait()
+        lanes = turned.shape[1]
+        first = tokens + kind * own * (width // lanes)
+        places = [slice(first + lane * own, first + (lane + 1) * own) for lane in range(width // lanes)]
+        return jnp.concatenate(
+            [
+                jnp.concatenate([found[flip][at, place] for place in places], axis=1)
+                for flip, at in slots
+            ],
+            axis=0,
+        )
+
     gated = (gates(0) * jnp.concatenate(rows, axis=0)).astype(BF16)
-    projected = jnp.dot(gated, weight[...], preferred_element_type=F32)
-    out[...] = (gates(1) * projected).astype(BF16)
-    for store in start([(out, out_hbm)], sems, len(loads)):
+    projected = gates(1) * jnp.dot(gated, weight[...], preferred_element_type=F32)
+    for slot, (flip, at) in enumerate(slots):
+        wide[first_sample(share, each, flip) + at] = projected[slot * own : (slot + 1) * own]
+    out[...] = wide[...].reshape(count * own, width).astype(BF16)
+    for store in start([(out, out_hbm)], sems):
         store.wait()
 
 
@@ -656,14 +635,9 @@
         functools.partial(attend_kernel, share),
         outs,
         (own_bias, output_weight, *found, *values),
-        scratch=(
-            held(own_bias),
-            held(output_weight),
-            pltpu.VMEM((sample_count, *found_shape.shape[1:]), F32),
-            pltpu.VMEM((sample_count, tokens, width + 128), BF16),
-            held(outs[0]),
-        ),
-        copies=3 + share + sample_count,
+        scratch=(pltpu.VMEM((sample_count, own, width), F32), held(outs[0])),
+        copies=1,
+        near=True,
         flops=2 * sample_count * HD * own * tokens * width,
         exps=sample_count * HD * own * tokens,
     )

time: 52.4 us -> 51.6 us (0.985)
  Pallas kernels: 25.3 us -> 24.7 us
    pallas_call x5, Pallas kernels: 25.3 us -> 24.7 us  [call(): pl.pallas_call(body, out_shape=out_shape, in_specs=in_specs, out_specs=tu...]
  transfers between devices with their start and end apart: 8 -> 8, of which waited for: 3 -> 3; matrix products, arithmetic and copies ran while one was open for 0% -> 0% of each run, Pallas kernels for 36% -> 37%
where the time goes in v2:
time: 51.6 us; the launch traced here: 51.1 us
  Pallas kernels  24.7 us (48%)
  starting transfers between devices  16.8 us (33%)
  waiting for transfers between devices  6.69 us (13%)
  local copies, waits for them, and re-layouts  2.1 us (4%)
  between operations  0.74 us (1%)
    pallas_call x5, Pallas kernels, call(): pl.pallas_call(body, out_shape=out_shape, in_specs=in_specs, out_specs=tu...  24.7 us
    all_to_all x1, starting transfers between devices, local(): lax.all_to_all(bias, ('row', 'hi', 'lo'), split_axis=0, concat_axis=0, ax...  7.82 us
    all_to_all x1, starting transfers between devices, local(): lax.all_to_all(pair_bias, ('hi', 'lo'), split_axis=0, concat_axis=0, axis...  5.19 us
    all_to_all x1, waiting for transfers between devices, local(): lax.all_to_all(pair_bias, ('hi', 'lo'), split_axis=0, concat_axis=0, axis...  4.47 us
    unnamed x16, local copies, waits for them, and re-layouts  2.09 us
    ppermute x3, starting transfers between devices, local(): more = [lax.ppermute(part, 'lo', flip) for part in ready]  1.78 us
    ppermute x1, waiting for transfers between devices, local(): lax.ppermute(normed, 'row', [((r + step) % ranks, r) for r in range(ranks)])  1.59 us
    ppermute x1, starting transfers between devices, local(): lax.ppermute(normed, 'row', [((r + step) % ranks, r) for r in range(ranks)])  1.46 us
  transfers between devices with their start and end apart: 8, of which 3 were waited for; matrix products, arithmetic and copies ran while one was open for 0% of the time, Pallas kernels for 37%

profile of v2, /device:TPU:0, one launch (start us, length us, event | category | flops | bytes accessed | tf_op | source)
XLA Modules:
  0.0 51.1 jit_solution(16085443437088484115)
XLA Ops:
  0.6 3.3 %shard_map.140 = (f32[8,4,16,128]{3,2,1,0:T(8,128)}, bf16[16,128,128]{2,1,0:T(8,128)(2,1)}) custom-call(bf16[128,16,128]{2,1,0:T(8,128)(2,1)} %refs_0_.7, bf16[4,128]{1,0:T(4,128)(2,1)} %bitcast.6), custom_call_target="tpu_custom_call" | custom-call | flops 2097152 | bytes 1311744 | tf_op jit(solution)/shard_map/pallas_call | solution.py:70
  4.0 7.8 %all-to-all-start = ((f32[8,4,16,128]{3,2,1,0:T(8,128)}), f32[8,4,16,128]{3,2,1,0:T(8,128)S(1)}, u32[]{:S(2)}, u32[]{:S(2)}) async-start(f32[8,4,16,128]{3,2,1,0:T(8,128)} %get-tuple-element.12.refs_6_), calls=%async_computation | async-start | bytes 524288 | tf_op jit(solution)/shard_map/all_to_all | solution.py:502
  11.8 1.5 %collective-permute-start.3 = (bf16[16,128,128]{2,1,0:T(8,128)(2,1)}, bf16[16,128,128]{2,1,0:T(8,128)(2,1)S(1)}, u32[]{:S(2)}, u32[]{:S(2)}) collective-permute-start(bf16[16,128,128]{2,1,0:T(8,128)(2,1)} %get-tuple-element.17.refs_8_), channel_id=1, source_target_pairs={{16,0},{0,16},{17,1},{1,17},{18,2},{2,18},{19,3},{3,19},{20,4},{4,... | collective-permute-start | bytes 1572872 | tf_op jit(solution)/shard_map/ppermute | solution.py:506
  13.2 5.6 %shard_map.141 = (bf16[2,256,768]{2,1,0:T(8,128)(2,1)}, bf16[2,256,768]{2,1,0:T(8,128)(2,1)}, bf16[2,16,768]{2,1,0:T(8,128)(2,1)}, bf16[2,16,384]{2,1,0:T(8,128)(2,1)}) custom-call(s32[4]{0:T(128)} %refs_0_.5, bf16[256,384]{1,0:T(8,128)(2,1)} %refs_1_.4, bf16[256,384]{1,0:T(8,128)(2,1)} %refs_2_.2, bf16[384,1536]{1,0:T(8,128)(2,1)} %refs_3_.1, ...), custom_call_target="tpu_custom_call" | custom-call | flops 2415919104 | bytes 9510928 | tf_op jit(solution)/shard_map/pallas_call | solution.py:70
  18.8 0.1 collective-permute-start.5
  18.9 0.0 all-to-all-done
  18.9 0.0 copy-start.4
  18.9 1.6 %collective-permute-start.1 = (f32[2,2,4,16,128]{4,3,2,1,0:T(8,128)S(1)}, f32[2,2,4,16,128]{4,3,2,1,0:T(8,128)S(1)}, u32[]{:S(2)}, u32[]{:S(2)}) collective-permute-start(f32[2,2,4,16,128]{4,3,2,1,0:T(8,128)S(1)} %constant_dynamic-slice_fusion.refs_5_.refs_4_), channel_id=1, source_target_pairs={{2,0},{3,1},{0,2},{1,3},{6,4},{7,5},{4,6},{5,7},{10,8},{11,9},{8,1... | collective-permute-start | bytes 393224 | tf_op jit(solution)/shard_map/ppermute | solution.py:575
  20.5 0.2 collective-permute-start
  20.7 0.0 copy-done.4
  20.7 3.5 %shard_map.142 = (f32[2,352,128]{2,1,0:T(8,128)}, f32[2,352,128]{2,1,0:T(8,128)}) custom-call(bf16[768,3072]{1,0:T(8,128)(2,1)} %refs_0_.6, bf16[384,768]{1,0:T(8,128)(2,1)} %refs_1_.5, bf16[2,16,768]{2,1,0:T(8,128)(2,1)} %get-tuple-element.13.refs_2_, bf16[2,16,384]{2,1,0:T(8,128)(2,1)} %get-tuple-element.14.refs_3_, ...), custom_call_target="tpu_custom_call" | custom-call | flops 2147483648 | bytes 6889472 | tf_op jit(solution)/shard_map/pallas_call | solution.py:70
  24.3 0.6 %collective-permute-done.1.refs_0_ = f32[2,2,4,16,128]{4,3,2,1,0:T(8,128)S(1)} collective-permute-done((f32[2,2,4,16,128]{4,3,2,1,0:T(8,128)S(1)}, f32[2,2,4,16,128]{4,3,2,1,0:T(8,128)S(1)}, u32[]{:S(2)}, u32[]{:S(2)}) %collective-permute-start.1) | collective-permute-done | bytes 131104 | tf_op jit(solution)/shard_map/ppermute | solution.py:575
  24.9 0.0 copy-start.3
  24.9 0.6 %copy-done.3 = f32[2,2,4,16,128]{4,3,2,1,0:T(8,128)} copy-done((f32[2,2,4,16,128]{4,3,2,1,0:T(8,128)}, f32[2,2,4,16,128]{4,3,2,1,0:T(8,128)S(1)}, u32[]{:S(2)}) %copy-start.3) | copy-done | bytes 131096
  25.5 0.0 collective-permute-start.2
  25.5 0.5 collective-permute-start.4
  26.0 1.6 %collective-permute-done.3.refs_9_ = bf16[16,128,128]{2,1,0:T(8,128)(2,1)S(1)} collective-permute-done((bf16[16,128,128]{2,1,0:T(8,128)(2,1)}, bf16[16,128,128]{2,1,0:T(8,128)(2,1)S(1)}, u32[]{:S(2)}, u32[]{:S(2)}) %collective-permute-start.3) | collective-permute-done | bytes 524320 | tf_op jit(solution)/shard_map/ppermute | solution.py:506
  27.6 0.0 copy-start.5
  27.6 0.0 collective-permute-done.refs_5_
  27.6 0.0 collective-permute-done.2.refs_7_
  27.6 0.8 %copy-done.5 = bf16[16,128,128]{2,1,0:T(8,128)(2,1)} copy-done((bf16[16,128,128]{2,1,0:T(8,128)(2,1)}, bf16[16,128,128]{2,1,0:T(8,128)(2,1)S(1)}, u32[]{:S(2)}) %copy-start.5) | copy-done | bytes 524312
  28.4 0.0 copy-done.6
  28.5 0.6 %copy-done.7 = f32[2,2,4,16,128]{4,3,2,1,0:T(8,128)} copy-done((f32[2,2,4,16,128]{4,3,2,1,0:T(8,128)}, f32[2,2,4,16,128]{4,3,2,1,0:T(8,128)S(1)}, u32[]{:S(2)}) %copy-start.7) | copy-done | bytes 131096
  29.1 9.8 %shard_map.144 = (bf16[128,16,128]{2,1,0:T(8,128)(2,1)}, f32[16,16,128]{2,1,0:T(8,128)}) custom-call(bf16[128,16,128]{2,1,0:T(8,128)(2,1)} %refs_0_.7, bf16[128,512]{1,0:T(8,128)(2,1)} %refs_1_.6, bf16[128,128]{1,0:T(8,128)(2,1)} %refs_2_.3, bf16[16,128]{1,0:T(8,128)(2,1)} %bitcast.7, f32[2,2,4,16,128]{4,3,2,1,0:T(8,128)} %copy-done.4, ...), custom_call_target="tpu_custom_call" | custom-call | flops 1073741824 | bytes 2920448 | tf_op jit(solution)/shard_map/pallas_call | solution.py:70
  38.9 5.2 %all-to-all-start.1 = ((f32[16,16,128]{2,1,0:T(8,128)}), f32[16,16,128]{2,1,0:T(8,128)S(1)}, u32[]{:S(2)}, u32[]{:S(2)}) async-start(f32[16,16,128]{2,1,0:T(8,128)} %get-tuple-element.19), calls=%async_computation.1 | async-start | bytes 262144 | tf_op jit(solution)/shard_map/all_to_all | solution.py:629
  44.1 0.0 collective-permute-done.5.refs_5_
  44.1 0.0 collective-permute-done.4.refs_3_
  44.1 4.5 %all-to-all-done.1.refs_0_ = f32[16,16,128]{2,1,0:T(8,128)S(1)} async-done(((f32[16,16,128]{2,1,0:T(8,128)}), f32[16,16,128]{2,1,0:T(8,128)S(1)}, u32[]{:S(2)}, u32[]{:S(2)}) %all-to-all-start.1) | async-done | bytes 131104 | tf_op jit(solution)/shard_map/all_to_all | solution.py:629
  48.6 0.0 copy-done
  48.6 0.0 copy-done.1
  48.6 0.0 copy-done.2
  48.6 2.5 %shard_map.145 = bf16[32,768]{1,0:T(8,128)(2,1)} custom-call(f32[16,16,128]{2,1,0:T(8,128)S(1)} %all-to-all-done.1.refs_0_, bf16[768,768]{1,0:T(8,128)(2,1)S(1)} %copy-done.1, f32[2,352,128]{2,1,0:T(8,128)S(1)} %copy-done, f32[2,352,128]{2,1,0:T(8,128)} %collective-permute-done.4.refs_3_, bf16[2,256,768]{2,1,0:T(8,128)(2,1)S(1)} %copy-done.2, ...), custom_call_target="tpu_custom_call" | custom-call | flops 201326592 | bytes 3653632 | tf_op jit(solution)/shard_map/pallas_call | solution.py:70
  (7 shorter events, 0.0 us)
Async XLA Ops:
  4.0 14.9 %all-to-all-start = ((f32[8,4,16,128]{3,2,1,0:T(8,128)}), f32[8,4,16,128]{3,2,1,0:T(8,128)S(1)}, u32[]{:S(2)}, u32[]{:S(2)}) async-start(f32[8,4,16,128]{3,2,1,0:T(8,128)} %get-tuple-element.12.refs_6_), calls=%async_computation | async-start | bytes 524288 | tf_op jit(solution)/shard_map/all_to_all | solution.py:502
  11.8 15.8 %collective-permute-start.3 = (bf16[16,128,128]{2,1,0:T(8,128)(2,1)}, bf16[16,128,128]{2,1,0:T(8,128)(2,1)S(1)}, u32[]{:S(2)}, u32[]{:S(2)}) collective-permute-start(bf16[16,128,128]{2,1,0:T(8,128)(2,1)} %get-tuple-element.17.refs_8_), channel_id=1, source_target_pairs={{16,0},{0,16},{17,1},{1,17},{18,2},{2,18},{19,3},{3,19},{20,4},{4,... | collective-permute-start | bytes 1572872 | tf_op jit(solution)/shard_map/ppermute | solution.py:506
  18.8 25.3 %collective-permute-start.5 = (bf16[2,256,768]{2,1,0:T(8,128)(2,1)}, bf16[2,256,768]{2,1,0:T(8,128)(2,1)S(1)}, u32[]{:S(2)}, u32[]{:S(2)}) collective-permute-start(bf16[2,256,768]{2,1,0:T(8,128)(2,1)} %get-tuple-element.21.refs_4_), channel_id=1, source_target_pairs={{1,0},{0,1},{3,2},{2,3},{5,4},{4,5},{7,6},{6,7},{9,8},{8,9},{11,10... | collective-permute-start | bytes 2359304 | tf_op jit(solution)/shard_map/ppermute | solution.py:581
  18.9 1.8 %copy-start.4 = (f32[2,2,4,16,128]{4,3,2,1,0:T(8,128)}, f32[2,2,4,16,128]{4,3,2,1,0:T(8,128)S(1)}, u32[]{:S(2)}) copy-start(f32[2,2,4,16,128]{4,3,2,1,0:T(8,128)S(1)} %constant_dynamic-slice_fusion.refs_5_.refs_4_) | copy-start | bytes 393220
  18.9 5.9 %collective-permute-start.1 = (f32[2,2,4,16,128]{4,3,2,1,0:T(8,128)S(1)}, f32[2,2,4,16,128]{4,3,2,1,0:T(8,128)S(1)}, u32[]{:S(2)}, u32[]{:S(2)}) collective-permute-start(f32[2,2,4,16,128]{4,3,2,1,0:T(8,128)S(1)} %constant_dynamic-slice_fusion.refs_5_.refs_4_), channel_id=1, source_target_pairs={{2,0},{3,1},{0,2},{1,3},{6,4},{7,5},{4,6},{5,7},{10,8},{11,9},{8,1... | collective-permute-start | bytes 393224 | tf_op jit(solution)/shard_map/ppermute | solution.py:575
  20.5 7.1 %collective-permute-start = (f32[2,2,4,16,128]{4,3,2,1,0:T(8,128)S(1)}, f32[2,2,4,16,128]{4,3,2,1,0:T(8,128)S(1)}, u32[]{:S(2)}, u32[]{:S(2)}) collective-permute-start(f32[2,2,4,16,128]{4,3,2,1,0:T(8,128)S(1)} %constant_dynamic-slice_fusion.refs_5_.refs_4_), channel_id=1, source_target_pairs={{1,0},{0,1},{3,2},{2,3},{5,4},{4,5},{7,6},{6,7},{9,8},{8,9},{11,10... | collective-permute-start | bytes 393224 | tf_op jit(solution)/shard_map/ppermute | solution.py:575
  24.9 0.6 %copy-start.3 = (f32[2,2,4,16,128]{4,3,2,1,0:T(8,128)}, f32[2,2,4,16,128]{4,3,2,1,0:T(8,128)S(1)}, u32[]{:S(2)}) copy-start(f32[2,2,4,16,128]{4,3,2,1,0:T(8,128)S(1)} %collective-permute-done.1.refs_0_) | copy-start | bytes 393220
  25.5 2.1 %collective-permute-start.2 = (f32[2,2,4,16,128]{4,3,2,1,0:T(8,128)}, f32[2,2,4,16,128]{4,3,2,1,0:T(8,128)S(1)}, u32[]{:S(2)}, u32[]{:S(2)}) collective-permute-start(f32[2,2,4,16,128]{4,3,2,1,0:T(8,128)} %shard_map.143.refs_6_), channel_id=1, source_target_pairs={{1,0},{0,1},{3,2},{2,3},{5,4},{4,5},{7,6},{6,7},{9,8},{8,9},{11,10... | collective-permute-start | bytes 393224 | tf_op jit(solution)/shard_map/ppermute | solution.py:575
  25.5 18.5 %collective-permute-start.4 = (f32[2,352,128]{2,1,0:T(8,128)}, f32[2,352,128]{2,1,0:T(8,128)}, u32[]{:S(2)}, u32[]{:S(2)}) collective-permute-start(f32[2,352,128]{2,1,0:T(8,128)} %get-tuple-element.20), channel_id=1, source_target_pairs={{1,0},{0,1},{3,2},{2,3},{5,4},{4,5},{7,6},{6,7},{9,8},{8,9},{11,10... | collective-permute-start | bytes 1081352 | tf_op jit(solution)/shard_map/ppermute | solution.py:582
  27.6 0.8 %copy-start.5 = (bf16[16,128,128]{2,1,0:T(8,128)(2,1)}, bf16[16,128,128]{2,1,0:T(8,128)(2,1)S(1)}, u32[]{:S(2)}) copy-start(bf16[16,128,128]{2,1,0:T(8,128)(2,1)S(1)} %collective-permute-done.3.refs_9_) | copy-start | bytes 1572868
  27.6 0.8 %copy-start.6 = (f32[2,2,4,16,128]{4,3,2,1,0:T(8,128)}, f32[2,2,4,16,128]{4,3,2,1,0:T(8,128)S(1)}, u32[]{:S(2)}) copy-start(f32[2,2,4,16,128]{4,3,2,1,0:T(8,128)S(1)} %collective-permute-done.refs_5_) | copy-start | bytes 393220
  28.4 0.6 %copy-start.7 = (f32[2,2,4,16,128]{4,3,2,1,0:T(8,128)}, f32[2,2,4,16,128]{4,3,2,1,0:T(8,128)S(1)}, u32[]{:S(2)}) copy-start(f32[2,2,4,16,128]{4,3,2,1,0:T(8,128)S(1)} %collective-permute-done.2.refs_7_) | copy-start | bytes 393220
  29.1 19.5 %copy-start = (f32[2,352,128]{2,1,0:T(8,128)S(1)}, f32[2,352,128]{2,1,0:T(8,128)}, u32[]{:S(2)}) copy-start(f32[2,352,128]{2,1,0:T(8,128)} %get-tuple-element.16.refs_1_.refs_10_.refs_2_) | copy-start | bytes 1081348
  29.1 19.5 %copy-start.1 = (bf16[768,768]{1,0:T(8,128)(2,1)S(1)}, bf16[768,768]{1,0:T(8,128)(2,1)}, u32[]{:S(2)}) copy-start(bf16[768,768]{1,0:T(8,128)(2,1)} %refs_1_.7) | copy-start | bytes 3538948
  29.1 19.5 %copy-start.2 = (bf16[2,256,768]{2,1,0:T(8,128)(2,1)S(1)}, bf16[2,256,768]{2,1,0:T(8,128)(2,1)}, u32[]{:S(2)}) copy-start(bf16[2,256,768]{2,1,0:T(8,128)(2,1)} %get-tuple-element.21.refs_4_) | copy-start | bytes 2359300
  38.9 9.7 %all-to-all-start.1 = ((f32[16,16,128]{2,1,0:T(8,128)}), f32[16,16,128]{2,1,0:T(8,128)S(1)}, u32[]{:S(2)}, u32[]{:S(2)}) async-start(f32[16,16,128]{2,1,0:T(8,128)} %get-tuple-element.19), calls=%async_computation.1 | async-start | bytes 262144 | tf_op jit(solution)/shard_map/all_to_all | solution.py:629

commit v3 on v2

--- a/solution.py
+++ b/solution.py
@@ -97,8 +97,11 @@
 
 
 def turns(high, low):
-    slow = sorted(range(high), key=lambda h: (h < high // 2, abs(2 * h - high)))
-    return [h * low + lo for h in slow for lo in range(low)]
+    order = []
+    for h in range(high // 2):
+        for lo in range(low):
+            order += [((high // 2 + h) * low + lo), ((high // 2 - 1 - h) * low + lo)]
+    return order
 
 
 def hold(value, after):
@@ -128,8 +131,9 @@
     loads = start([(weight_hbm, weight)] + [(pair_hbm.at[h], pair.at[h]) for h in slices], sems)
     for at, load in enumerate(loads[1:]):
         load.wait()
-        tile = pair[at * some : (at + 1) * some].astype(F32).reshape(some * cols, channels)
-        wide[at * some * cols : (at + 1) * some * cols, :] = normalize(tile)
+        for first in range(at * some, (at + 1) * some, 8):
+            tile = pair[first : first + 8].astype(F32).reshape(8 * cols, channels)
+            wide[first * cols : (first + 8) * cols, :] = normalize(tile)
     loads[0].wait()
     for col in range(cols):
         one = wide[pl.ds(col, rows, stride=cols), :].astype(BF16)
@@ -279,7 +283,7 @@
     pair, weight, out_weight, bias_weight = refs[:4]
     gathered, normed, new, pair_bias, refs = refs[4], refs[5], refs[6], refs[7], refs[8:]
     bias_rows, bias, query, key, value, gate, wide = refs[:7]
-    slots, sems = (refs[7:10], refs[10:13]), refs[13]
+    slots, renormed, sems = (refs[7:9], refs[9:11]), refs[11], refs[12]
     rows, cols, channels = pair.shape
     width = HT * DT
     span = gathered.shape[2]
@@ -335,7 +339,7 @@
         load.wait()
 
     def score(col, slot):
-        scores, peak, _ = slots[slot]
+        scores, _ = slots[slot]
         own = query[col]
         blocks = []
         for head in range(HT):
@@ -343,15 +347,25 @@
             block = [zeros[0], own[head * DT : (head + 1) * DT], zeros[1]]
             blocks.append(jnp.concatenate([b for b in block if b.shape[0]], axis=0))
         stacked = jnp.concatenate(blocks, axis=1)
-        raw = jnp.dot(key[col], stacked, preferred_element_type=F32) + bias[...]
-        scores[...] = raw
-        peak[...] = jnp.max(raw, axis=0, keepdims=True)
+        scores[...] = jnp.dot(key[col], stacked, preferred_element_type=F32)
 
     def attend(col, slot):
-        scores, peak, weights = slots[slot]
-        exponent = jnp.exp(scores[...] - peak[...])
-        scale = 1.0 / jnp.sum(exponent, axis=0, keepdims=True)
-        weights[...] = exponent.astype(BF16)
+        scores, weights = slots[slot]
+        piece = 32
+        pieces = [slice(at, at + piece) for at in range(0, scores.shape[0], piece)]
+        rough = None
+        for at in pieces:
+            some = (scores[at] + bias[at]).reshape(piece // 8, 8, -1)
+            some = jnp.max(some, axis=0)
+            rough = some if rough is None else jnp.maximum(rough, some)
+        peak = jnp.max(rough, axis=0, keepdims=True)
+        rough = None
+        for at in pieces:
+            exponent = jnp.exp(scores[at] + bias[at] - peak)
+            weights[at] = exponent.astype(BF16)
+            some = jnp.sum(exponent.reshape(piece // 8, 8, -1), axis=0)
+            rough = some if rough is None else rough + some
+        scale = 1.0 / jnp.sum(rough, axis=0, keepdims=True)
         parts = []
         for head in range(0, HT, 2):
             here = slice(head * rows, (head + 2) * rows)
@@ -376,24 +390,27 @@
             score(jnp.minimum(col + 1, cols - 1), (side + 1) % 2)
             attend(col, side % 2)
 
-    updated = (pair[...].astype(F32).reshape(rows * cols, channels) + wide[...]).astype(BF16)
-    new[...] = updated.reshape(rows, cols, channels)
-    stores = start([(new, new_hbm)], sems, len(loads))
     owners, _, lanes = pair_bias.shape
     own = rows // owners
+    for owner in range(owners):
+        here = slice(owner * own, (owner + 1) * own)
+        some = pair[here].astype(F32).reshape(own * cols, channels)
+        some = (some + wide[owner * own * cols : (owner + 1) * own * cols, :]).astype(BF16)
+        new[here] = some.reshape(own, cols, channels)
+        renormed[owner] = normalize(some).astype(BF16).reshape(own, cols, channels)
+    stores = start([(new, new_hbm)], sems, len(loads))
     lane = lax.broadcasted_iota(jnp.int32, (lanes, HD), 0)
     pick = (lane // own == lax.broadcasted_iota(jnp.int32, (lanes, HD), 1)).astype(BF16)
     spread = jnp.dot(pick, bias_weight[...], preferred_element_type=F32)
     token_of = lax.rem(lax.broadcasted_iota(jnp.int32, (lanes, channels), 0), own)
-    renormed = normalize(updated).astype(BF16).reshape(owners, own, cols, channels)
-    total = jnp.zeros((owners * cols, lanes), F32)
-    for token in range(own):
-        total += lax.dot_general(
-            renormed[:, token].reshape(owners * cols, channels),
-            jnp.where(token_of == token, spread, 0.0).astype(BF16),
-            NT,
-            preferred_element_type=F32,
-        )
+    spots = [jnp.where(token_of == token, spread, 0.0).astype(BF16) for token in range(own)]
+    flat = [renormed[:, token].reshape(owners * cols, channels) for token in range(own)]
+    total = lax.dot_general(
+        jnp.concatenate(flat, axis=1),
+        jnp.concatenate(spots, axis=1),
+        NT,
+        preferred_element_type=F32,
+    )
     total = total.reshape(owners, cols, lanes)
     for place, owner in enumerate(turns(owners // low, low)):
         pair_bias[place] = total[owner]
@@ -615,11 +632,11 @@
                 pltpu.VMEM(*slot)
                 for slot in (
                     ((keys, HT * rows), F32),
-                    ((1, HT * rows), F32),
                     ((keys, HT * rows), BF16),
                 )
                 * 2
             ],
+            pltpu.VMEM((col_count, own, cols, channels), BF16),
         ),
         copies=6 + ranks + low,
         after=(found[0],),

time: 51.6 us -> 53 us (1.027)
  waiting for transfers between devices: 6.69 us -> 7.78 us
    all_to_all x1, waiting for transfers between devices: 4.47 us -> 5.56 us  [local(): lax.all_to_all(pair_bias, ('hi', 'lo'), split_axis=0, concat_axis=0, axis...]
where the time goes in v3:
time: 53 us; the launch traced here: 52.7 us
  Pallas kernels  25.2 us (48%)
  starting transfers between devices  16.8 us (32%)
  waiting for transfers between devices  7.78 us (15%)
  local copies, waits for them, and re-layouts  2.1 us (4%)
  between operations  0.74 us (1%)
    pallas_call x5, Pallas kernels, call(): pl.pallas_call(body, out_shape=out_shape, in_specs=in_specs, out_specs=tu...  25.2 us
    all_to_all x1, starting transfers between devices, local(): lax.all_to_all(bias, ('row', 'hi', 'lo'), split_axis=0, concat_axis=0, ax...  7.82 us
    all_to_all x1, waiting for transfers between devices, local(): lax.all_to_all(pair_bias, ('hi', 'lo'), split_axis=0, concat_axis=0, axis...  5.56 us
    all_to_all x1, starting transfers between devices, local(): lax.all_to_all(pair_bias, ('hi', 'lo'), split_axis=0, concat_axis=0, axis...  5.18 us
    unnamed x16, local copies, waits for them, and re-layouts  2.09 us
    ppermute x3, starting transfers between devices, local(): more = [lax.ppermute(part, 'lo', flip) for part in ready]  1.78 us
    ppermute x1, waiting for transfers between devices, local(): lax.ppermute(normed, 'row', [((r + step) % ranks, r) for r in range(ranks)])  1.59 us
    ppermute x1, starting transfers between devices, local(): lax.ppermute(normed, 'row', [((r + step) % ranks, r) for r in range(ranks)])  1.46 us
  transfers between devices with their start and end apart: 8, of which 3 were waited for; matrix products, arithmetic and copies ran while one was open for 0% of the time, Pallas kernels for 37%

profile of v3, /device:TPU:0, one launch (start us, length us, event | category | flops | bytes accessed | tf_op | source)
XLA Modules:
  0.0 52.7 jit_solution(14045762348184150037)
XLA Ops:
  0.6 3.3 %shard_map.140 = (f32[8,4,16,128]{3,2,1,0:T(8,128)}, bf16[16,128,128]{2,1,0:T(8,128)(2,1)}) custom-call(bf16[128,16,128]{2,1,0:T(8,128)(2,1)} %refs_0_.7, bf16[4,128]{1,0:T(4,128)(2,1)} %bitcast.6), custom_call_target="tpu_custom_call" | custom-call | flops 2097152 | bytes 1311744 | tf_op jit(solution)/shard_map/pallas_call | solution.py:70
  4.0 7.8 %all-to-all-start = ((f32[8,4,16,128]{3,2,1,0:T(8,128)}), f32[8,4,16,128]{3,2,1,0:T(8,128)S(1)}, u32[]{:S(2)}, u32[]{:S(2)}) async-start(f32[8,4,16,128]{3,2,1,0:T(8,128)} %get-tuple-element.12.refs_6_), calls=%async_computation | async-start | bytes 524288 | tf_op jit(solution)/shard_map/all_to_all | solution.py:519
  11.8 1.5 %collective-permute-start.3 = (bf16[16,128,128]{2,1,0:T(8,128)(2,1)}, bf16[16,128,128]{2,1,0:T(8,128)(2,1)S(1)}, u32[]{:S(2)}, u32[]{:S(2)}) collective-permute-start(bf16[16,128,128]{2,1,0:T(8,128)(2,1)} %get-tuple-element.17.refs_8_), channel_id=1, source_target_pairs={{16,0},{0,16},{17,1},{1,17},{18,2},{2,18},{19,3},{3,19},{20,4},{4,... | collective-permute-start | bytes 1572872 | tf_op jit(solution)/shard_map/ppermute | solution.py:523
  13.2 5.6 %shard_map.141 = (bf16[2,256,768]{2,1,0:T(8,128)(2,1)}, bf16[2,256,768]{2,1,0:T(8,128)(2,1)}, bf16[2,16,768]{2,1,0:T(8,128)(2,1)}, bf16[2,16,384]{2,1,0:T(8,128)(2,1)}) custom-call(s32[4]{0:T(128)} %refs_0_.5, bf16[256,384]{1,0:T(8,128)(2,1)} %refs_1_.4, bf16[256,384]{1,0:T(8,128)(2,1)} %refs_2_.2, bf16[384,1536]{1,0:T(8,128)(2,1)} %refs_3_.1, ...), custom_call_target="tpu_custom_call" | custom-call | flops 2415919104 | bytes 9510928 | tf_op jit(solution)/shard_map/pallas_call | solution.py:70
  18.8 0.1 collective-permute-start.5
  18.9 0.0 all-to-all-done
  18.9 0.0 copy-start.4
  18.9 1.6 %collective-permute-start.1 = (f32[2,2,4,16,128]{4,3,2,1,0:T(8,128)S(1)}, f32[2,2,4,16,128]{4,3,2,1,0:T(8,128)S(1)}, u32[]{:S(2)}, u32[]{:S(2)}) collective-permute-start(f32[2,2,4,16,128]{4,3,2,1,0:T(8,128)S(1)} %constant_dynamic-slice_fusion.refs_5_.refs_4_), channel_id=1, source_target_pairs={{2,0},{3,1},{0,2},{1,3},{6,4},{7,5},{4,6},{5,7},{10,8},{11,9},{8,1... | collective-permute-start | bytes 393224 | tf_op jit(solution)/shard_map/ppermute | solution.py:592
  20.5 0.2 collective-permute-start
  20.7 0.0 copy-done.4
  20.7 3.5 %shard_map.142 = (f32[2,352,128]{2,1,0:T(8,128)}, f32[2,352,128]{2,1,0:T(8,128)}) custom-call(bf16[768,3072]{1,0:T(8,128)(2,1)} %refs_0_.6, bf16[384,768]{1,0:T(8,128)(2,1)} %refs_1_.5, bf16[2,16,768]{2,1,0:T(8,128)(2,1)} %get-tuple-element.13.refs_2_, bf16[2,16,384]{2,1,0:T(8,128)(2,1)} %get-tuple-element.14.refs_3_, ...), custom_call_target="tpu_custom_call" | custom-call | flops 2147483648 | bytes 6889472 | tf_op jit(solution)/shard_map/pallas_call | solution.py:70
  24.3 0.6 %collective-permute-done.1.refs_0_ = f32[2,2,4,16,128]{4,3,2,1,0:T(8,128)S(1)} collective-permute-done((f32[2,2,4,16,128]{4,3,2,1,0:T(8,128)S(1)}, f32[2,2,4,16,128]{4,3,2,1,0:T(8,128)S(1)}, u32[]{:S(2)}, u32[]{:S(2)}) %collective-permute-start.1) | collective-permute-done | bytes 131104 | tf_op jit(solution)/shard_map/ppermute | solution.py:592
  24.9 0.0 copy-start.3
  24.9 0.6 %copy-done.3 = f32[2,2,4,16,128]{4,3,2,1,0:T(8,128)} copy-done((f32[2,2,4,16,128]{4,3,2,1,0:T(8,128)}, f32[2,2,4,16,128]{4,3,2,1,0:T(8,128)S(1)}, u32[]{:S(2)}) %copy-start.3) | copy-done | bytes 131096
  25.5 0.0 collective-permute-start.2
  25.5 0.5 collective-permute-start.4
  26.0 1.6 %collective-permute-done.3.refs_9_ = bf16[16,128,128]{2,1,0:T(8,128)(2,1)S(1)} collective-permute-done((bf16[16,128,128]{2,1,0:T(8,128)(2,1)}, bf16[16,128,128]{2,1,0:T(8,128)(2,1)S(1)}, u32[]{:S(2)}, u32[]{:S(2)}) %collective-permute-start.3) | collective-permute-done | bytes 524320 | tf_op jit(solution)/shard_map/ppermute | solution.py:523
  27.6 0.0 copy-start.5
  27.6 0.0 collective-permute-done.refs_5_
  27.6 0.0 collective-permute-done.2.refs_7_
  27.6 0.8 %copy-done.5 = bf16[16,128,128]{2,1,0:T(8,128)(2,1)} copy-done((bf16[16,128,128]{2,1,0:T(8,128)(2,1)}, bf16[16,128,128]{2,1,0:T(8,128)(2,1)S(1)}, u32[]{:S(2)}) %copy-start.5) | copy-done | bytes 524312
  28.4 0.0 copy-done.6
  28.5 0.6 %copy-done.7 = f32[2,2,4,16,128]{4,3,2,1,0:T(8,128)} copy-done((f32[2,2,4,16,128]{4,3,2,1,0:T(8,128)}, f32[2,2,4,16,128]{4,3,2,1,0:T(8,128)S(1)}, u32[]{:S(2)}) %copy-start.7) | copy-done | bytes 131096
  29.1 10.3 %shard_map.144 = (bf16[128,16,128]{2,1,0:T(8,128)(2,1)}, f32[16,16,128]{2,1,0:T(8,128)}) custom-call(bf16[128,16,128]{2,1,0:T(8,128)(2,1)} %refs_0_.7, bf16[128,512]{1,0:T(8,128)(2,1)} %refs_1_.6, bf16[128,128]{1,0:T(8,128)(2,1)} %refs_2_.3, bf16[16,128]{1,0:T(8,128)(2,1)} %bitcast.7, f32[2,2,4,16,128]{4,3,2,1,0:T(8,128)} %copy-done.4, ...), custom_call_target="tpu_custom_call" | custom-call | flops 1073741824 | bytes 2920448 | tf_op jit(solution)/shard_map/pallas_call | solution.py:70
  39.4 5.2 %all-to-all-start.1 = ((f32[16,16,128]{2,1,0:T(8,128)}), f32[16,16,128]{2,1,0:T(8,128)S(1)}, u32[]{:S(2)}, u32[]{:S(2)}) async-start(f32[16,16,128]{2,1,0:T(8,128)} %get-tuple-element.19), calls=%async_computation.1 | async-start | bytes 262144 | tf_op jit(solution)/shard_map/all_to_all | solution.py:646
  44.6 0.0 collective-permute-done.5.refs_5_
  44.6 0.0 collective-permute-done.4.refs_3_
  44.6 5.6 %all-to-all-done.1.refs_0_ = f32[16,16,128]{2,1,0:T(8,128)S(1)} async-done(((f32[16,16,128]{2,1,0:T(8,128)}), f32[16,16,128]{2,1,0:T(8,128)S(1)}, u32[]{:S(2)}, u32[]{:S(2)}) %all-to-all-start.1) | async-done | bytes 131104 | tf_op jit(solution)/shard_map/all_to_all | solution.py:646
  50.2 0.0 copy-done
  50.2 0.0 copy-done.1
  50.2 0.0 copy-done.2
  50.2 2.5 %shard_map.145 = bf16[32,768]{1,0:T(8,128)(2,1)} custom-call(f32[16,16,128]{2,1,0:T(8,128)S(1)} %all-to-all-done.1.refs_0_, bf16[768,768]{1,0:T(8,128)(2,1)S(1)} %copy-done.1, f32[2,352,128]{2,1,0:T(8,128)S(1)} %copy-done, f32[2,352,128]{2,1,0:T(8,128)} %collective-permute-done.4.refs_3_, bf16[2,256,768]{2,1,0:T(8,128)(2,1)S(1)} %copy-done.2, ...), custom_call_target="tpu_custom_call" | custom-call | flops 201326592 | bytes 3653632 | tf_op jit(solution)/shard_map/pallas_call | solution.py:70
  (7 shorter events, 0.0 us)
Async XLA Ops:
  4.0 14.9 %all-to-all-start = ((f32[8,4,16,128]{3,2,1,0:T(8,128)}), f32[8,4,16,128]{3,2,1,0:T(8,128)S(1)}, u32[]{:S(2)}, u32[]{:S(2)}) async-start(f32[8,4,16,128]{3,2,1,0:T(8,128)} %get-tuple-element.12.refs_6_), calls=%async_computation | async-start | bytes 524288 | tf_op jit(solution)/shard_map/all_to_all | solution.py:519
  11.8 15.8 %collective-permute-start.3 = (bf16[16,128,128]{2,1,0:T(8,128)(2,1)}, bf16[16,128,128]{2,1,0:T(8,128)(2,1)S(1)}, u32[]{:S(2)}, u32[]{:S(2)}) collective-permute-start(bf16[16,128,128]{2,1,0:T(8,128)(2,1)} %get-tuple-element.17.refs_8_), channel_id=1, source_target_pairs={{16,0},{0,16},{17,1},{1,17},{18,2},{2,18},{19,3},{3,19},{20,4},{4,... | collective-permute-start | bytes 1572872 | tf_op jit(solution)/shard_map/ppermute | solution.py:523
  18.8 25.8 %collective-permute-start.5 = (bf16[2,256,768]{2,1,0:T(8,128)(2,1)}, bf16[2,256,768]{2,1,0:T(8,128)(2,1)S(1)}, u32[]{:S(2)}, u32[]{:S(2)}) collective-permute-start(bf16[2,256,768]{2,1,0:T(8,128)(2,1)} %get-tuple-element.21.refs_4_), channel_id=1, source_target_pairs={{1,0},{0,1},{3,2},{2,3},{5,4},{4,5},{7,6},{6,7},{9,8},{8,9},{11,10... | collective-permute-start | bytes 2359304 | tf_op jit(solution)/shard_map/ppermute | solution.py:598
  18.9 1.8 %copy-start.4 = (f32[2,2,4,16,128]{4,3,2,1,0:T(8,128)}, f32[2,2,4,16,128]{4,3,2,1,0:T(8,128)S(1)}, u32[]{:S(2)}) copy-start(f32[2,2,4,16,128]{4,3,2,1,0:T(8,128)S(1)} %constant_dynamic-slice_fusion.refs_5_.refs_4_) | copy-start | bytes 393220
  18.9 5.9 %collective-permute-start.1 = (f32[2,2,4,16,128]{4,3,2,1,0:T(8,128)S(1)}, f32[2,2,4,16,128]{4,3,2,1,0:T(8,128)S(1)}, u32[]{:S(2)}, u32[]{:S(2)}) collective-permute-start(f32[2,2,4,16,128]{4,3,2,1,0:T(8,128)S(1)} %constant_dynamic-slice_fusion.refs_5_.refs_4_), channel_id=1, source_target_pairs={{2,0},{3,1},{0,2},{1,3},{6,4},{7,5},{4,6},{5,7},{10,8},{11,9},{8,1... | collective-permute-start | bytes 393224 | tf_op jit(solution)/shard_map/ppermute | solution.py:592
  20.5 7.1 %collective-permute-start = (f32[2,2,4,16,128]{4,3,2,1,0:T(8,128)S(1)}, f32[2,2,4,16,128]{4,3,2,1,0:T(8,128)S(1)}, u32[]{:S(2)}, u32[]{:S(2)}) collective-permute-start(f32[2,2,4,16,128]{4,3,2,1,0:T(8,128)S(1)} %constant_dynamic-slice_fusion.refs_5_.refs_4_), channel_id=1, source_target_pairs={{1,0},{0,1},{3,2},{2,3},{5,4},{4,5},{7,6},{6,7},{9,8},{8,9},{11,10... | collective-permute-start | bytes 393224 | tf_op jit(solution)/shard_map/ppermute | solution.py:592
  24.9 0.6 %copy-start.3 = (f32[2,2,4,16,128]{4,3,2,1,0:T(8,128)}, f32[2,2,4,16,128]{4,3,2,1,0:T(8,128)S(1)}, u32[]{:S(2)}) copy-start(f32[2,2,4,16,128]{4,3,2,1,0:T(8,128)S(1)} %collective-permute-done.1.refs_0_) | copy-start | bytes 393220
  25.5 2.1 %collective-permute-start.2 = (f32[2,2,4,16,128]{4,3,2,1,0:T(8,128)}, f32[2,2,4,16,128]{4,3,2,1,0:T(8,128)S(1)}, u32[]{:S(2)}, u32[]{:S(2)}) collective-permute-start(f32[2,2,4,16,128]{4,3,2,1,0:T(8,128)} %shard_map.143.refs_6_), channel_id=1, source_target_pairs={{1,0},{0,1},{3,2},{2,3},{5,4},{4,5},{7,6},{6,7},{9,8},{8,9},{11,10... | collective-permute-start | bytes 393224 | tf_op jit(solution)/shard_map/ppermute | solution.py:592
  25.5 19.1 %collective-permute-start.4 = (f32[2,352,128]{2,1,0:T(8,128)}, f32[2,352,128]{2,1,0:T(8,128)}, u32[]{:S(2)}, u32[]{:S(2)}) collective-permute-start(f32[2,352,128]{2,1,0:T(8,128)} %get-tuple-element.20), channel_id=1, source_target_pairs={{1,0},{0,1},{3,2},{2,3},{5,4},{4,5},{7,6},{6,7},{9,8},{8,9},{11,10... | collective-permute-start | bytes 1081352 | tf_op jit(solution)/shard_map/ppermute | solution.py:599
  27.6 0.8 %copy-start.5 = (bf16[16,128,128]{2,1,0:T(8,128)(2,1)}, bf16[16,128,128]{2,1,0:T(8,128)(2,1)S(1)}, u32[]{:S(2)}) copy-start(bf16[16,128,128]{2,1,0:T(8,128)(2,1)S(1)} %collective-permute-done.3.refs_9_) | copy-start | bytes 1572868
  27.6 0.8 %copy-start.6 = (f32[2,2,4,16,128]{4,3,2,1,0:T(8,128)}, f32[2,2,4,16,128]{4,3,2,1,0:T(8,128)S(1)}, u32[]{:S(2)}) copy-start(f32[2,2,4,16,128]{4,3,2,1,0:T(8,128)S(1)} %collective-permute-done.refs_5_) | copy-start | bytes 393220
  28.4 0.6 %copy-start.7 = (f32[2,2,4,16,128]{4,3,2,1,0:T(8,128)}, f32[2,2,4,16,128]{4,3,2,1,0:T(8,128)S(1)}, u32[]{:S(2)}) copy-start(f32[2,2,4,16,128]{4,3,2,1,0:T(8,128)S(1)} %collective-permute-done.2.refs_7_) | copy-start | bytes 393220
  29.1 21.1 %copy-start = (f32[2,352,128]{2,1,0:T(8,128)S(1)}, f32[2,352,128]{2,1,0:T(8,128)}, u32[]{:S(2)}) copy-start(f32[2,352,128]{2,1,0:T(8,128)} %get-tuple-element.16.refs_1_.refs_10_.refs_2_) | copy-start | bytes 1081348
  29.1 21.1 %copy-start.1 = (bf16[768,768]{1,0:T(8,128)(2,1)S(1)}, bf16[768,768]{1,0:T(8,128)(2,1)}, u32[]{:S(2)}) copy-start(bf16[768,768]{1,0:T(8,128)(2,1)} %refs_1_.7) | copy-start | bytes 3538948
  29.1 21.1 %copy-start.2 = (bf16[2,256,768]{2,1,0:T(8,128)(2,1)S(1)}, bf16[2,256,768]{2,1,0:T(8,128)(2,1)}, u32[]{:S(2)}) copy-start(bf16[2,256,768]{2,1,0:T(8,128)(2,1)} %get-tuple-element.21.refs_4_) | copy-start | bytes 2359300
  39.4 10.8 %all-to-all-start.1 = ((f32[16,16,128]{2,1,0:T(8,128)}), f32[16,16,128]{2,1,0:T(8,128)S(1)}, u32[]{:S(2)}, u32[]{:S(2)}) async-start(f32[16,16,128]{2,1,0:T(8,128)} %get-tuple-element.19), calls=%async_computation.1 | async-start | bytes 262144 | tf_op jit(solution)/shard_map/all_to_all | solution.py:646

commit v4 on v2

--- a/solution.py
+++ b/solution.py
@@ -21,8 +21,6 @@
 SIGMA_MAX = 160.0
 SIGMA_MIN = 0.0004
 
-VMEM_LIMIT = 60 << 20
-NEAR_LIMIT = 48 << 20
 
 F32 = jnp.float32
 BF16 = jnp.bfloat16
@@ -58,8 +56,13 @@
     return pltpu.VMEM(operand.shape, operand.dtype)
 
 
-def call(kernel, out_shape, operands, scratch=(), copies=0, after=(), near=False, flops=0, exps=0):
-    in_specs = [pl.BlockSpec(memory_space=pltpu.VMEM if near else pltpu.HBM)] * len(operands)
+def call(
+    kernel, out_shape, operands, scratch=(), copies=0, after=(), near=(), mib=60, flops=0, exps=0
+):
+    in_specs = [
+        pl.BlockSpec(memory_space=pltpu.VMEM if at in near else pltpu.HBM)
+        for at in range(len(operands))
+    ]
     in_specs += [pl.BlockSpec(memory_space=pl.ANY)] * len(after)
     moved = nbytes(*operands, *out_shape)
     count = len(operands)
@@ -73,7 +76,7 @@
         in_specs=in_specs,
         out_specs=tuple(pl.BlockSpec(memory_space=pltpu.HBM) for _ in out_shape),
         scratch_shapes=[*scratch, pltpu.SemaphoreType.DMA((copies,))],
-        compiler_params=pltpu.CompilerParams(vmem_limit_bytes=NEAR_LIMIT if near else VMEM_LIMIT),
+        compiler_params=pltpu.CompilerParams(vmem_limit_bytes=mib << 20),
         cost_estimate=pl.CostEstimate(flops=flops, bytes_accessed=moved, transcendentals=exps),
     )(*operands, *after)
 
@@ -111,7 +114,7 @@
         ],
         out_specs=pl.BlockSpec(memory_space=pltpu.HBM),
         input_output_aliases={0: 0},
-        compiler_params=pltpu.CompilerParams(vmem_limit_bytes=VMEM_LIMIT),
+        compiler_params=pltpu.CompilerParams(vmem_limit_bytes=48 << 20),
     )(value, after)
 
 
@@ -272,30 +275,17 @@
 
 
 def triangle_kernel(ranks, low, *refs):
-    pair_hbm, weight_hbm, out_weight_hbm, bias_weight_hbm = refs[:4]
-    gathered_hbm, refs = refs[4 : 4 + low], refs[4 + low :]
+    pair, weight, out_weight, bias_weight = refs[:4]
+    gathered, refs = refs[4 : 4 + low], refs[4 + low :]
     normed_hbm, refs = refs[:ranks], refs[ranks:]
     new_hbm, pair_bias_hbm, refs = refs[0], refs[1], refs[2:]
-    pair, weight, out_weight, bias_weight = refs[:4]
-    gathered, normed, new, pair_bias, refs = refs[4], refs[5], refs[6], refs[7], refs[8:]
+    normed, new, pair_bias, refs = refs[0], refs[1], refs[2], refs[3:]
     bias_rows, bias, query, key, value, gate, wide = refs[:7]
-    slots, sems = (refs[7:10], refs[10:13]), refs[13]
+    slots, (gated, renormed, sems) = (refs[7:10], refs[10:13]), refs[13:]
     rows, cols, channels = pair.shape
     width = HT * DT
-    span = gathered.shape[2]
-    loads = start(
-        [
-            (weight_hbm, weight),
-            *[(normed_hbm[at], normed.at[at]) for at in range(ranks)],
-            *[(gathered_hbm[at], gathered.at[at]) for at in range(low)],
-            (pair_hbm, pair),
-            (out_weight_hbm, out_weight),
-            (bias_weight_hbm, bias_weight),
-        ],
-        sems,
-    )
-    for load in loads[: 1 + ranks + low]:
-        load.wait()
+    span = gathered[0].shape[1]
+    loads = start([(normed_hbm[at], normed.at[at]) for at in range(ranks)], sems)
     row, fast = lax.axis_index("row"), lax.axis_index("lo")
     for flip in range(low):
         for slow in range(span):
@@ -304,8 +294,10 @@
             first = pl.multiple_of((block * low + sender) * cols, cols)
             for source in range(ranks):
                 step = lax.rem(source + ranks - row, ranks)
-                bias_rows[step, :, pl.ds(first, cols), :] = gathered[flip, source, slow]
+                bias_rows[step, :, pl.ds(first, cols), :] = gathered[flip][source, slow]
     turned = jnp.transpose(weight[...].astype(F32)).astype(BF16)
+    for load in loads:
+        load.wait()
     own_lines = jnp.concatenate([turned[:width], turned[2 * width :]], axis=0)
     peer_lines = turned[2 * width : 3 * width]
     batch = 4
@@ -331,9 +323,6 @@
             bias[step * rows : (step + 1) * rows, head * rows : (head + 1) * rows] = jnp.transpose(
                 bias_rows[step, head]
             )
-    for load in loads[1 + ranks + low :]:
-        load.wait()
-
     def score(col, slot):
         scores, peak, _ = slots[slot]
         own = query[col]
@@ -362,10 +351,7 @@
             )
             summed = summed * scale[:, here]
             parts += [summed[:DT, :rows], summed[DT:, rows:]]
-        gated = (gate[col] * jnp.concatenate(parts, axis=0)).astype(BF16)
-        wide[pl.ds(col, rows, stride=cols), :] = lax.dot_general(
-            gated, out_weight[...], (((0,), (0,)), ((), ())), preferred_element_type=F32
-        )
+        gated[col] = (gate[col] * jnp.concatenate(parts, axis=0)).astype(BF16)
 
     score(0, 0)
 
@@ -376,24 +362,34 @@
             score(jnp.minimum(col + 1, cols - 1), (side + 1) % 2)
             attend(col, side % 2)
 
-    updated = (pair[...].astype(F32).reshape(rows * cols, channels) + wide[...]).astype(BF16)
-    new[...] = updated.reshape(rows, cols, channels)
-    stores = start([(new, new_hbm)], sems, len(loads))
+    for at in range(0, cols, batch):
+        some = jnp.concatenate([gated[at + side] for side in range(batch)], axis=1)
+        raw = lax.dot_general(
+            some, out_weight[...], (((0,), (0,)), ((), ())), preferred_element_type=F32
+        )
+        for side in range(batch):
+            wide[pl.ds(at + side, rows, stride=cols), :] = raw[side * rows : (side + 1) * rows]
     owners, _, lanes = pair_bias.shape
     own = rows // owners
+    for owner in range(owners):
+        here = slice(owner * own, (owner + 1) * own)
+        some = pair[here].astype(F32).reshape(own * cols, channels)
+        some = (some + wide[owner * own * cols : (owner + 1) * own * cols, :]).astype(BF16)
+        new[here] = some.reshape(own, cols, channels)
+        renormed[owner] = normalize(some).astype(BF16).reshape(own, cols, channels)
+    stores = start([(new, new_hbm)], sems, len(loads))
     lane = lax.broadcasted_iota(jnp.int32, (lanes, HD), 0)
     pick = (lane // own == lax.broadcasted_iota(jnp.int32, (lanes, HD), 1)).astype(BF16)
     spread = jnp.dot(pick, bias_weight[...], preferred_element_type=F32)
     token_of = lax.rem(lax.broadcasted_iota(jnp.int32, (lanes, channels), 0), own)
-    renormed = normalize(updated).astype(BF16).reshape(owners, own, cols, channels)
-    total = jnp.zeros((owners * cols, lanes), F32)
-    for token in range(own):
-        total += lax.dot_general(
-            renormed[:, token].reshape(owners * cols, channels),
-            jnp.where(token_of == token, spread, 0.0).astype(BF16),
-            NT,
-            preferred_element_type=F32,
-        )
+    spots = [jnp.where(token_of == token, spread, 0.0).astype(BF16) for token in range(own)]
+    flat = [renormed[:, token].reshape(owners * cols, channels) for token in range(own)]
+    total = lax.dot_general(
+        jnp.concatenate(flat, axis=1),
+        jnp.concatenate(spots, axis=1),
+        NT,
+        preferred_element_type=F32,
+    )
     total = total.reshape(owners, cols, lanes)
     for place, owner in enumerate(turns(owners // low, low)):
         pair_bias[place] = total[owner]
@@ -565,6 +561,7 @@
             ),
             copies=6 + share,
             after=(gathered[0],),
+            mib=53,
             flops=64 * rows * cols * channels * HT * DT,
         )
     )
@@ -596,11 +593,6 @@
             *peers,
         ),
         scratch=(
-            held(pair_repr),
-            held(tri_weight),
-            held(tri_output_weight),
-            held(pair_weight),
-            pltpu.VMEM((low, ranks, span, HT, cols, rows), F32),
             pltpu.VMEM((ranks, cols, rows, channels), BF16),
             held(outs[0]),
             held(outs[1]),
@@ -620,9 +612,13 @@
                 )
                 * 2
             ],
+            pltpu.VMEM((cols, HT * DT, rows), BF16),
+            pltpu.VMEM((col_count, own, cols, channels), BF16),
         ),
-        copies=6 + ranks + low,
+        copies=2 + ranks,
         after=(found[0],),
+        near=range(4 + low),
+        mib=52,
         flops=4 * HT * rows * cols * keys * HT * DT,
         exps=HT * rows * cols * keys,
     )
@@ -637,7 +633,8 @@
         (own_bias, output_weight, *found, *values),
         scratch=(pltpu.VMEM((sample_count, own, width), F32), held(outs[0])),
         copies=1,
-        near=True,
+        near=range(2 + 2 * share),
+        mib=48,
         flops=2 * sample_count * HD * own * tokens * width,
         exps=sample_count * HD * own * tokens,
     )

time: 51.6 us -> 49.7 us (0.963)
  Pallas kernels: 24.7 us -> 23.4 us
  waiting for transfers between devices: 6.69 us -> 5.59 us
    pallas_call x5, Pallas kernels: 24.7 us -> 23.3 us  [call(): pl.pallas_call(body, out_shape=out_shape, in_specs=in_specs, out_specs=tu...]
    ppermute x3, waiting for transfers between devices: 0.62 us -> 0.01 us  [local(): more = [lax.ppermute(part, 'lo', flip) for part in ready]]
    unnamed x16 -> x18, local copies, waits for them, and re-layouts: 2.09 us -> 2.35 us
  transfers between devices with their start and end apart: 8 -> 8, of which waited for: 3 -> 2; matrix products, arithmetic and copies ran while one was open for 0% -> 0% of each run, Pallas kernels for 37% -> 36%
where the time goes in v4:
time: 49.7 us; the launch traced here: 49 us
  Pallas kernels  23.4 us (47%)
  starting transfers between devices  16.9 us (34%)
  waiting for transfers between devices  5.59 us (11%)
  local copies, waits for them, and re-layouts  2.37 us (5%)
  between operations  0.76 us (2%)
    pallas_call x5, Pallas kernels, call(): pl.pallas_call(body, out_shape=out_shape, in_specs=in_specs, out_specs=tu...  23.3 us
    all_to_all x1, starting transfers between devices, local(): lax.all_to_all(bias, ('row', 'hi', 'lo'), split_axis=0, concat_axis=0, ax...  7.82 us
    all_to_all x1, starting transfers between devices, local(): lax.all_to_all(pair_bias, ('hi', 'lo'), split_axis=0, concat_axis=0, axis...  5.19 us
    all_to_all x1, waiting for transfers between devices, local(): lax.all_to_all(pair_bias, ('hi', 'lo'), split_axis=0, concat_axis=0, axis...  4.47 us
    unnamed x18, local copies, waits for them, and re-layouts  2.35 us
    ppermute x3, starting transfers between devices, local(): more = [lax.ppermute(part, 'lo', flip) for part in ready]  2.17 us
    ppermute x1, starting transfers between devices, local(): lax.ppermute(normed, 'row', [((r + step) % ranks, r) for r in range(ranks)])  1.46 us
    ppermute x1, waiting for transfers between devices, local(): lax.ppermute(normed, 'row', [((r + step) % ranks, r) for r in range(ranks)])  1.1 us
  transfers between devices with their start and end apart: 8, of which 2 were waited for; matrix products, arithmetic and copies ran while one was open for 0% of the time, Pallas kernels for 36%

profile of v4, /device:TPU:0, one launch (start us, length us, event | category | flops | bytes accessed | tf_op | source)
XLA Modules:
  0.0 49.0 jit_solution(4882280589392198621)
XLA Ops:
  0.6 3.3 %shard_map.140 = (f32[8,4,16,128]{3,2,1,0:T(8,128)}, bf16[16,128,128]{2,1,0:T(8,128)(2,1)}) custom-call(bf16[128,16,128]{2,1,0:T(8,128)(2,1)} %refs_0_.7, bf16[4,128]{1,0:T(4,128)(2,1)} %bitcast.7), custom_call_target="tpu_custom_call" | custom-call | flops 2097152 | bytes 1311744 | tf_op jit(solution)/shard_map/pallas_call | solution.py:73
  3.9 7.8 %all-to-all-start = ((f32[8,4,16,128]{3,2,1,0:T(8,128)}), f32[8,4,16,128]{3,2,1,0:T(8,128)S(1)}, u32[]{:S(2)}, u32[]{:S(2)}) async-start(f32[8,4,16,128]{3,2,1,0:T(8,128)} %get-tuple-element.12.refs_6_), calls=%async_computation | async-start | bytes 524288 | tf_op jit(solution)/shard_map/all_to_all | solution.py:498
  11.8 1.5 %collective-permute-start.3 = (bf16[16,128,128]{2,1,0:T(8,128)(2,1)}, bf16[16,128,128]{2,1,0:T(8,128)(2,1)S(1)}, u32[]{:S(2)}, u32[]{:S(2)}) collective-permute-start(bf16[16,128,128]{2,1,0:T(8,128)(2,1)} %get-tuple-element.17.refs_8_), channel_id=1, source_target_pairs={{16,0},{0,16},{17,1},{1,17},{18,2},{2,18},{19,3},{3,19},{20,4},{4,... | collective-permute-start | bytes 1572872 | tf_op jit(solution)/shard_map/ppermute | solution.py:502
  13.2 5.6 %shard_map.141 = (bf16[2,256,768]{2,1,0:T(8,128)(2,1)}, bf16[2,256,768]{2,1,0:T(8,128)(2,1)}, bf16[2,16,768]{2,1,0:T(8,128)(2,1)}, bf16[2,16,384]{2,1,0:T(8,128)(2,1)}) custom-call(s32[4]{0:T(128)} %refs_0_.5, bf16[256,384]{1,0:T(8,128)(2,1)} %refs_1_.4, bf16[256,384]{1,0:T(8,128)(2,1)} %refs_2_.2, bf16[384,1536]{1,0:T(8,128)(2,1)} %refs_3_.1, ...), custom_call_target="tpu_custom_call" | custom-call | flops 2415919104 | bytes 9510928 | tf_op jit(solution)/shard_map/pallas_call | solution.py:73
  18.8 0.1 collective-permute-start.5
  18.9 0.0 all-to-all-done
  18.9 1.6 %collective-permute-start.1 = (f32[2,2,4,16,128]{4,3,2,1,0:T(8,128)S(1)}, f32[2,2,4,16,128]{4,3,2,1,0:T(8,128)S(1)}, u32[]{:S(2)}, u32[]{:S(2)}) collective-permute-start(f32[2,2,4,16,128]{4,3,2,1,0:T(8,128)S(1)} %constant_dynamic-slice_fusion.refs_5_.refs_4_), channel_id=1, source_target_pairs={{2,0},{3,1},{0,2},{1,3},{6,4},{7,5},{4,6},{5,7},{10,8},{11,9},{8,1... | collective-permute-start | bytes 393224 | tf_op jit(solution)/shard_map/ppermute | solution.py:572
  20.5 0.2 collective-permute-start
  20.7 0.8 %copy-done.6 = bf16[2,16,768]{2,1,0:T(8,128)(2,1)S(1)} copy-done((bf16[2,16,768]{2,1,0:T(8,128)(2,1)S(1)}, bf16[2,16,768]{2,1,0:T(8,128)(2,1)}, u32[]{:S(2)}) %copy-start.6) | copy-done | bytes 49176
  21.5 0.7 %copy-done.7 = bf16[2,16,384]{2,1,0:T(8,128)(2,1)S(1)} copy-done((bf16[2,16,384]{2,1,0:T(8,128)(2,1)S(1)}, bf16[2,16,384]{2,1,0:T(8,128)(2,1)}, u32[]{:S(2)}) %copy-start.7) | copy-done | bytes 24600
  22.3 3.7 %shard_map.142 = (f32[2,352,128]{2,1,0:T(8,128)S(1)}, f32[2,352,128]{2,1,0:T(8,128)}) custom-call(bf16[768,3072]{1,0:T(8,128)(2,1)} %refs_0_.6, bf16[384,768]{1,0:T(8,128)(2,1)} %refs_1_.5, bf16[2,16,768]{2,1,0:T(8,128)(2,1)S(1)} %copy-done.6, bf16[2,16,384]{2,1,0:T(8,128)(2,1)S(1)} %copy-done.7, bf16[2,256,768]{2,1,0:T(8,128)(2,1)} %get-tuple-element.15.refs_4_, ...), custom_call_target="tpu_custom_call" | custom-call | flops 2147483648 | bytes 6889472 | tf_op jit(solution)/shard_map/pallas_call | solution.py:73
  25.9 0.0 collective-permute-done.1.refs_0_
  25.9 0.4 collective-permute-start.2
  26.3 0.2 collective-permute-start.4
  26.5 1.1 %collective-permute-done.3.refs_9_ = bf16[16,128,128]{2,1,0:T(8,128)(2,1)S(1)} collective-permute-done((bf16[16,128,128]{2,1,0:T(8,128)(2,1)}, bf16[16,128,128]{2,1,0:T(8,128)(2,1)S(1)}, u32[]{:S(2)}, u32[]{:S(2)}) %collective-permute-start.3) | collective-permute-done | bytes 524320 | tf_op jit(solution)/shard_map/ppermute | solution.py:502
  27.6 0.0 collective-permute-done.refs_5_
  27.6 0.0 collective-permute-done.2.refs_7_
  27.6 0.8 %copy-done.8 = bf16[16,128,128]{2,1,0:T(8,128)(2,1)} copy-done((bf16[16,128,128]{2,1,0:T(8,128)(2,1)}, bf16[16,128,128]{2,1,0:T(8,128)(2,1)S(1)}, u32[]{:S(2)}) %copy-start.8) | copy-done | bytes 524312
  28.4 0.0 copy-done.2
  28.4 0.0 copy-done.3
  28.4 0.0 copy-done.4
  28.4 0.0 copy-done.5
  28.4 0.0 copy-start
  28.4 0.0 copy-start.1
  28.4 8.3 %shard_map.144 = (bf16[128,16,128]{2,1,0:T(8,128)(2,1)}, f32[16,16,128]{2,1,0:T(8,128)}) custom-call(bf16[128,16,128]{2,1,0:T(8,128)(2,1)S(1)} %copy-done.2, bf16[128,512]{1,0:T(8,128)(2,1)S(1)} %copy-done.3, bf16[128,128]{1,0:T(8,128)(2,1)S(1)} %copy-done.4, bf16[16,128]{1,0:T(8,128)(2,1)S(1)} %bitcast.4, ...), custom_call_target="tpu_custom_call" | custom-call | flops 1073741824 | bytes 2920448 | tf_op jit(solution)/shard_map/pallas_call | solution.py:73
  36.8 5.2 %all-to-all-start.1 = ((f32[16,16,128]{2,1,0:T(8,128)}), f32[16,16,128]{2,1,0:T(8,128)S(1)}, u32[]{:S(2)}, u32[]{:S(2)}) async-start(f32[16,16,128]{2,1,0:T(8,128)} %get-tuple-element.19), calls=%async_computation.1 | async-start | bytes 262144 | tf_op jit(solution)/shard_map/all_to_all | solution.py:625
  42.0 0.0 collective-permute-done.5.refs_5_
  42.0 0.0 collective-permute-done.4.refs_3_
  42.0 4.5 %all-to-all-done.1.refs_0_ = f32[16,16,128]{2,1,0:T(8,128)S(1)} async-done(((f32[16,16,128]{2,1,0:T(8,128)}), f32[16,16,128]{2,1,0:T(8,128)S(1)}, u32[]{:S(2)}, u32[]{:S(2)}) %all-to-all-start.1) | async-done | bytes 131104 | tf_op jit(solution)/shard_map/all_to_all | solution.py:625
  46.5 0.0 copy-done
  46.5 0.0 copy-done.1
  46.5 2.5 %shard_map.145 = bf16[32,768]{1,0:T(8,128)(2,1)} custom-call(f32[16,16,128]{2,1,0:T(8,128)S(1)} %all-to-all-done.1.refs_0_, bf16[768,768]{1,0:T(8,128)(2,1)S(1)} %copy-done, f32[2,352,128]{2,1,0:T(8,128)S(1)} %get-tuple-element.16.refs_1_.refs_10_.refs_2_, f32[2,352,128]{2,1,0:T(8,128)} %collective-permute-done.4.refs_3_, ...), custom_call_target="tpu_custom_call" | custom-call | flops 201326592 | bytes 3653632 | tf_op jit(solution)/shard_map/pallas_call | solution.py:73
  (9 shorter events, 0.0 us)
Async XLA Ops:
  3.9 15.0 %all-to-all-start = ((f32[8,4,16,128]{3,2,1,0:T(8,128)}), f32[8,4,16,128]{3,2,1,0:T(8,128)S(1)}, u32[]{:S(2)}, u32[]{:S(2)}) async-start(f32[8,4,16,128]{3,2,1,0:T(8,128)} %get-tuple-element.12.refs_6_), calls=%async_computation | async-start | bytes 524288 | tf_op jit(solution)/shard_map/all_to_all | solution.py:498
  11.8 15.8 %collective-permute-start.3 = (bf16[16,128,128]{2,1,0:T(8,128)(2,1)}, bf16[16,128,128]{2,1,0:T(8,128)(2,1)S(1)}, u32[]{:S(2)}, u32[]{:S(2)}) collective-permute-start(bf16[16,128,128]{2,1,0:T(8,128)(2,1)} %get-tuple-element.17.refs_8_), channel_id=1, source_target_pairs={{16,0},{0,16},{17,1},{1,17},{18,2},{2,18},{19,3},{3,19},{20,4},{4,... | collective-permute-start | bytes 1572872 | tf_op jit(solution)/shard_map/ppermute | solution.py:502
  18.8 23.2 %collective-permute-start.5 = (bf16[2,256,768]{2,1,0:T(8,128)(2,1)}, bf16[2,256,768]{2,1,0:T(8,128)(2,1)S(1)}, u32[]{:S(2)}, u32[]{:S(2)}) collective-permute-start(bf16[2,256,768]{2,1,0:T(8,128)(2,1)} %get-tuple-element.21.refs_4_), channel_id=1, source_target_pairs={{1,0},{0,1},{3,2},{2,3},{5,4},{4,5},{7,6},{6,7},{9,8},{8,9},{11,10... | collective-permute-start | bytes 2359304 | tf_op jit(solution)/shard_map/ppermute | solution.py:578
  18.9 7.0 %collective-permute-start.1 = (f32[2,2,4,16,128]{4,3,2,1,0:T(8,128)S(1)}, f32[2,2,4,16,128]{4,3,2,1,0:T(8,128)S(1)}, u32[]{:S(2)}, u32[]{:S(2)}) collective-permute-start(f32[2,2,4,16,128]{4,3,2,1,0:T(8,128)S(1)} %constant_dynamic-slice_fusion.refs_5_.refs_4_), channel_id=1, source_target_pairs={{2,0},{3,1},{0,2},{1,3},{6,4},{7,5},{4,6},{5,7},{10,8},{11,9},{8,1... | collective-permute-start | bytes 393224 | tf_op jit(solution)/shard_map/ppermute | solution.py:572
  20.5 7.1 %collective-permute-start = (f32[2,2,4,16,128]{4,3,2,1,0:T(8,128)S(1)}, f32[2,2,4,16,128]{4,3,2,1,0:T(8,128)S(1)}, u32[]{:S(2)}, u32[]{:S(2)}) collective-permute-start(f32[2,2,4,16,128]{4,3,2,1,0:T(8,128)S(1)} %constant_dynamic-slice_fusion.refs_5_.refs_4_), channel_id=1, source_target_pairs={{1,0},{0,1},{3,2},{2,3},{5,4},{4,5},{7,6},{6,7},{9,8},{8,9},{11,10... | collective-permute-start | bytes 393224 | tf_op jit(solution)/shard_map/ppermute | solution.py:572
  20.7 0.8 %copy-start.6 = (bf16[2,16,768]{2,1,0:T(8,128)(2,1)S(1)}, bf16[2,16,768]{2,1,0:T(8,128)(2,1)}, u32[]{:S(2)}) copy-start(bf16[2,16,768]{2,1,0:T(8,128)(2,1)} %get-tuple-element.13.refs_2_) | copy-start | bytes 147460
  21.5 0.7 %copy-start.7 = (bf16[2,16,384]{2,1,0:T(8,128)(2,1)S(1)}, bf16[2,16,384]{2,1,0:T(8,128)(2,1)}, u32[]{:S(2)}) copy-start(bf16[2,16,384]{2,1,0:T(8,128)(2,1)} %get-tuple-element.14.refs_3_) | copy-start | bytes 73732
  22.2 6.2 %copy-start.2 = (bf16[128,16,128]{2,1,0:T(8,128)(2,1)S(1)}, bf16[128,16,128]{2,1,0:T(8,128)(2,1)}, u32[]{:S(2)}) copy-start(bf16[128,16,128]{2,1,0:T(8,128)(2,1)} %refs_0_.7) | copy-start | bytes 1572868
  22.2 6.2 %copy-start.3 = (bf16[128,512]{1,0:T(8,128)(2,1)S(1)}, bf16[128,512]{1,0:T(8,128)(2,1)}, u32[]{:S(2)}) copy-start(bf16[128,512]{1,0:T(8,128)(2,1)} %refs_1_.6) | copy-start | bytes 393220
  22.2 6.2 %copy-start.4 = (bf16[128,128]{1,0:T(8,128)(2,1)S(1)}, bf16[128,128]{1,0:T(8,128)(2,1)}, u32[]{:S(2)}) copy-start(bf16[128,128]{1,0:T(8,128)(2,1)} %refs_2_.3) | copy-start | bytes 98308
  22.2 6.2 %copy-start.5 = (bf16[128,16]{0,1:T(8,128)(2,1)S(1)}, bf16[128,16]{0,1:T(8,128)(2,1)}, u32[]{:S(2)}) copy-start(bf16[128,16]{0,1:T(8,128)(2,1)} %param.23) | copy-start | bytes 12292
  25.9 1.7 %collective-permute-start.2 = (f32[2,2,4,16,128]{4,3,2,1,0:T(8,128)S(1)}, f32[2,2,4,16,128]{4,3,2,1,0:T(8,128)S(1)}, u32[]{:S(2)}, u32[]{:S(2)}) collective-permute-start(f32[2,2,4,16,128]{4,3,2,1,0:T(8,128)S(1)} %shard_map.143.refs_6_), channel_id=1, source_target_pairs={{1,0},{0,1},{3,2},{2,3},{5,4},{4,5},{7,6},{6,7},{9,8},{8,9},{11,10... | collective-permute-start | bytes 393224 | tf_op jit(solution)/shard_map/ppermute | solution.py:572
  26.3 15.7 %collective-permute-start.4 = (f32[2,352,128]{2,1,0:T(8,128)}, f32[2,352,128]{2,1,0:T(8,128)}, u32[]{:S(2)}, u32[]{:S(2)}) collective-permute-start(f32[2,352,128]{2,1,0:T(8,128)} %get-tuple-element.20), channel_id=1, source_target_pairs={{1,0},{0,1},{3,2},{2,3},{5,4},{4,5},{7,6},{6,7},{9,8},{8,9},{11,10... | collective-permute-start | bytes 1081352 | tf_op jit(solution)/shard_map/ppermute | solution.py:579
  27.6 0.8 %copy-start.8 = (bf16[16,128,128]{2,1,0:T(8,128)(2,1)}, bf16[16,128,128]{2,1,0:T(8,128)(2,1)S(1)}, u32[]{:S(2)}) copy-start(bf16[16,128,128]{2,1,0:T(8,128)(2,1)S(1)} %collective-permute-done.3.refs_9_) | copy-start | bytes 1572868
  28.4 18.0 %copy-start = (bf16[768,768]{1,0:T(8,128)(2,1)S(1)}, bf16[768,768]{1,0:T(8,128)(2,1)}, u32[]{:S(2)}) copy-start(bf16[768,768]{1,0:T(8,128)(2,1)} %refs_1_.7) | copy-start | bytes 3538948
  28.4 18.0 %copy-start.1 = (bf16[2,256,768]{2,1,0:T(8,128)(2,1)S(1)}, bf16[2,256,768]{2,1,0:T(8,128)(2,1)}, u32[]{:S(2)}) copy-start(bf16[2,256,768]{2,1,0:T(8,128)(2,1)} %get-tuple-element.21.refs_4_) | copy-start | bytes 2359300
  36.8 9.7 %all-to-all-start.1 = ((f32[16,16,128]{2,1,0:T(8,128)}), f32[16,16,128]{2,1,0:T(8,128)S(1)}, u32[]{:S(2)}, u32[]{:S(2)}) async-start(f32[16,16,128]{2,1,0:T(8,128)} %get-tuple-element.19), calls=%async_computation.1 | async-start | bytes 262144 | tf_op jit(solution)/shard_map/all_to_all | solution.py:625

commit v5 on v4

--- a/solution.py
+++ b/solution.py
@@ -100,7 +100,7 @@
 
 
 def turns(high, low):
-    slow = sorted(range(high), key=lambda h: (h < high // 2, abs(2 * h - high)))
+    slow = [(high // 2 + high - 1 + at) % high for at in range(high)]
     return [h * low + lo for h in slow for lo in range(low)]
 
 
@@ -150,11 +150,11 @@
 
 def condition_kernel(share, *refs):
     levels_hbm, cond_hbm, noise_hbm, modulation_hbm, samples_hbm, attention_hbm = refs[:6]
-    key_hbm, value_hbm, rows_hbm, cond_rows_hbm = refs[6:10]
-    levels, cond, noise, modulation, samples, attention, key, value = refs[10:18]
-    adapted, conditions, sems = refs[18:]
+    key_hbm, value_hbm = refs[6:8]
+    levels, cond, noise, modulation, samples, attention, key, value = refs[8:16]
+    adapted, conditions, sems = refs[16:]
     count, tokens, width = samples.shape
-    extra = rows_hbm.shape[1]
+    extra = (key.shape[1] - tokens) // 2
     first = first_sample(share, count)
     loads = start(
         [
@@ -200,45 +200,46 @@
     place, places = own_place()
     chip = lax.div(lax.axis_index("row") * places + place, share) * extra
     here = pl.ds(pl.multiple_of(chip, extra), extra)
-    stores = start(
-        [(adapted.at[:, here], rows_hbm), (conditions.at[:, here], cond_rows_hbm)], sems, 7
-    )
+    key[:, tokens : tokens + extra, :] = adapted[:, here, :]
+    key[:, tokens + extra :, : cond.shape[1]] = conditions[:, here, :]
+    key[:, tokens + extra :, cond.shape[1] :] = jnp.zeros(
+        (count, extra, width - cond.shape[1]), BF16
+    )
+    stores = []
     for at, (part, target) in enumerate(((key, key_hbm), (value, value_hbm))):
         loads[5 + at].wait()
         for sample in range(count):
-            part[sample] = jnp.dot(
+            part[sample, :tokens, :] = jnp.dot(
                 adapted[sample], attention[at], preferred_element_type=F32
             ).astype(BF16)
-        stores += start([(part, target)], sems, 9 + at)
+        stores += start([(part, target)], sems, 7 + at)
     for store in stores:
         store.wait()
 
 
 def token_kernel(share, *refs):
-    attention_hbm, gate_hbm, rows_hbm, cond_hbm, key_hbm = refs[:5]
-    targets, refs = refs[5 : 5 + share], refs[5 + share :]
-    attention, gate_weight, rows, cond, key, found, wide, sems = refs
+    attention_hbm, gate_hbm, key_hbm = refs[:3]
+    targets, refs = refs[3 : 3 + share], refs[3 + share :]
+    attention, gate_weight, key, found, wide, sems = refs
     count, tokens, width = key.shape
-    extra = rows.shape[1]
+    tokens = found.shape[2] - 2 * width // HD
+    extra = (key.shape[1] - tokens) // 2
     own = extra // share
     loads = start(
         [
-            (rows_hbm, rows),
+            (key_hbm, key),
             (attention_hbm.at[:, pl.ds(0, width)], attention.at[0]),
-            (key_hbm, key),
             (attention_hbm.at[:, pl.ds(3 * width, width)], attention.at[1]),
-            (cond_hbm, cond),
             (gate_hbm, gate_weight),
         ],
         sems,
     )
     for load in loads[:2]:
         load.wait()
-    flat = rows[...].reshape(count * extra, width)
+    flat = key[:, tokens : tokens + extra, :].reshape(count * extra, width)
     raw = jnp.dot(flat, attention[0], preferred_element_type=F32)
     query = (raw * DH ** (-0.5)).astype(BF16).astype(F32)
     masks = head_masks(width)
-    loads[2].wait()
     for sample in range(count):
         stacked = []
         for core in range(share):
@@ -246,14 +247,13 @@
             one = query[at : at + own]
             stacked += [jnp.where(m, one, 0.0) for m in masks]
         stacked = jnp.concatenate(stacked, axis=0).astype(BF16)
-        raw = lax.dot_general(key[sample], stacked, NT, preferred_element_type=F32)
+        raw = lax.dot_general(key[sample, :tokens, :], stacked, NT, preferred_element_type=F32)
         for core in range(share):
             found[core, sample, :tokens, :] = raw[:, core * HD * own : (core + 1) * HD * own]
+    loads[2].wait()
+    wide[0] = jax.nn.sigmoid(jnp.dot(flat, attention[1], preferred_element_type=F32))
     loads[3].wait()
-    wide[0] = jax.nn.sigmoid(jnp.dot(flat, attention[1], preferred_element_type=F32))
-    for load in loads[4:]:
-        load.wait()
-    flat = cond[...].reshape(count * extra, cond.shape[2])
+    flat = key[:, tokens + extra :, :].reshape(count * extra, width)[:, : gate_weight.shape[0]]
     wide[1] = jax.nn.sigmoid(jnp.dot(flat, gate_weight[...], preferred_element_type=F32))
     lanes = found.shape[3]
     for core in range(share):
@@ -507,15 +507,10 @@
     each = sample_count // share
     part = (each, tokens, width)
     extra = share * own
-    conditions = single_cond.shape[1]
-    key, value, own_rows, cond_rows = call(
+    key_shape = shape((each, tokens + 2 * extra, width), BF16)
+    key, value = call(
         functools.partial(condition_kernel, share),
-        (
-            shape(part, BF16),
-            shape(part, BF16),
-            shape((each, extra, width), BF16),
-            shape((each, extra, conditions), BF16),
-        ),
+        (key_shape, shape(part, BF16)),
         (
             levels,
             single_cond,
@@ -531,12 +526,12 @@
             held(modulation_weight),
             pltpu.VMEM(part, BF16),
             pltpu.VMEM((2, width, width), BF16),
-            pltpu.VMEM(part, BF16),
+            held(key_shape),
             pltpu.VMEM(part, BF16),
             pltpu.VMEM(part, BF16),
             pltpu.VMEM((each, *single_cond.shape), BF16),
         ),
-        copies=11,
+        copies=9,
         after=(bias,),
         flops=4 * each * tokens * width * 2 * width,
         exps=each * tokens * width,
@@ -549,17 +544,15 @@
         call(
             functools.partial(token_kernel, share),
             (found_shape,) * share,
-            (attention_weight, output_gate_weight, own_rows, cond_rows, key),
+            (attention_weight, output_gate_weight, key),
             scratch=(
                 pltpu.VMEM((2, width, width), BF16),
                 held(output_gate_weight),
-                held(own_rows),
-                held(cond_rows),
                 held(key),
                 pltpu.VMEM((share, *found_shape.shape), F32),
                 pltpu.VMEM((2, each * extra, width), F32),
             ),
-            copies=6 + share,
+            copies=4 + share,
             after=(gathered[0],),
             mib=53,
             flops=64 * rows * cols * channels * HT * DT,

time: 49.7 us -> 50.5 us (1.016)
  waiting for transfers between devices: 5.59 us -> 9.12 us
  local copies, waits for them, and re-layouts: 2.37 us -> 0.82 us
  starting transfers between devices: 16.9 us -> 15.9 us
    all_to_all x1, waiting for transfers between devices: 4.47 us -> 6.55 us  [local(): lax.all_to_all(pair_bias, ('hi', 'lo'), split_axis=0, concat_axis=0, axis...]
    unnamed x18 -> x14, local copies, waits for them, and re-layouts: 2.35 us -> 0.81 us
    ppermute x1, waiting for transfers between devices: 1.1 us -> 2.16 us  [local(): lax.ppermute(normed, 'row', [((r + step) % ranks, r) for r in range(ranks)])]
    all_to_all x1, starting transfers between devices: 5.19 us -> 4.29 us  [local(): lax.all_to_all(pair_bias, ('hi', 'lo'), split_axis=0, concat_axis=0, axis...]
  transfers between devices with their start and end apart: 8 -> 8, of which waited for: 2 -> 3; matrix products, arithmetic and copies ran while one was open for 0% -> 0% of each run, Pallas kernels for 36% -> 35%
where the time goes in v5:
time: 50.5 us; the launch traced here: 50.1 us
  Pallas kernels  23.5 us (47%)
  starting transfers between devices  15.9 us (31%)
  waiting for transfers between devices  9.12 us (18%)
  local copies, waits for them, and re-layouts  0.82 us (2%)
  between operations  0.74 us (1%)
    pallas_call x5, Pallas kernels, call(): pl.pallas_call(body, out_shape=out_shape, in_specs=in_specs, out_specs=tu...  23.5 us
    all_to_all x1, starting transfers between devices, local(): lax.all_to_all(bias, ('row', 'hi', 'lo'), split_axis=0, concat_axis=0, ax...  7.82 us
    all_to_all x1, waiting for transfers between devices, local(): lax.all_to_all(pair_bias, ('hi', 'lo'), split_axis=0, concat_axis=0, axis...  6.55 us
    all_to_all x1, starting transfers between devices, local(): lax.all_to_all(pair_bias, ('hi', 'lo'), split_axis=0, concat_axis=0, axis...  4.29 us
    ppermute x1, waiting for transfers between devices, local(): lax.ppermute(normed, 'row', [((r + step) % ranks, r) for r in range(ranks)])  2.16 us
    ppermute x3, starting transfers between devices, local(): more = [lax.ppermute(part, 'lo', flip) for part in ready]  1.78 us
    ppermute x1, starting transfers between devices, local(): lax.ppermute(normed, 'row', [((r + step) % ranks, r) for r in range(ranks)])  1.46 us
  transfers between devices with their start and end apart: 8, of which 3 were waited for; matrix products, arithmetic and copies ran while one was open for 0% of the time, Pallas kernels for 35%

profile of v5, /device:TPU:0, one launch (start us, length us, event | category | flops | bytes accessed | tf_op | source)
XLA Modules:
  0.0 50.1 jit_solution(6329540359525332956)
XLA Ops:
  0.6 3.3 %shard_map.140 = (f32[8,4,16,128]{3,2,1,0:T(8,128)}, bf16[16,128,128]{2,1,0:T(8,128)(2,1)}) custom-call(bf16[128,16,128]{2,1,0:T(8,128)(2,1)} %refs_0_.7, bf16[4,128]{1,0:T(4,128)(2,1)} %bitcast.7), custom_call_target="tpu_custom_call" | custom-call | flops 2097152 | bytes 1311744 | tf_op jit(solution)/shard_map/pallas_call | solution.py:73
  3.9 7.8 %all-to-all-start = ((f32[8,4,16,128]{3,2,1,0:T(8,128)}), f32[8,4,16,128]{3,2,1,0:T(8,128)S(1)}, u32[]{:S(2)}, u32[]{:S(2)}) async-start(f32[8,4,16,128]{3,2,1,0:T(8,128)} %get-tuple-element.10.refs_6_), calls=%async_computation | async-start | bytes 524288 | tf_op jit(solution)/shard_map/all_to_all | solution.py:498
  11.8 1.5 %collective-permute-start.3 = (bf16[16,128,128]{2,1,0:T(8,128)(2,1)}, bf16[16,128,128]{2,1,0:T(8,128)(2,1)S(1)}, u32[]{:S(2)}, u32[]{:S(2)}) collective-permute-start(bf16[16,128,128]{2,1,0:T(8,128)(2,1)} %get-tuple-element.13.refs_8_), channel_id=1, source_target_pairs={{16,0},{0,16},{17,1},{1,17},{18,2},{2,18},{19,3},{3,19},{20,4},{4,... | collective-permute-start | bytes 1572872 | tf_op jit(solution)/shard_map/ppermute | solution.py:502
  13.2 5.6 %shard_map.141 = (bf16[2,288,768]{2,1,0:T(8,128)(2,1)}, bf16[2,256,768]{2,1,0:T(8,128)(2,1)}) custom-call(s32[4]{0:T(128)} %refs_0_.5, bf16[256,384]{1,0:T(8,128)(2,1)} %refs_1_.4, bf16[256,384]{1,0:T(8,128)(2,1)} %refs_2_.2, bf16[384,1536]{1,0:T(8,128)(2,1)} %refs_3_.1, bf16[4,256,768]{2,1,0:T(8,128)(2,1)} %refs_4_.1, bf16[768,3072]{1,0:T(8,128)(2,1)} %refs_0_.6, ...), custom_call_target="tpu_custom_call" | custom-call | flops 2415919104 | bytes 9535504 | tf_op jit(solution)/shard_map/pallas_call | solution.py:73
  18.9 0.1 collective-permute-start.5
  18.9 0.0 all-to-all-done
  19.0 1.6 %collective-permute-start.1 = (f32[2,2,4,16,128]{4,3,2,1,0:T(8,128)S(1)}, f32[2,2,4,16,128]{4,3,2,1,0:T(8,128)S(1)}, u32[]{:S(2)}, u32[]{:S(2)}) collective-permute-start(f32[2,2,4,16,128]{4,3,2,1,0:T(8,128)S(1)} %constant_dynamic-slice_fusion.refs_3_.refs_4_), channel_id=1, source_target_pairs={{2,0},{3,1},{0,2},{1,3},{6,4},{7,5},{4,6},{5,7},{10,8},{11,9},{8,1... | collective-permute-start | bytes 393224 | tf_op jit(solution)/shard_map/ppermute | solution.py:565
  20.6 0.2 collective-permute-start
  20.8 0.0 copy-start.2
  20.8 0.0 copy-start.3
  20.8 3.7 %shard_map.142 = (f32[2,352,128]{2,1,0:T(8,128)S(1)}, f32[2,352,128]{2,1,0:T(8,128)}) custom-call(bf16[768,3072]{1,0:T(8,128)(2,1)} %refs_0_.6, bf16[384,768]{1,0:T(8,128)(2,1)} %refs_1_.5, bf16[2,288,768]{2,1,0:T(8,128)(2,1)} %get-tuple-element.11.refs_2_, f32[2,2,4,16,128]{4,3,2,1,0:T(8,128)S(1)} %constant_dynamic-slice_fusion.refs_3_.refs_4_), custom_call_target="tpu_custom_call" | custom-call | flops 2147483648 | bytes 6914048 | tf_op jit(solution)/shard_map/pallas_call | solution.py:73
  24.5 0.4 collective-permute-done.1.refs_0_
  24.9 0.0 collective-permute-start.2
  24.9 0.5 %collective-permute-start.4 = (f32[2,352,128]{2,1,0:T(8,128)}, f32[2,352,128]{2,1,0:T(8,128)}, u32[]{:S(2)}, u32[]{:S(2)}) collective-permute-start(f32[2,352,128]{2,1,0:T(8,128)} %get-tuple-element.16), channel_id=1, source_target_pairs={{1,0},{0,1},{3,2},{2,3},{5,4},{4,5},{7,6},{6,7},{9,8},{8,9},{11,10... | collective-permute-start | bytes 1081352 | tf_op jit(solution)/shard_map/ppermute | solution.py:572
  25.4 2.2 %collective-permute-done.3.refs_9_ = bf16[16,128,128]{2,1,0:T(8,128)(2,1)S(1)} collective-permute-done((bf16[16,128,128]{2,1,0:T(8,128)(2,1)}, bf16[16,128,128]{2,1,0:T(8,128)(2,1)S(1)}, u32[]{:S(2)}, u32[]{:S(2)}) %collective-permute-start.3) | collective-permute-done | bytes 524320 | tf_op jit(solution)/shard_map/ppermute | solution.py:502
  27.6 0.0 collective-permute-done.refs_5_
  27.6 0.0 collective-permute-done.2.refs_7_
  27.6 0.8 %copy-done.6 = bf16[16,128,128]{2,1,0:T(8,128)(2,1)} copy-done((bf16[16,128,128]{2,1,0:T(8,128)(2,1)}, bf16[16,128,128]{2,1,0:T(8,128)(2,1)S(1)}, u32[]{:S(2)}) %copy-start.6) | copy-done | bytes 524312
  28.4 0.0 copy-done.2
  28.4 0.0 copy-done.3
  28.4 0.0 copy-done.4
  28.4 0.0 copy-done.5
  28.4 0.0 copy-start
  28.4 0.0 copy-start.1
  28.4 8.3 %shard_map.144 = (bf16[128,16,128]{2,1,0:T(8,128)(2,1)}, f32[16,16,128]{2,1,0:T(8,128)}) custom-call(bf16[128,16,128]{2,1,0:T(8,128)(2,1)S(1)} %copy-done.2, bf16[128,512]{1,0:T(8,128)(2,1)S(1)} %copy-done.3, bf16[128,128]{1,0:T(8,128)(2,1)S(1)} %copy-done.4, bf16[16,128]{1,0:T(8,128)(2,1)S(1)} %bitcast.4, ...), custom_call_target="tpu_custom_call" | custom-call | flops 1073741824 | bytes 2920448 | tf_op jit(solution)/shard_map/pallas_call | solution.py:73
  36.7 4.3 %all-to-all-start.1 = ((f32[16,16,128]{2,1,0:T(8,128)}), f32[16,16,128]{2,1,0:T(8,128)S(1)}, u32[]{:S(2)}, u32[]{:S(2)}) async-start(f32[16,16,128]{2,1,0:T(8,128)} %get-tuple-element.15), calls=%async_computation.1 | async-start | bytes 262144 | tf_op jit(solution)/shard_map/all_to_all | solution.py:618
  41.0 0.0 collective-permute-done.5.refs_5_
  41.0 0.0 collective-permute-done.4.refs_3_
  41.1 6.5 %all-to-all-done.1.refs_0_ = f32[16,16,128]{2,1,0:T(8,128)S(1)} async-done(((f32[16,16,128]{2,1,0:T(8,128)}), f32[16,16,128]{2,1,0:T(8,128)S(1)}, u32[]{:S(2)}, u32[]{:S(2)}) %all-to-all-start.1) | async-done | bytes 131104 | tf_op jit(solution)/shard_map/all_to_all | solution.py:618
  47.6 0.0 copy-done
  47.6 0.0 copy-done.1
  47.6 2.5 %shard_map.145 = bf16[32,768]{1,0:T(8,128)(2,1)} custom-call(f32[16,16,128]{2,1,0:T(8,128)S(1)} %all-to-all-done.1.refs_0_, bf16[768,768]{1,0:T(8,128)(2,1)S(1)} %copy-done, f32[2,352,128]{2,1,0:T(8,128)S(1)} %get-tuple-element.12.refs_1_.refs_10_.refs_2_, f32[2,352,128]{2,1,0:T(8,128)} %collective-permute-done.4.refs_3_, ...), custom_call_target="tpu_custom_call" | custom-call | flops 201326592 | bytes 3653632 | tf_op jit(solution)/shard_map/pallas_call | solution.py:73
  (5 shorter events, 0.0 us)
Async XLA Ops:
  3.9 15.0 %all-to-all-start = ((f32[8,4,16,128]{3,2,1,0:T(8,128)}), f32[8,4,16,128]{3,2,1,0:T(8,128)S(1)}, u32[]{:S(2)}, u32[]{:S(2)}) async-start(f32[8,4,16,128]{3,2,1,0:T(8,128)} %get-tuple-element.10.refs_6_), calls=%async_computation | async-start | bytes 524288 | tf_op jit(solution)/shard_map/all_to_all | solution.py:498
  11.8 15.8 %collective-permute-start.3 = (bf16[16,128,128]{2,1,0:T(8,128)(2,1)}, bf16[16,128,128]{2,1,0:T(8,128)(2,1)S(1)}, u32[]{:S(2)}, u32[]{:S(2)}) collective-permute-start(bf16[16,128,128]{2,1,0:T(8,128)(2,1)} %get-tuple-element.13.refs_8_), channel_id=1, source_target_pairs={{16,0},{0,16},{17,1},{1,17},{18,2},{2,18},{19,3},{3,19},{20,4},{4,... | collective-permute-start | bytes 1572872 | tf_op jit(solution)/shard_map/ppermute | solution.py:502
  18.9 22.2 %collective-permute-start.5 = (bf16[2,256,768]{2,1,0:T(8,128)(2,1)}, bf16[2,256,768]{2,1,0:T(8,128)(2,1)S(1)}, u32[]{:S(2)}, u32[]{:S(2)}) collective-permute-start(bf16[2,256,768]{2,1,0:T(8,128)(2,1)} %get-tuple-element.17.refs_4_), channel_id=1, source_target_pairs={{1,0},{0,1},{3,2},{2,3},{5,4},{4,5},{7,6},{6,7},{9,8},{8,9},{11,10... | collective-permute-start | bytes 2359304 | tf_op jit(solution)/shard_map/ppermute | solution.py:571
  19.0 5.9 %collective-permute-start.1 = (f32[2,2,4,16,128]{4,3,2,1,0:T(8,128)S(1)}, f32[2,2,4,16,128]{4,3,2,1,0:T(8,128)S(1)}, u32[]{:S(2)}, u32[]{:S(2)}) collective-permute-start(f32[2,2,4,16,128]{4,3,2,1,0:T(8,128)S(1)} %constant_dynamic-slice_fusion.refs_3_.refs_4_), channel_id=1, source_target_pairs={{2,0},{3,1},{0,2},{1,3},{6,4},{7,5},{4,6},{5,7},{10,8},{11,9},{8,1... | collective-permute-start | bytes 393224 | tf_op jit(solution)/shard_map/ppermute | solution.py:565
  20.6 7.0 %collective-permute-start = (f32[2,2,4,16,128]{4,3,2,1,0:T(8,128)S(1)}, f32[2,2,4,16,128]{4,3,2,1,0:T(8,128)S(1)}, u32[]{:S(2)}, u32[]{:S(2)}) collective-permute-start(f32[2,2,4,16,128]{4,3,2,1,0:T(8,128)S(1)} %constant_dynamic-slice_fusion.refs_3_.refs_4_), channel_id=1, source_target_pairs={{1,0},{0,1},{3,2},{2,3},{5,4},{4,5},{7,6},{6,7},{9,8},{8,9},{11,10... | collective-permute-start | bytes 393224 | tf_op jit(solution)/shard_map/ppermute | solution.py:565
  20.8 7.6 %copy-start.2 = (bf16[128,16,128]{2,1,0:T(8,128)(2,1)S(1)}, bf16[128,16,128]{2,1,0:T(8,128)(2,1)}, u32[]{:S(2)}) copy-start(bf16[128,16,128]{2,1,0:T(8,128)(2,1)} %refs_0_.7) | copy-start | bytes 1572868
  20.8 7.6 %copy-start.3 = (bf16[128,512]{1,0:T(8,128)(2,1)S(1)}, bf16[128,512]{1,0:T(8,128)(2,1)}, u32[]{:S(2)}) copy-start(bf16[128,512]{1,0:T(8,128)(2,1)} %refs_1_.6) | copy-start | bytes 393220
  20.8 7.6 %copy-start.4 = (bf16[128,128]{1,0:T(8,128)(2,1)S(1)}, bf16[128,128]{1,0:T(8,128)(2,1)}, u32[]{:S(2)}) copy-start(bf16[128,128]{1,0:T(8,128)(2,1)} %refs_2_.3) | copy-start | bytes 98308
  20.8 7.6 %copy-start.5 = (bf16[128,16]{0,1:T(8,128)(2,1)S(1)}, bf16[128,16]{0,1:T(8,128)(2,1)}, u32[]{:S(2)}) copy-start(bf16[128,16]{0,1:T(8,128)(2,1)} %param.23) | copy-start | bytes 12292
  24.9 2.7 %collective-permute-start.2 = (f32[2,2,4,16,128]{4,3,2,1,0:T(8,128)S(1)}, f32[2,2,4,16,128]{4,3,2,1,0:T(8,128)S(1)}, u32[]{:S(2)}, u32[]{:S(2)}) collective-permute-start(f32[2,2,4,16,128]{4,3,2,1,0:T(8,128)S(1)} %shard_map.143.refs_6_), channel_id=1, source_target_pairs={{1,0},{0,1},{3,2},{2,3},{5,4},{4,5},{7,6},{6,7},{9,8},{8,9},{11,10... | collective-permute-start | bytes 393224 | tf_op jit(solution)/shard_map/ppermute | solution.py:565
  24.9 16.1 %collective-permute-start.4 = (f32[2,352,128]{2,1,0:T(8,128)}, f32[2,352,128]{2,1,0:T(8,128)}, u32[]{:S(2)}, u32[]{:S(2)}) collective-permute-start(f32[2,352,128]{2,1,0:T(8,128)} %get-tuple-element.16), channel_id=1, source_target_pairs={{1,0},{0,1},{3,2},{2,3},{5,4},{4,5},{7,6},{6,7},{9,8},{8,9},{11,10... | collective-permute-start | bytes 1081352 | tf_op jit(solution)/shard_map/ppermute | solution.py:572
  27.6 0.8 %copy-start.6 = (bf16[16,128,128]{2,1,0:T(8,128)(2,1)}, bf16[16,128,128]{2,1,0:T(8,128)(2,1)S(1)}, u32[]{:S(2)}) copy-start(bf16[16,128,128]{2,1,0:T(8,128)(2,1)S(1)} %collective-permute-done.3.refs_9_) | copy-start | bytes 1572868
  28.4 19.2 %copy-start = (bf16[768,768]{1,0:T(8,128)(2,1)S(1)}, bf16[768,768]{1,0:T(8,128)(2,1)}, u32[]{:S(2)}) copy-start(bf16[768,768]{1,0:T(8,128)(2,1)} %refs_1_.7) | copy-start | bytes 3538948
  28.4 19.2 %copy-start.1 = (bf16[2,256,768]{2,1,0:T(8,128)(2,1)S(1)}, bf16[2,256,768]{2,1,0:T(8,128)(2,1)}, u32[]{:S(2)}) copy-start(bf16[2,256,768]{2,1,0:T(8,128)(2,1)} %get-tuple-element.17.refs_4_) | copy-start | bytes 2359300
  36.7 10.9 %all-to-all-start.1 = ((f32[16,16,128]{2,1,0:T(8,128)}), f32[16,16,128]{2,1,0:T(8,128)S(1)}, u32[]{:S(2)}, u32[]{:S(2)}) async-start(f32[16,16,128]{2,1,0:T(8,128)} %get-tuple-element.15), calls=%async_computation.1 | async-start | bytes 262144 | tf_op jit(solution)/shard_map/all_to_all | solution.py:618

commit v6 on v5

--- a/solution.py
+++ b/solution.py
@@ -100,8 +100,8 @@
 
 
 def turns(high, low):
-    slow = [(high // 2 + high - 1 + at) % high for at in range(high)]
-    return [h * low + lo for h in slow for lo in range(low)]
+    slow = sorted(range(high), key=lambda h: (h < high // 2, abs(2 * h - high)))
+    return [h * low + lo for h in slow for lo in reversed(range(low))]
 
 
 def hold(value, after):

time: 50.5 us -> 48.5 us (0.960)
  waiting for transfers between devices: 9.12 us -> 6.4 us
  starting transfers between devices: 15.9 us -> 16.6 us
    all_to_all x1, waiting for transfers between devices: 6.55 us -> 3.82 us  [local(): lax.all_to_all(pair_bias, ('hi', 'lo'), split_axis=0, concat_axis=0, axis...]
    all_to_all x1, starting transfers between devices: 4.29 us -> 4.94 us  [local(): lax.all_to_all(pair_bias, ('hi', 'lo'), split_axis=0, concat_axis=0, axis...]
  transfers between devices with their start and end apart: 8 -> 8, of which waited for: 3 -> 3; matrix products, arithmetic and copies ran while one was open for 0% -> 0% of each run, Pallas kernels for 35% -> 37%
where the time goes in v6:
time: 48.5 us; the launch traced here: 48 us
  Pallas kernels  23.5 us (48%)
  starting transfers between devices  16.6 us (34%)
  waiting for transfers between devices  6.4 us (13%)
  local copies, waits for them, and re-layouts  0.82 us (2%)
  between operations  0.74 us (2%)
    pallas_call x5, Pallas kernels, call(): pl.pallas_call(body, out_shape=out_shape, in_specs=in_specs, out_specs=tu...  23.5 us
    all_to_all x1, starting transfers between devices, local(): lax.all_to_all(bias, ('row', 'hi', 'lo'), split_axis=0, concat_axis=0, ax...  7.82 us
    all_to_all x1, starting transfers between devices, local(): lax.all_to_all(pair_bias, ('hi', 'lo'), split_axis=0, concat_axis=0, axis...  4.94 us
    all_to_all x1, waiting for transfers between devices, local(): lax.all_to_all(pair_bias, ('hi', 'lo'), split_axis=0, concat_axis=0, axis...  3.82 us
    ppermute x1, waiting for transfers between devices, local(): lax.ppermute(normed, 'row', [((r + step) % ranks, r) for r in range(ranks)])  2.16 us
    ppermute x3, starting transfers between devices, local(): more = [lax.ppermute(part, 'lo', flip) for part in ready]  1.78 us
    ppermute x1, starting transfers between devices, local(): lax.ppermute(normed, 'row', [((r + step) % ranks, r) for r in range(ranks)])  1.46 us
  transfers between devices with their start and end apart: 8, of which 3 were waited for; matrix products, arithmetic and copies ran while one was open for 0% of the time, Pallas kernels for 37%

profile of v6, /device:TPU:0, one launch (start us, length us, event | category | flops | bytes accessed | tf_op | source)
XLA Modules:
  0.0 48.0 jit_solution(15480665009901122181)
XLA Ops:
  0.6 3.3 %shard_map.140 = (f32[8,4,16,128]{3,2,1,0:T(8,128)}, bf16[16,128,128]{2,1,0:T(8,128)(2,1)}) custom-call(bf16[128,16,128]{2,1,0:T(8,128)(2,1)} %refs_0_.7, bf16[4,128]{1,0:T(4,128)(2,1)} %bitcast.7), custom_call_target="tpu_custom_call" | custom-call | flops 2097152 | bytes 1311744 | tf_op jit(solution)/shard_map/pallas_call | solution.py:73
  3.9 7.8 %all-to-all-start = ((f32[8,4,16,128]{3,2,1,0:T(8,128)}), f32[8,4,16,128]{3,2,1,0:T(8,128)S(1)}, u32[]{:S(2)}, u32[]{:S(2)}) async-start(f32[8,4,16,128]{3,2,1,0:T(8,128)} %get-tuple-element.10.refs_6_), calls=%async_computation | async-start | bytes 524288 | tf_op jit(solution)/shard_map/all_to_all | solution.py:498
  11.8 1.5 %collective-permute-start.3 = (bf16[16,128,128]{2,1,0:T(8,128)(2,1)}, bf16[16,128,128]{2,1,0:T(8,128)(2,1)S(1)}, u32[]{:S(2)}, u32[]{:S(2)}) collective-permute-start(bf16[16,128,128]{2,1,0:T(8,128)(2,1)} %get-tuple-element.13.refs_8_), channel_id=1, source_target_pairs={{16,0},{0,16},{17,1},{1,17},{18,2},{2,18},{19,3},{3,19},{20,4},{4,... | collective-permute-start | bytes 1572872 | tf_op jit(solution)/shard_map/ppermute | solution.py:502
  13.2 5.6 %shard_map.141 = (bf16[2,288,768]{2,1,0:T(8,128)(2,1)}, bf16[2,256,768]{2,1,0:T(8,128)(2,1)}) custom-call(s32[4]{0:T(128)} %refs_0_.5, bf16[256,384]{1,0:T(8,128)(2,1)} %refs_1_.4, bf16[256,384]{1,0:T(8,128)(2,1)} %refs_2_.2, bf16[384,1536]{1,0:T(8,128)(2,1)} %refs_3_.1, bf16[4,256,768]{2,1,0:T(8,128)(2,1)} %refs_4_.1, bf16[768,3072]{1,0:T(8,128)(2,1)} %refs_0_.6, ...), custom_call_target="tpu_custom_call" | custom-call | flops 2415919104 | bytes 9535504 | tf_op jit(solution)/shard_map/pallas_call | solution.py:73
  18.9 0.1 collective-permute-start.5
  18.9 0.0 all-to-all-done
  19.0 1.6 %collective-permute-start.1 = (f32[2,2,4,16,128]{4,3,2,1,0:T(8,128)S(1)}, f32[2,2,4,16,128]{4,3,2,1,0:T(8,128)S(1)}, u32[]{:S(2)}, u32[]{:S(2)}) collective-permute-start(f32[2,2,4,16,128]{4,3,2,1,0:T(8,128)S(1)} %constant_dynamic-slice_fusion.refs_3_.refs_4_), channel_id=1, source_target_pairs={{2,0},{3,1},{0,2},{1,3},{6,4},{7,5},{4,6},{5,7},{10,8},{11,9},{8,1... | collective-permute-start | bytes 393224 | tf_op jit(solution)/shard_map/ppermute | solution.py:565
  20.6 0.2 collective-permute-start
  20.8 0.0 copy-start.2
  20.8 0.0 copy-start.4
  20.8 3.7 %shard_map.142 = (f32[2,352,128]{2,1,0:T(8,128)S(1)}, f32[2,352,128]{2,1,0:T(8,128)}) custom-call(bf16[768,3072]{1,0:T(8,128)(2,1)} %refs_0_.6, bf16[384,768]{1,0:T(8,128)(2,1)} %refs_1_.5, bf16[2,288,768]{2,1,0:T(8,128)(2,1)} %get-tuple-element.11.refs_2_, f32[2,2,4,16,128]{4,3,2,1,0:T(8,128)S(1)} %constant_dynamic-slice_fusion.refs_3_.refs_4_), custom_call_target="tpu_custom_call" | custom-call | flops 2147483648 | bytes 6914048 | tf_op jit(solution)/shard_map/pallas_call | solution.py:73
  24.5 0.4 collective-permute-done.1.refs_0_
  24.9 0.0 collective-permute-start.2
  24.9 0.5 %collective-permute-start.4 = (f32[2,352,128]{2,1,0:T(8,128)}, f32[2,352,128]{2,1,0:T(8,128)}, u32[]{:S(2)}, u32[]{:S(2)}) collective-permute-start(f32[2,352,128]{2,1,0:T(8,128)} %get-tuple-element.16), channel_id=1, source_target_pairs={{1,0},{0,1},{3,2},{2,3},{5,4},{4,5},{7,6},{6,7},{9,8},{8,9},{11,10... | collective-permute-start | bytes 1081352 | tf_op jit(solution)/shard_map/ppermute | solution.py:572
  25.4 2.2 %collective-permute-done.3.refs_9_ = bf16[16,128,128]{2,1,0:T(8,128)(2,1)S(1)} collective-permute-done((bf16[16,128,128]{2,1,0:T(8,128)(2,1)}, bf16[16,128,128]{2,1,0:T(8,128)(2,1)S(1)}, u32[]{:S(2)}, u32[]{:S(2)}) %collective-permute-start.3) | collective-permute-done | bytes 524320 | tf_op jit(solution)/shard_map/ppermute | solution.py:502
  27.6 0.0 collective-permute-done.refs_5_
  27.6 0.0 collective-permute-done.2.refs_7_
  27.6 0.8 %copy-done.6 = bf16[16,128,128]{2,1,0:T(8,128)(2,1)} copy-done((bf16[16,128,128]{2,1,0:T(8,128)(2,1)}, bf16[16,128,128]{2,1,0:T(8,128)(2,1)S(1)}, u32[]{:S(2)}) %copy-start.6) | copy-done | bytes 524312
  28.4 0.0 copy-done.2
  28.4 0.0 copy-done.3
  28.4 0.0 copy-done.4
  28.4 0.0 copy-done.5
  28.4 0.0 copy-start
  28.4 0.0 copy-start.1
  28.4 8.3 %shard_map.144 = (bf16[128,16,128]{2,1,0:T(8,128)(2,1)}, f32[16,16,128]{2,1,0:T(8,128)}) custom-call(bf16[128,16,128]{2,1,0:T(8,128)(2,1)S(1)} %copy-done.2, bf16[128,512]{1,0:T(8,128)(2,1)S(1)} %copy-done.3, bf16[128,128]{1,0:T(8,128)(2,1)S(1)} %copy-done.4, bf16[16,128]{1,0:T(8,128)(2,1)S(1)} %bitcast.4, ...), custom_call_target="tpu_custom_call" | custom-call | flops 1073741824 | bytes 2920448 | tf_op jit(solution)/shard_map/pallas_call | solution.py:73
  36.7 4.9 %all-to-all-start.1 = ((f32[16,16,128]{2,1,0:T(8,128)}), f32[16,16,128]{2,1,0:T(8,128)S(1)}, u32[]{:S(2)}, u32[]{:S(2)}) async-start(f32[16,16,128]{2,1,0:T(8,128)} %get-tuple-element.15), calls=%async_computation.1 | async-start | bytes 262144 | tf_op jit(solution)/shard_map/all_to_all | solution.py:618
  41.7 0.0 collective-permute-done.5.refs_5_
  41.7 0.0 collective-permute-done.4.refs_3_
  41.7 3.8 %all-to-all-done.1.refs_0_ = f32[16,16,128]{2,1,0:T(8,128)S(1)} async-done(((f32[16,16,128]{2,1,0:T(8,128)}), f32[16,16,128]{2,1,0:T(8,128)S(1)}, u32[]{:S(2)}, u32[]{:S(2)}) %all-to-all-start.1) | async-done | bytes 131104 | tf_op jit(solution)/shard_map/all_to_all | solution.py:618
  45.5 0.0 copy-done
  45.5 0.0 copy-done.1
  45.5 2.5 %shard_map.145 = bf16[32,768]{1,0:T(8,128)(2,1)} custom-call(f32[16,16,128]{2,1,0:T(8,128)S(1)} %all-to-all-done.1.refs_0_, bf16[768,768]{1,0:T(8,128)(2,1)S(1)} %copy-done, f32[2,352,128]{2,1,0:T(8,128)S(1)} %get-tuple-element.12.refs_1_.refs_10_.refs_2_, f32[2,352,128]{2,1,0:T(8,128)} %collective-permute-done.4.refs_3_, ...), custom_call_target="tpu_custom_call" | custom-call | flops 201326592 | bytes 3653632 | tf_op jit(solution)/shard_map/pallas_call | solution.py:73
  (5 shorter events, 0.0 us)
Async XLA Ops:
  3.9 15.0 %all-to-all-start = ((f32[8,4,16,128]{3,2,1,0:T(8,128)}), f32[8,4,16,128]{3,2,1,0:T(8,128)S(1)}, u32[]{:S(2)}, u32[]{:S(2)}) async-start(f32[8,4,16,128]{3,2,1,0:T(8,128)} %get-tuple-element.10.refs_6_), calls=%async_computation | async-start | bytes 524288 | tf_op jit(solution)/shard_map/all_to_all | solution.py:498
  11.8 15.8 %collective-permute-start.3 = (bf16[16,128,128]{2,1,0:T(8,128)(2,1)}, bf16[16,128,128]{2,1,0:T(8,128)(2,1)S(1)}, u32[]{:S(2)}, u32[]{:S(2)}) collective-permute-start(bf16[16,128,128]{2,1,0:T(8,128)(2,1)} %get-tuple-element.13.refs_8_), channel_id=1, source_target_pairs={{16,0},{0,16},{17,1},{1,17},{18,2},{2,18},{19,3},{3,19},{20,4},{4,... | collective-permute-start | bytes 1572872 | tf_op jit(solution)/shard_map/ppermute | solution.py:502
  18.9 22.8 %collective-permute-start.5 = (bf16[2,256,768]{2,1,0:T(8,128)(2,1)}, bf16[2,256,768]{2,1,0:T(8,128)(2,1)S(1)}, u32[]{:S(2)}, u32[]{:S(2)}) collective-permute-start(bf16[2,256,768]{2,1,0:T(8,128)(2,1)} %get-tuple-element.17.refs_4_), channel_id=1, source_target_pairs={{1,0},{0,1},{3,2},{2,3},{5,4},{4,5},{7,6},{6,7},{9,8},{8,9},{11,10... | collective-permute-start | bytes 2359304 | tf_op jit(solution)/shard_map/ppermute | solution.py:571
  19.0 5.9 %collective-permute-start.1 = (f32[2,2,4,16,128]{4,3,2,1,0:T(8,128)S(1)}, f32[2,2,4,16,128]{4,3,2,1,0:T(8,128)S(1)}, u32[]{:S(2)}, u32[]{:S(2)}) collective-permute-start(f32[2,2,4,16,128]{4,3,2,1,0:T(8,128)S(1)} %constant_dynamic-slice_fusion.refs_3_.refs_4_), channel_id=1, source_target_pairs={{2,0},{3,1},{0,2},{1,3},{6,4},{7,5},{4,6},{5,7},{10,8},{11,9},{8,1... | collective-permute-start | bytes 393224 | tf_op jit(solution)/shard_map/ppermute | solution.py:565
  20.6 7.0 %collective-permute-start = (f32[2,2,4,16,128]{4,3,2,1,0:T(8,128)S(1)}, f32[2,2,4,16,128]{4,3,2,1,0:T(8,128)S(1)}, u32[]{:S(2)}, u32[]{:S(2)}) collective-permute-start(f32[2,2,4,16,128]{4,3,2,1,0:T(8,128)S(1)} %constant_dynamic-slice_fusion.refs_3_.refs_4_), channel_id=1, source_target_pairs={{1,0},{0,1},{3,2},{2,3},{5,4},{4,5},{7,6},{6,7},{9,8},{8,9},{11,10... | collective-permute-start | bytes 393224 | tf_op jit(solution)/shard_map/ppermute | solution.py:565
  20.8 7.6 %copy-start.2 = (bf16[128,16,128]{2,1,0:T(8,128)(2,1)S(1)}, bf16[128,16,128]{2,1,0:T(8,128)(2,1)}, u32[]{:S(2)}) copy-start(bf16[128,16,128]{2,1,0:T(8,128)(2,1)} %refs_0_.7) | copy-start | bytes 1572868
  20.8 7.6 %copy-start.3 = (bf16[128,512]{1,0:T(8,128)(2,1)S(1)}, bf16[128,512]{1,0:T(8,128)(2,1)}, u32[]{:S(2)}) copy-start(bf16[128,512]{1,0:T(8,128)(2,1)} %refs_1_.6) | copy-start | bytes 393220
  20.8 7.6 %copy-start.4 = (bf16[128,128]{1,0:T(8,128)(2,1)S(1)}, bf16[128,128]{1,0:T(8,128)(2,1)}, u32[]{:S(2)}) copy-start(bf16[128,128]{1,0:T(8,128)(2,1)} %refs_2_.3) | copy-start | bytes 98308
  20.8 7.6 %copy-start.5 = (bf16[128,16]{0,1:T(8,128)(2,1)S(1)}, bf16[128,16]{0,1:T(8,128)(2,1)}, u32[]{:S(2)}) copy-start(bf16[128,16]{0,1:T(8,128)(2,1)} %param.23) | copy-start | bytes 12292
  24.9 2.7 %collective-permute-start.2 = (f32[2,2,4,16,128]{4,3,2,1,0:T(8,128)S(1)}, f32[2,2,4,16,128]{4,3,2,1,0:T(8,128)S(1)}, u32[]{:S(2)}, u32[]{:S(2)}) collective-permute-start(f32[2,2,4,16,128]{4,3,2,1,0:T(8,128)S(1)} %shard_map.143.refs_6_), channel_id=1, source_target_pairs={{1,0},{0,1},{3,2},{2,3},{5,4},{4,5},{7,6},{6,7},{9,8},{8,9},{11,10... | collective-permute-start | bytes 393224 | tf_op jit(solution)/shard_map/ppermute | solution.py:565
  24.9 16.8 %collective-permute-start.4 = (f32[2,352,128]{2,1,0:T(8,128)}, f32[2,352,128]{2,1,0:T(8,128)}, u32[]{:S(2)}, u32[]{:S(2)}) collective-permute-start(f32[2,352,128]{2,1,0:T(8,128)} %get-tuple-element.16), channel_id=1, source_target_pairs={{1,0},{0,1},{3,2},{2,3},{5,4},{4,5},{7,6},{6,7},{9,8},{8,9},{11,10... | collective-permute-start | bytes 1081352 | tf_op jit(solution)/shard_map/ppermute | solution.py:572
  27.6 0.8 %copy-start.6 = (bf16[16,128,128]{2,1,0:T(8,128)(2,1)}, bf16[16,128,128]{2,1,0:T(8,128)(2,1)S(1)}, u32[]{:S(2)}) copy-start(bf16[16,128,128]{2,1,0:T(8,128)(2,1)S(1)} %collective-permute-done.3.refs_9_) | copy-start | bytes 1572868
  28.4 17.1 %copy-start = (bf16[768,768]{1,0:T(8,128)(2,1)S(1)}, bf16[768,768]{1,0:T(8,128)(2,1)}, u32[]{:S(2)}) copy-start(bf16[768,768]{1,0:T(8,128)(2,1)} %refs_1_.7) | copy-start | bytes 3538948
  28.4 17.1 %copy-start.1 = (bf16[2,256,768]{2,1,0:T(8,128)(2,1)S(1)}, bf16[2,256,768]{2,1,0:T(8,128)(2,1)}, u32[]{:S(2)}) copy-start(bf16[2,256,768]{2,1,0:T(8,128)(2,1)} %get-tuple-element.17.refs_4_) | copy-start | bytes 2359300
  36.7 8.8 %all-to-all-start.1 = ((f32[16,16,128]{2,1,0:T(8,128)}), f32[16,16,128]{2,1,0:T(8,128)S(1)}, u32[]{:S(2)}, u32[]{:S(2)}) async-start(f32[16,16,128]{2,1,0:T(8,128)} %get-tuple-element.15), calls=%async_computation.1 | async-start | bytes 262144 | tf_op jit(solution)/shard_map/all_to_all | solution.py:618

commit v7 on v6

--- a/solution.py
+++ b/solution.py
@@ -413,17 +413,21 @@
     order = turns(bias.shape[0] // low, low)
     turned = jnp.concatenate([bias[order.index(c)] for c in range(len(order))], axis=0)
     masks = head_masks(width)
-    ones = jnp.ones((tokens, turned.shape[1]), BF16)
     turn = (((0,), (0,)), ((), ()))
     slots = [(flip, at) for flip in range(share) for at in range(each)]
-    rows = []
+    weights, totals = [], []
     for flip, at in slots:
         scores = found[flip][at, :tokens] + turned
         peak = jnp.max(scores, axis=0, keepdims=True)
-        weights = jnp.exp(scores - peak).astype(BF16)
-        summed = lax.dot_general(weights, value[flip][at], turn, preferred_element_type=F32)
-        total = lax.dot_general(weights, ones, turn, preferred_element_type=F32)
-        summed = summed * (1.0 / total[:, :1])
+        exponent = jnp.exp(scores - peak)
+        weights.append(exponent.astype(BF16))
+        totals.append(jnp.sum(exponent, axis=0, keepdims=True))
+    totals.append(jnp.ones((-count % 8, turned.shape[1]), F32))
+    scale = 1.0 / jnp.transpose(jnp.concatenate([t for t in totals if t.shape[0]], axis=0))
+    rows = []
+    for slot, (flip, at) in enumerate(slots):
+        summed = lax.dot_general(weights[slot], value[flip][at], turn, preferred_element_type=F32)
+        summed = summed * scale[:, slot : slot + 1]
         attended = jnp.where(masks[0], summed[:own], 0.0)
         for head in range(1, HD):
             attended = jnp.where(masks[head], summed[head * own : (head + 1) * own], attended)

time: 48.5 us -> 48.3 us (level)
  no operation moved by 1% of the time
where the time goes in v7:
time: 48.3 us; the launch traced here: 47.9 us
  Pallas kernels  23.3 us (48%)
  starting transfers between devices  16.6 us (34%)
  waiting for transfers between devices  6.4 us (13%)
  local copies, waits for them, and re-layouts  0.82 us (2%)
  between operations  0.74 us (2%)
    pallas_call x5, Pallas kernels, call(): pl.pallas_call(body, out_shape=out_shape, in_specs=in_specs, out_specs=tu...  23.3 us
    all_to_all x1, starting transfers between devices, local(): lax.all_to_all(bias, ('row', 'hi', 'lo'), split_axis=0, concat_axis=0, ax...  7.82 us
    all_to_all x1, starting transfers between devices, local(): lax.all_to_all(pair_bias, ('hi', 'lo'), split_axis=0, concat_axis=0, axis...  4.94 us
    all_to_all x1, waiting for transfers between devices, local(): lax.all_to_all(pair_bias, ('hi', 'lo'), split_axis=0, concat_axis=0, axis...  3.82 us
    ppermute x1, waiting for transfers between devices, local(): lax.ppermute(normed, 'row', [((r + step) % ranks, r) for r in range(ranks)])  2.16 us
    ppermute x3, starting transfers between devices, local(): more = [lax.ppermute(part, 'lo', flip) for part in ready]  1.78 us
    ppermute x1, starting transfers between devices, local(): lax.ppermute(normed, 'row', [((r + step) % ranks, r) for r in range(ranks)])  1.46 us
  transfers between devices with their start and end apart: 8, of which 3 were waited for; matrix products, arithmetic and copies ran while one was open for 0% of the time, Pallas kernels for 37%

profile of v7, /device:TPU:0, one launch (start us, length us, event | category | flops | bytes accessed | tf_op | source)
XLA Modules:
  0.0 47.9 jit_solution(7343398429508760562)
XLA Ops:
  0.6 3.3 %shard_map.140 = (f32[8,4,16,128]{3,2,1,0:T(8,128)}, bf16[16,128,128]{2,1,0:T(8,128)(2,1)}) custom-call(bf16[128,16,128]{2,1,0:T(8,128)(2,1)} %refs_0_.7, bf16[4,128]{1,0:T(4,128)(2,1)} %bitcast.7), custom_call_target="tpu_custom_call" | custom-call | flops 2097152 | bytes 1311744 | tf_op jit(solution)/shard_map/pallas_call | solution.py:73
  3.9 7.8 %all-to-all-start = ((f32[8,4,16,128]{3,2,1,0:T(8,128)}), f32[8,4,16,128]{3,2,1,0:T(8,128)S(1)}, u32[]{:S(2)}, u32[]{:S(2)}) async-start(f32[8,4,16,128]{3,2,1,0:T(8,128)} %get-tuple-element.10.refs_6_), calls=%async_computation | async-start | bytes 524288 | tf_op jit(solution)/shard_map/all_to_all | solution.py:502
  11.8 1.5 %collective-permute-start.3 = (bf16[16,128,128]{2,1,0:T(8,128)(2,1)}, bf16[16,128,128]{2,1,0:T(8,128)(2,1)S(1)}, u32[]{:S(2)}, u32[]{:S(2)}) collective-permute-start(bf16[16,128,128]{2,1,0:T(8,128)(2,1)} %get-tuple-element.13.refs_8_), channel_id=1, source_target_pairs={{16,0},{0,16},{17,1},{1,17},{18,2},{2,18},{19,3},{3,19},{20,4},{4,... | collective-permute-start | bytes 1572872 | tf_op jit(solution)/shard_map/ppermute | solution.py:506
  13.2 5.6 %shard_map.141 = (bf16[2,288,768]{2,1,0:T(8,128)(2,1)}, bf16[2,256,768]{2,1,0:T(8,128)(2,1)}) custom-call(s32[4]{0:T(128)} %refs_0_.5, bf16[256,384]{1,0:T(8,128)(2,1)} %refs_1_.4, bf16[256,384]{1,0:T(8,128)(2,1)} %refs_2_.2, bf16[384,1536]{1,0:T(8,128)(2,1)} %refs_3_.1, bf16[4,256,768]{2,1,0:T(8,128)(2,1)} %refs_4_.1, bf16[768,3072]{1,0:T(8,128)(2,1)} %refs_0_.6, ...), custom_call_target="tpu_custom_call" | custom-call | flops 2415919104 | bytes 9535504 | tf_op jit(solution)/shard_map/pallas_call | solution.py:73
  18.9 0.1 collective-permute-start.5
  18.9 0.0 all-to-all-done
  19.0 1.6 %collective-permute-start.1 = (f32[2,2,4,16,128]{4,3,2,1,0:T(8,128)S(1)}, f32[2,2,4,16,128]{4,3,2,1,0:T(8,128)S(1)}, u32[]{:S(2)}, u32[]{:S(2)}) collective-permute-start(f32[2,2,4,16,128]{4,3,2,1,0:T(8,128)S(1)} %constant_dynamic-slice_fusion.refs_3_.refs_4_), channel_id=1, source_target_pairs={{2,0},{3,1},{0,2},{1,3},{6,4},{7,5},{4,6},{5,7},{10,8},{11,9},{8,1... | collective-permute-start | bytes 393224 | tf_op jit(solution)/shard_map/ppermute | solution.py:569
  20.6 0.2 collective-permute-start
  20.8 0.0 copy-start.2
  20.8 0.0 copy-start.3
  20.8 3.7 %shard_map.142 = (f32[2,352,128]{2,1,0:T(8,128)S(1)}, f32[2,352,128]{2,1,0:T(8,128)}) custom-call(bf16[768,3072]{1,0:T(8,128)(2,1)} %refs_0_.6, bf16[384,768]{1,0:T(8,128)(2,1)} %refs_1_.5, bf16[2,288,768]{2,1,0:T(8,128)(2,1)} %get-tuple-element.11.refs_2_, f32[2,2,4,16,128]{4,3,2,1,0:T(8,128)S(1)} %constant_dynamic-slice_fusion.refs_3_.refs_4_), custom_call_target="tpu_custom_call" | custom-call | flops 2147483648 | bytes 6914048 | tf_op jit(solution)/shard_map/pallas_call | solution.py:73
  24.5 0.4 collective-permute-done.1.refs_0_
  24.9 0.0 collective-permute-start.2
  24.9 0.5 %collective-permute-start.4 = (f32[2,352,128]{2,1,0:T(8,128)}, f32[2,352,128]{2,1,0:T(8,128)}, u32[]{:S(2)}, u32[]{:S(2)}) collective-permute-start(f32[2,352,128]{2,1,0:T(8,128)} %get-tuple-element.16), channel_id=1, source_target_pairs={{1,0},{0,1},{3,2},{2,3},{5,4},{4,5},{7,6},{6,7},{9,8},{8,9},{11,10... | collective-permute-start | bytes 1081352 | tf_op jit(solution)/shard_map/ppermute | solution.py:576
  25.4 2.2 %collective-permute-done.3.refs_9_ = bf16[16,128,128]{2,1,0:T(8,128)(2,1)S(1)} collective-permute-done((bf16[16,128,128]{2,1,0:T(8,128)(2,1)}, bf16[16,128,128]{2,1,0:T(8,128)(2,1)S(1)}, u32[]{:S(2)}, u32[]{:S(2)}) %collective-permute-start.3) | collective-permute-done | bytes 524320 | tf_op jit(solution)/shard_map/ppermute | solution.py:506
  27.6 0.0 collective-permute-done.refs_5_
  27.6 0.0 collective-permute-done.2.refs_7_
  27.6 0.8 %copy-done.6 = bf16[16,128,128]{2,1,0:T(8,128)(2,1)} copy-done((bf16[16,128,128]{2,1,0:T(8,128)(2,1)}, bf16[16,128,128]{2,1,0:T(8,128)(2,1)S(1)}, u32[]{:S(2)}) %copy-start.6) | copy-done | bytes 524312
  28.4 0.0 copy-done.2
  28.4 0.0 copy-done.3
  28.4 0.0 copy-done.4
  28.4 0.0 copy-done.5
  28.4 0.0 copy-start
  28.4 0.0 copy-start.1
  28.4 8.3 %shard_map.144 = (bf16[128,16,128]{2,1,0:T(8,128)(2,1)}, f32[16,16,128]{2,1,0:T(8,128)}) custom-call(bf16[128,16,128]{2,1,0:T(8,128)(2,1)S(1)} %copy-done.2, bf16[128,512]{1,0:T(8,128)(2,1)S(1)} %copy-done.3, bf16[128,128]{1,0:T(8,128)(2,1)S(1)} %copy-done.4, bf16[16,128]{1,0:T(8,128)(2,1)S(1)} %bitcast.4, ...), custom_call_target="tpu_custom_call" | custom-call | flops 1073741824 | bytes 2920448 | tf_op jit(solution)/shard_map/pallas_call | solution.py:73
  36.7 4.9 %all-to-all-start.1 = ((f32[16,16,128]{2,1,0:T(8,128)}), f32[16,16,128]{2,1,0:T(8,128)S(1)}, u32[]{:S(2)}, u32[]{:S(2)}) async-start(f32[16,16,128]{2,1,0:T(8,128)} %get-tuple-element.15), calls=%async_computation.1 | async-start | bytes 262144 | tf_op jit(solution)/shard_map/all_to_all | solution.py:622
  41.7 0.0 collective-permute-done.5.refs_5_
  41.7 0.0 collective-permute-done.4.refs_3_
  41.7 3.8 %all-to-all-done.1.refs_0_ = f32[16,16,128]{2,1,0:T(8,128)S(1)} async-done(((f32[16,16,128]{2,1,0:T(8,128)}), f32[16,16,128]{2,1,0:T(8,128)S(1)}, u32[]{:S(2)}, u32[]{:S(2)}) %all-to-all-start.1) | async-done | bytes 131104 | tf_op jit(solution)/shard_map/all_to_all | solution.py:622
  45.5 0.0 copy-done
  45.5 0.0 copy-done.1
  45.5 2.4 %shard_map.145 = bf16[32,768]{1,0:T(8,128)(2,1)} custom-call(f32[16,16,128]{2,1,0:T(8,128)S(1)} %all-to-all-done.1.refs_0_, bf16[768,768]{1,0:T(8,128)(2,1)S(1)} %copy-done, f32[2,352,128]{2,1,0:T(8,128)S(1)} %get-tuple-element.12.refs_1_.refs_10_.refs_2_, f32[2,352,128]{2,1,0:T(8,128)} %collective-permute-done.4.refs_3_, ...), custom_call_target="tpu_custom_call" | custom-call | flops 201326592 | bytes 3653632 | tf_op jit(solution)/shard_map/pallas_call | solution.py:73
  (5 shorter events, 0.0 us)
Async XLA Ops:
  3.9 15.0 %all-to-all-start = ((f32[8,4,16,128]{3,2,1,0:T(8,128)}), f32[8,4,16,128]{3,2,1,0:T(8,128)S(1)}, u32[]{:S(2)}, u32[]{:S(2)}) async-start(f32[8,4,16,128]{3,2,1,0:T(8,128)} %get-tuple-element.10.refs_6_), calls=%async_computation | async-start | bytes 524288 | tf_op jit(solution)/shard_map/all_to_all | solution.py:502
  11.8 15.8 %collective-permute-start.3 = (bf16[16,128,128]{2,1,0:T(8,128)(2,1)}, bf16[16,128,128]{2,1,0:T(8,128)(2,1)S(1)}, u32[]{:S(2)}, u32[]{:S(2)}) collective-permute-start(bf16[16,128,128]{2,1,0:T(8,128)(2,1)} %get-tuple-element.13.refs_8_), channel_id=1, source_target_pairs={{16,0},{0,16},{17,1},{1,17},{18,2},{2,18},{19,3},{3,19},{20,4},{4,... | collective-permute-start | bytes 1572872 | tf_op jit(solution)/shard_map/ppermute | solution.py:506
  18.9 22.8 %collective-permute-start.5 = (bf16[2,256,768]{2,1,0:T(8,128)(2,1)}, bf16[2,256,768]{2,1,0:T(8,128)(2,1)S(1)}, u32[]{:S(2)}, u32[]{:S(2)}) collective-permute-start(bf16[2,256,768]{2,1,0:T(8,128)(2,1)} %get-tuple-element.17.refs_4_), channel_id=1, source_target_pairs={{1,0},{0,1},{3,2},{2,3},{5,4},{4,5},{7,6},{6,7},{9,8},{8,9},{11,10... | collective-permute-start | bytes 2359304 | tf_op jit(solution)/shard_map/ppermute | solution.py:575
  19.0 5.9 %collective-permute-start.1 = (f32[2,2,4,16,128]{4,3,2,1,0:T(8,128)S(1)}, f32[2,2,4,16,128]{4,3,2,1,0:T(8,128)S(1)}, u32[]{:S(2)}, u32[]{:S(2)}) collective-permute-start(f32[2,2,4,16,128]{4,3,2,1,0:T(8,128)S(1)} %constant_dynamic-slice_fusion.refs_3_.refs_4_), channel_id=1, source_target_pairs={{2,0},{3,1},{0,2},{1,3},{6,4},{7,5},{4,6},{5,7},{10,8},{11,9},{8,1... | collective-permute-start | bytes 393224 | tf_op jit(solution)/shard_map/ppermute | solution.py:569
  20.6 7.0 %collective-permute-start = (f32[2,2,4,16,128]{4,3,2,1,0:T(8,128)S(1)}, f32[2,2,4,16,128]{4,3,2,1,0:T(8,128)S(1)}, u32[]{:S(2)}, u32[]{:S(2)}) collective-permute-start(f32[2,2,4,16,128]{4,3,2,1,0:T(8,128)S(1)} %constant_dynamic-slice_fusion.refs_3_.refs_4_), channel_id=1, source_target_pairs={{1,0},{0,1},{3,2},{2,3},{5,4},{4,5},{7,6},{6,7},{9,8},{8,9},{11,10... | collective-permute-start | bytes 393224 | tf_op jit(solution)/shard_map/ppermute | solution.py:569
  20.8 7.6 %copy-start.2 = (bf16[128,16,128]{2,1,0:T(8,128)(2,1)S(1)}, bf16[128,16,128]{2,1,0:T(8,128)(2,1)}, u32[]{:S(2)}) copy-start(bf16[128,16,128]{2,1,0:T(8,128)(2,1)} %refs_0_.7) | copy-start | bytes 1572868
  20.8 7.6 %copy-start.3 = (bf16[128,512]{1,0:T(8,128)(2,1)S(1)}, bf16[128,512]{1,0:T(8,128)(2,1)}, u32[]{:S(2)}) copy-start(bf16[128,512]{1,0:T(8,128)(2,1)} %refs_1_.6) | copy-start | bytes 393220
  20.8 7.6 %copy-start.4 = (bf16[128,128]{1,0:T(8,128)(2,1)S(1)}, bf16[128,128]{1,0:T(8,128)(2,1)}, u32[]{:S(2)}) copy-start(bf16[128,128]{1,0:T(8,128)(2,1)} %refs_2_.3) | copy-start | bytes 98308
  20.8 7.6 %copy-start.5 = (bf16[128,16]{0,1:T(8,128)(2,1)S(1)}, bf16[128,16]{0,1:T(8,128)(2,1)}, u32[]{:S(2)}) copy-start(bf16[128,16]{0,1:T(8,128)(2,1)} %param.23) | copy-start | bytes 12292
  24.9 2.7 %collective-permute-start.2 = (f32[2,2,4,16,128]{4,3,2,1,0:T(8,128)S(1)}, f32[2,2,4,16,128]{4,3,2,1,0:T(8,128)S(1)}, u32[]{:S(2)}, u32[]{:S(2)}) collective-permute-start(f32[2,2,4,16,128]{4,3,2,1,0:T(8,128)S(1)} %shard_map.143.refs_6_), channel_id=1, source_target_pairs={{1,0},{0,1},{3,2},{2,3},{5,4},{4,5},{7,6},{6,7},{9,8},{8,9},{11,10... | collective-permute-start | bytes 393224 | tf_op jit(solution)/shard_map/ppermute | solution.py:569
  24.9 16.8 %collective-permute-start.4 = (f32[2,352,128]{2,1,0:T(8,128)}, f32[2,352,128]{2,1,0:T(8,128)}, u32[]{:S(2)}, u32[]{:S(2)}) collective-permute-start(f32[2,352,128]{2,1,0:T(8,128)} %get-tuple-element.16), channel_id=1, source_target_pairs={{1,0},{0,1},{3,2},{2,3},{5,4},{4,5},{7,6},{6,7},{9,8},{8,9},{11,10... | collective-permute-start | bytes 1081352 | tf_op jit(solution)/shard_map/ppermute | solution.py:576
  27.6 0.8 %copy-start.6 = (bf16[16,128,128]{2,1,0:T(8,128)(2,1)}, bf16[16,128,128]{2,1,0:T(8,128)(2,1)S(1)}, u32[]{:S(2)}) copy-start(bf16[16,128,128]{2,1,0:T(8,128)(2,1)S(1)} %collective-permute-done.3.refs_9_) | copy-start | bytes 1572868
  28.4 17.1 %copy-start = (bf16[768,768]{1,0:T(8,128)(2,1)S(1)}, bf16[768,768]{1,0:T(8,128)(2,1)}, u32[]{:S(2)}) copy-start(bf16[768,768]{1,0:T(8,128)(2,1)} %refs_1_.7) | copy-start | bytes 3538948
  28.4 17.1 %copy-start.1 = (bf16[2,256,768]{2,1,0:T(8,128)(2,1)S(1)}, bf16[2,256,768]{2,1,0:T(8,128)(2,1)}, u32[]{:S(2)}) copy-start(bf16[2,256,768]{2,1,0:T(8,128)(2,1)} %get-tuple-element.17.refs_4_) | copy-start | bytes 2359300
  36.7 8.8 %all-to-all-start.1 = ((f32[16,16,128]{2,1,0:T(8,128)}), f32[16,16,128]{2,1,0:T(8,128)S(1)}, u32[]{:S(2)}, u32[]{:S(2)}) async-start(f32[16,16,128]{2,1,0:T(8,128)} %get-tuple-element.15), calls=%async_computation.1 | async-start | bytes 262144 | tf_op jit(solution)/shard_map/all_to_all | solution.py:622

commit v8 on v7

--- a/solution.py
+++ b/solution.py
@@ -355,10 +355,10 @@
 
     score(0, 0)
 
-    @pl.loop(0, cols // batch)
+    @pl.loop(0, cols // 8)
     def _(group):
-        for side in range(batch):
-            col = group * batch + side
+        for side in range(8):
+            col = group * 8 + side
             score(jnp.minimum(col + 1, cols - 1), (side + 1) % 2)
             attend(col, side % 2)
 

time: 48.3 us -> 48.1 us (level)
  no operation moved by 1% of the time
where the time goes in v8:
time: 48.1 us; the launch traced here: 47.6 us
  Pallas kernels  23.1 us (48%)
  starting transfers between devices  16.6 us (35%)
  waiting for transfers between devices  6.4 us (13%)
  local copies, waits for them, and re-layouts  0.82 us (2%)
  between operations  0.74 us (2%)
    pallas_call x5, Pallas kernels, call(): pl.pallas_call(body, out_shape=out_shape, in_specs=in_specs, out_specs=tu...  23.1 us
    all_to_all x1, starting transfers between devices, local(): lax.all_to_all(bias, ('row', 'hi', 'lo'), split_axis=0, concat_axis=0, ax...  7.82 us
    all_to_all x1, starting transfers between devices, local(): lax.all_to_all(pair_bias, ('hi', 'lo'), split_axis=0, concat_axis=0, axis...  4.95 us
    all_to_all x1, waiting for transfers between devices, local(): lax.all_to_all(pair_bias, ('hi', 'lo'), split_axis=0, concat_axis=0, axis...  3.82 us
    ppermute x1, waiting for transfers between devices, local(): lax.ppermute(normed, 'row', [((r + step) % ranks, r) for r in range(ranks)])  2.16 us
    ppermute x3, starting transfers between devices, local(): more = [lax.ppermute(part, 'lo', flip) for part in ready]  1.78 us
    ppermute x1, starting transfers between devices, local(): lax.ppermute(normed, 'row', [((r + step) % ranks, r) for r in range(ranks)])  1.46 us
  transfers between devices with their start and end apart: 8, of which 3 were waited for; matrix products, arithmetic and copies ran while one was open for 0% of the time, Pallas kernels for 37%

profile of v8, /device:TPU:0, one launch (start us, length us, event | category | flops | bytes accessed | tf_op | source)
XLA Modules:
  0.0 47.6 jit_solution(54621160593795992)
XLA Ops:
  0.6 3.3 %shard_map.140 = (f32[8,4,16,128]{3,2,1,0:T(8,128)}, bf16[16,128,128]{2,1,0:T(8,128)(2,1)}) custom-call(bf16[128,16,128]{2,1,0:T(8,128)(2,1)} %refs_0_.7, bf16[4,128]{1,0:T(4,128)(2,1)} %bitcast.7), custom_call_target="tpu_custom_call" | custom-call | flops 2097152 | bytes 1311744 | tf_op jit(solution)/shard_map/pallas_call | solution.py:73
  3.9 7.8 %all-to-all-start = ((f32[8,4,16,128]{3,2,1,0:T(8,128)}), f32[8,4,16,128]{3,2,1,0:T(8,128)S(1)}, u32[]{:S(2)}, u32[]{:S(2)}) async-start(f32[8,4,16,128]{3,2,1,0:T(8,128)} %get-tuple-element.10.refs_6_), calls=%async_computation | async-start | bytes 524288 | tf_op jit(solution)/shard_map/all_to_all | solution.py:502
  11.8 1.5 %collective-permute-start.3 = (bf16[16,128,128]{2,1,0:T(8,128)(2,1)}, bf16[16,128,128]{2,1,0:T(8,128)(2,1)S(1)}, u32[]{:S(2)}, u32[]{:S(2)}) collective-permute-start(bf16[16,128,128]{2,1,0:T(8,128)(2,1)} %get-tuple-element.13.refs_8_), channel_id=1, source_target_pairs={{16,0},{0,16},{17,1},{1,17},{18,2},{2,18},{19,3},{3,19},{20,4},{4,... | collective-permute-start | bytes 1572872 | tf_op jit(solution)/shard_map/ppermute | solution.py:506
  13.2 5.6 %shard_map.141 = (bf16[2,288,768]{2,1,0:T(8,128)(2,1)}, bf16[2,256,768]{2,1,0:T(8,128)(2,1)}) custom-call(s32[4]{0:T(128)} %refs_0_.5, bf16[256,384]{1,0:T(8,128)(2,1)} %refs_1_.4, bf16[256,384]{1,0:T(8,128)(2,1)} %refs_2_.2, bf16[384,1536]{1,0:T(8,128)(2,1)} %refs_3_.1, bf16[4,256,768]{2,1,0:T(8,128)(2,1)} %refs_4_.1, bf16[768,3072]{1,0:T(8,128)(2,1)} %refs_0_.6, ...), custom_call_target="tpu_custom_call" | custom-call | flops 2415919104 | bytes 9535504 | tf_op jit(solution)/shard_map/pallas_call | solution.py:73
  18.9 0.1 collective-permute-start.5
  18.9 0.0 all-to-all-done
  19.0 1.6 %collective-permute-start.1 = (f32[2,2,4,16,128]{4,3,2,1,0:T(8,128)S(1)}, f32[2,2,4,16,128]{4,3,2,1,0:T(8,128)S(1)}, u32[]{:S(2)}, u32[]{:S(2)}) collective-permute-start(f32[2,2,4,16,128]{4,3,2,1,0:T(8,128)S(1)} %constant_dynamic-slice_fusion.refs_3_.refs_4_), channel_id=1, source_target_pairs={{2,0},{3,1},{0,2},{1,3},{6,4},{7,5},{4,6},{5,7},{10,8},{11,9},{8,1... | collective-permute-start | bytes 393224 | tf_op jit(solution)/shard_map/ppermute | solution.py:569
  20.6 0.2 collective-permute-start
  20.8 0.0 copy-start.2
  20.8 0.0 copy-start.3
  20.8 3.7 %shard_map.142 = (f32[2,352,128]{2,1,0:T(8,128)S(1)}, f32[2,352,128]{2,1,0:T(8,128)}) custom-call(bf16[768,3072]{1,0:T(8,128)(2,1)} %refs_0_.6, bf16[384,768]{1,0:T(8,128)(2,1)} %refs_1_.5, bf16[2,288,768]{2,1,0:T(8,128)(2,1)} %get-tuple-element.11.refs_2_, f32[2,2,4,16,128]{4,3,2,1,0:T(8,128)S(1)} %constant_dynamic-slice_fusion.refs_3_.refs_4_), custom_call_target="tpu_custom_call" | custom-call | flops 2147483648 | bytes 6914048 | tf_op jit(solution)/shard_map/pallas_call | solution.py:73
  24.5 0.4 collective-permute-done.1.refs_0_
  24.9 0.0 collective-permute-start.2
  24.9 0.5 %collective-permute-start.4 = (f32[2,352,128]{2,1,0:T(8,128)}, f32[2,352,128]{2,1,0:T(8,128)}, u32[]{:S(2)}, u32[]{:S(2)}) collective-permute-start(f32[2,352,128]{2,1,0:T(8,128)} %get-tuple-element.16), channel_id=1, source_target_pairs={{1,0},{0,1},{3,2},{2,3},{5,4},{4,5},{7,6},{6,7},{9,8},{8,9},{11,10... | collective-permute-start | bytes 1081352 | tf_op jit(solution)/shard_map/ppermute | solution.py:576
  25.4 2.2 %collective-permute-done.3.refs_9_ = bf16[16,128,128]{2,1,0:T(8,128)(2,1)S(1)} collective-permute-done((bf16[16,128,128]{2,1,0:T(8,128)(2,1)}, bf16[16,128,128]{2,1,0:T(8,128)(2,1)S(1)}, u32[]{:S(2)}, u32[]{:S(2)}) %collective-permute-start.3) | collective-permute-done | bytes 524320 | tf_op jit(solution)/shard_map/ppermute | solution.py:506
  27.6 0.0 collective-permute-done.refs_5_
  27.6 0.0 collective-permute-done.2.refs_7_
  27.6 0.8 %copy-done.6 = bf16[16,128,128]{2,1,0:T(8,128)(2,1)} copy-done((bf16[16,128,128]{2,1,0:T(8,128)(2,1)}, bf16[16,128,128]{2,1,0:T(8,128)(2,1)S(1)}, u32[]{:S(2)}) %copy-start.6) | copy-done | bytes 524312
  28.4 0.0 copy-done.2
  28.4 0.0 copy-done.3
  28.4 0.0 copy-done.4
  28.4 0.0 copy-done.5
  28.4 0.0 copy-start
  28.4 0.0 copy-start.1
  28.4 8.1 %shard_map.144 = (bf16[128,16,128]{2,1,0:T(8,128)(2,1)}, f32[16,16,128]{2,1,0:T(8,128)}) custom-call(bf16[128,16,128]{2,1,0:T(8,128)(2,1)S(1)} %copy-done.2, bf16[128,512]{1,0:T(8,128)(2,1)S(1)} %copy-done.3, bf16[128,128]{1,0:T(8,128)(2,1)S(1)} %copy-done.4, bf16[16,128]{1,0:T(8,128)(2,1)S(1)} %bitcast.4, ...), custom_call_target="tpu_custom_call" | custom-call | flops 1073741824 | bytes 2920448 | tf_op jit(solution)/shard_map/pallas_call | solution.py:73
  36.5 4.9 %all-to-all-start.1 = ((f32[16,16,128]{2,1,0:T(8,128)}), f32[16,16,128]{2,1,0:T(8,128)S(1)}, u32[]{:S(2)}, u32[]{:S(2)}) async-start(f32[16,16,128]{2,1,0:T(8,128)} %get-tuple-element.15), calls=%async_computation.1 | async-start | bytes 262144 | tf_op jit(solution)/shard_map/all_to_all | solution.py:622
  41.4 0.0 collective-permute-done.5.refs_5_
  41.4 0.0 collective-permute-done.4.refs_3_
  41.4 3.8 %all-to-all-done.1.refs_0_ = f32[16,16,128]{2,1,0:T(8,128)S(1)} async-done(((f32[16,16,128]{2,1,0:T(8,128)}), f32[16,16,128]{2,1,0:T(8,128)S(1)}, u32[]{:S(2)}, u32[]{:S(2)}) %all-to-all-start.1) | async-done | bytes 131104 | tf_op jit(solution)/shard_map/all_to_all | solution.py:622
  45.3 0.0 copy-done
  45.3 0.0 copy-done.1
  45.3 2.4 %shard_map.145 = bf16[32,768]{1,0:T(8,128)(2,1)} custom-call(f32[16,16,128]{2,1,0:T(8,128)S(1)} %all-to-all-done.1.refs_0_, bf16[768,768]{1,0:T(8,128)(2,1)S(1)} %copy-done, f32[2,352,128]{2,1,0:T(8,128)S(1)} %get-tuple-element.12.refs_1_.refs_10_.refs_2_, f32[2,352,128]{2,1,0:T(8,128)} %collective-permute-done.4.refs_3_, ...), custom_call_target="tpu_custom_call" | custom-call | flops 201326592 | bytes 3653632 | tf_op jit(solution)/shard_map/pallas_call | solution.py:73
  (5 shorter events, 0.0 us)
Async XLA Ops:
  3.9 15.0 %all-to-all-start = ((f32[8,4,16,128]{3,2,1,0:T(8,128)}), f32[8,4,16,128]{3,2,1,0:T(8,128)S(1)}, u32[]{:S(2)}, u32[]{:S(2)}) async-start(f32[8,4,16,128]{3,2,1,0:T(8,128)} %get-tuple-element.10.refs_6_), calls=%async_computation | async-start | bytes 524288 | tf_op jit(solution)/shard_map/all_to_all | solution.py:502
  11.8 15.8 %collective-permute-start.3 = (bf16[16,128,128]{2,1,0:T(8,128)(2,1)}, bf16[16,128,128]{2,1,0:T(8,128)(2,1)S(1)}, u32[]{:S(2)}, u32[]{:S(2)}) collective-permute-start(bf16[16,128,128]{2,1,0:T(8,128)(2,1)} %get-tuple-element.13.refs_8_), channel_id=1, source_target_pairs={{16,0},{0,16},{17,1},{1,17},{18,2},{2,18},{19,3},{3,19},{20,4},{4,... | collective-permute-start | bytes 1572872 | tf_op jit(solution)/shard_map/ppermute | solution.py:506
  18.9 22.6 %collective-permute-start.5 = (bf16[2,256,768]{2,1,0:T(8,128)(2,1)}, bf16[2,256,768]{2,1,0:T(8,128)(2,1)S(1)}, u32[]{:S(2)}, u32[]{:S(2)}) collective-permute-start(bf16[2,256,768]{2,1,0:T(8,128)(2,1)} %get-tuple-element.17.refs_4_), channel_id=1, source_target_pairs={{1,0},{0,1},{3,2},{2,3},{5,4},{4,5},{7,6},{6,7},{9,8},{8,9},{11,10... | collective-permute-start | bytes 2359304 | tf_op jit(solution)/shard_map/ppermute | solution.py:575
  19.0 5.9 %collective-permute-start.1 = (f32[2,2,4,16,128]{4,3,2,1,0:T(8,128)S(1)}, f32[2,2,4,16,128]{4,3,2,1,0:T(8,128)S(1)}, u32[]{:S(2)}, u32[]{:S(2)}) collective-permute-start(f32[2,2,4,16,128]{4,3,2,1,0:T(8,128)S(1)} %constant_dynamic-slice_fusion.refs_3_.refs_4_), channel_id=1, source_target_pairs={{2,0},{3,1},{0,2},{1,3},{6,4},{7,5},{4,6},{5,7},{10,8},{11,9},{8,1... | collective-permute-start | bytes 393224 | tf_op jit(solution)/shard_map/ppermute | solution.py:569
  20.6 7.0 %collective-permute-start = (f32[2,2,4,16,128]{4,3,2,1,0:T(8,128)S(1)}, f32[2,2,4,16,128]{4,3,2,1,0:T(8,128)S(1)}, u32[]{:S(2)}, u32[]{:S(2)}) collective-permute-start(f32[2,2,4,16,128]{4,3,2,1,0:T(8,128)S(1)} %constant_dynamic-slice_fusion.refs_3_.refs_4_), channel_id=1, source_target_pairs={{1,0},{0,1},{3,2},{2,3},{5,4},{4,5},{7,6},{6,7},{9,8},{8,9},{11,10... | collective-permute-start | bytes 393224 | tf_op jit(solution)/shard_map/ppermute | solution.py:569
  20.8 7.6 %copy-start.2 = (bf16[128,16,128]{2,1,0:T(8,128)(2,1)S(1)}, bf16[128,16,128]{2,1,0:T(8,128)(2,1)}, u32[]{:S(2)}) copy-start(bf16[128,16,128]{2,1,0:T(8,128)(2,1)} %refs_0_.7) | copy-start | bytes 1572868
  20.8 7.6 %copy-start.3 = (bf16[128,512]{1,0:T(8,128)(2,1)S(1)}, bf16[128,512]{1,0:T(8,128)(2,1)}, u32[]{:S(2)}) copy-start(bf16[128,512]{1,0:T(8,128)(2,1)} %refs_1_.6) | copy-start | bytes 393220
  20.8 7.6 %copy-start.4 = (bf16[128,128]{1,0:T(8,128)(2,1)S(1)}, bf16[128,128]{1,0:T(8,128)(2,1)}, u32[]{:S(2)}) copy-start(bf16[128,128]{1,0:T(8,128)(2,1)} %refs_2_.3) | copy-start | bytes 98308
  20.8 7.6 %copy-start.5 = (bf16[128,16]{0,1:T(8,128)(2,1)S(1)}, bf16[128,16]{0,1:T(8,128)(2,1)}, u32[]{:S(2)}) copy-start(bf16[128,16]{0,1:T(8,128)(2,1)} %param.23) | copy-start | bytes 12292
  24.9 2.7 %collective-permute-start.2 = (f32[2,2,4,16,128]{4,3,2,1,0:T(8,128)S(1)}, f32[2,2,4,16,128]{4,3,2,1,0:T(8,128)S(1)}, u32[]{:S(2)}, u32[]{:S(2)}) collective-permute-start(f32[2,2,4,16,128]{4,3,2,1,0:T(8,128)S(1)} %shard_map.143.refs_6_), channel_id=1, source_target_pairs={{1,0},{0,1},{3,2},{2,3},{5,4},{4,5},{7,6},{6,7},{9,8},{8,9},{11,10... | collective-permute-start | bytes 393224 | tf_op jit(solution)/shard_map/ppermute | solution.py:569
  24.9 16.5 %collective-permute-start.4 = (f32[2,352,128]{2,1,0:T(8,128)}, f32[2,352,128]{2,1,0:T(8,128)}, u32[]{:S(2)}, u32[]{:S(2)}) collective-permute-start(f32[2,352,128]{2,1,0:T(8,128)} %get-tuple-element.16), channel_id=1, source_target_pairs={{1,0},{0,1},{3,2},{2,3},{5,4},{4,5},{7,6},{6,7},{9,8},{8,9},{11,10... | collective-permute-start | bytes 1081352 | tf_op jit(solution)/shard_map/ppermute | solution.py:576
  27.6 0.8 %copy-start.6 = (bf16[16,128,128]{2,1,0:T(8,128)(2,1)}, bf16[16,128,128]{2,1,0:T(8,128)(2,1)S(1)}, u32[]{:S(2)}) copy-start(bf16[16,128,128]{2,1,0:T(8,128)(2,1)S(1)} %collective-permute-done.3.refs_9_) | copy-start | bytes 1572868
  28.4 16.9 %copy-start = (bf16[768,768]{1,0:T(8,128)(2,1)S(1)}, bf16[768,768]{1,0:T(8,128)(2,1)}, u32[]{:S(2)}) copy-start(bf16[768,768]{1,0:T(8,128)(2,1)} %refs_1_.7) | copy-start | bytes 3538948
  28.4 16.9 %copy-start.1 = (bf16[2,256,768]{2,1,0:T(8,128)(2,1)S(1)}, bf16[2,256,768]{2,1,0:T(8,128)(2,1)}, u32[]{:S(2)}) copy-start(bf16[2,256,768]{2,1,0:T(8,128)(2,1)} %get-tuple-element.17.refs_4_) | copy-start | bytes 2359300
  36.5 8.8 %all-to-all-start.1 = ((f32[16,16,128]{2,1,0:T(8,128)}), f32[16,16,128]{2,1,0:T(8,128)S(1)}, u32[]{:S(2)}, u32[]{:S(2)}) async-start(f32[16,16,128]{2,1,0:T(8,128)} %get-tuple-element.15), calls=%async_computation.1 | async-start | bytes 262144 | tf_op jit(solution)/shard_map/all_to_all | solution.py:622
